TPU v7x, 256 devices: a whole 4x4x8 slice. The times are simulated.
256 devices in a mesh: band: 16 (over z, x_hi), gy: 4 (over x_lo, core), gz: 4 (over y).
Axes of the slice: x: 4 (x_hi: 2, x_lo: 2; x = x_hi * 2 + x_lo), y: 4, z: 8, core: 2. Of those that a mesh axis runs over, the one named last changes fastest.
Arguments:
- orbitals: bfloat16 [32, 128, 128, 256], P('band', 'gy', 'gz'), may hold values from -6 to 6
- potential: float32 [128, 128, 128], P(('gy', 'gz')), may hold values from -6 to 6
- cutoff_mask: int32 [128, 128, 128], P('gy', 'gz'), may hold values from 0 to 1, as said below
- channels: bfloat16 [4, 128, 128, 128], P(None, 'gy', 'gz'), may hold values from -0.125 to 0.125
- positions: float32 [8, 3], replicated, may hold values from 0 to 1
- proj_atom: int32 [32], replicated, may hold values from 0 to 7
- proj_chan: int32 [32], replicated, may hold values from 0 to 3
- coupling: float32 [32], replicated, may hold values from 0.5 to 2
- occupations: float32 [32], P('band'), may hold values from 0.03125 to 0.09375
Outputs:
- applied: bfloat16 [32, 128, 128, 256], P('band', 'gy', 'gz')
- density: float32 [128, 128, 128], P(('gy', 'gz'))
Inputs may be any that keep to these rules, and one draw needn't show every extreme that they name: With s = f(ky)^2 + f(kz)^2 + f(kx)^2, cutoff_mask is 1 wherever s < 56^2 and 0 wherever s >= 128^2 / 4; in between each plane wave's value is its own.
All inputs are finite; a program needn't handle non-finite values.
Results may differ from a plain program's by a relative error of at most 0.018.
Values may be sent and summed in bfloat16 or wider, within the bound.
No kernel may reach another device: no remote copies, remote signals or barrier semaphores. Data moves between devices by JAX's collectives and lax.ppermute only.
A program may use at most 128 MiB of HBM per device.

v0:
```python
import math

import jax
import jax.numpy as jnp
from jax import lax
from jax.sharding import PartitionSpec as P

kinetic_scale = 1.0 / 1024.0


def dft_table(length, sign_value):
    grid_index = jnp.arange(length, dtype=jnp.int32)
    product = grid_index[:, None] * grid_index[None, :] % length
    phase_angle = 2.0 * math.pi / length * product.astype(jnp.float32)
    cosine_part = jnp.cos(phase_angle) / math.sqrt(length)
    sine_part = sign_value * jnp.sin(phase_angle) / math.sqrt(length)
    upper_rows = jnp.stack([cosine_part, -sine_part], axis=1)
    lower_rows = jnp.stack([sine_part, cosine_part], axis=1)
    return jnp.stack([upper_rows, lower_rows], axis=0).astype(jnp.bfloat16)


def frequencies(first_index, span, length):
    grid_index = first_index + jnp.arange(span, dtype=jnp.int32)
    return jnp.where(grid_index >= length // 2, grid_index - length, grid_index).astype(jnp.float32)


def axis_phase(coordinate, freq):
    phase_angle = 2.0 * math.pi * (coordinate[:, None] * freq[None, :])
    return (jnp.cos(phase_angle), jnp.sin(phase_angle))


def projector_parts(channels, positions, atom_ids, kind_ids, freq_y, freq_z, freq_x):
    atom_hot = (
        atom_ids[:, None] == jnp.arange(positions.shape[0], dtype=jnp.int32)[None, :]
    ).astype(jnp.float32)
    located = jnp.dot(atom_hot, positions, precision=lax.Precision.HIGHEST)
    kind_hot = (
        kind_ids[:, None] == jnp.arange(channels.shape[0], dtype=jnp.int32)[None, :]
    ).astype(jnp.bfloat16)
    radial = jnp.einsum("bc,cyzx->byzx", kind_hot, channels, preferred_element_type=jnp.float32)
    cos_y, sin_y = axis_phase(located[:, 1], freq_y)
    cos_z, sin_z = axis_phase(located[:, 2], freq_z)
    cos_x, sin_x = axis_phase(located[:, 0], freq_x)
    cos_yz = cos_y[:, :, None] * cos_z[:, None, :] - sin_y[:, :, None] * sin_z[:, None, :]
    sin_yz = sin_y[:, :, None] * cos_z[:, None, :] + cos_y[:, :, None] * sin_z[:, None, :]
    cosine = (
        cos_yz[..., None] * cos_x[:, None, None, :] - sin_yz[..., None] * sin_x[:, None, None, :]
    )
    sine = sin_yz[..., None] * cos_x[:, None, None, :] + cos_yz[..., None] * sin_x[:, None, None, :]
    real_beta = (radial * cosine).astype(jnp.bfloat16)
    imag_beta = (-(radial * sine)).astype(jnp.bfloat16)
    return (real_beta, imag_beta)


def shards(
    orbitals,
    potential,
    cutoff_mask,
    channels,
    positions,
    proj_atom,
    proj_chan,
    coupling,
    occupations,
):
    orbit_count = orbitals.shape[0]
    rows_y = orbitals.shape[1]
    rows_z = orbitals.shape[2]
    length = orbitals.shape[3] // 2
    parts_y = lax.axis_size("gy")
    parts_z = lax.axis_size("gz")
    thin_x = length // (parts_y * parts_z)
    inverse = dft_table(length, 1.0)
    forward = dft_table(length, -1.0)
    inv_x = jnp.transpose(inverse, (2, 3, 0, 1)).reshape(2 * length, 2, parts_y, parts_z, thin_x)
    fwd_x = jnp.transpose(forward, (2, 3, 0, 1)).reshape(2, parts_y, parts_z, thin_x, 2 * length)
    mask_full = jnp.concatenate([cutoff_mask, cutoff_mask], axis=2) != 0
    masked = jnp.where(mask_full[None], orbitals, jnp.zeros_like(orbitals))
    freq_y = frequencies(lax.axis_index("gy") * rows_y, rows_y, length)
    freq_z = frequencies(lax.axis_index("gz") * rows_z, rows_z, length)
    freq_x = frequencies(0, length, length)
    real_orbs = masked[..., :length]
    imag_orbs = masked[..., length:]
    real_beta, imag_beta = projector_parts(
        channels, positions, proj_atom, proj_chan, freq_y, freq_z, freq_x
    )
    real_over = jnp.einsum(
        "pyzx,nyzx->pn", real_beta, real_orbs, preferred_element_type=jnp.float32
    )
    real_over = real_over + jnp.einsum(
        "pyzx,nyzx->pn", imag_beta, imag_orbs, preferred_element_type=jnp.float32
    )
    imag_over = jnp.einsum(
        "pyzx,nyzx->pn", real_beta, imag_orbs, preferred_element_type=jnp.float32
    )
    imag_over = imag_over - jnp.einsum(
        "pyzx,nyzx->pn", imag_beta, real_orbs, preferred_element_type=jnp.float32
    )
    partial_intersections = jnp.stack([real_over, imag_over], axis=0)
    intersections = lax.psum(partial_intersections, ("gy", "gz"))
    spread = jnp.einsum(
        "nyzk,kcpqx->npqcxyz", masked, inv_x, preferred_element_type=jnp.float32
    ).astype(jnp.bfloat16)
    spread = spread.reshape(orbit_count, parts_y, parts_z, 2, thin_x, rows_y * rows_z)
    arrived = lax.all_to_all(
        lax.all_to_all(spread, "gy", split_axis=1, concat_axis=5, tiled=True),
        "gz",
        split_axis=2,
        concat_axis=5,
        tiled=True,
    )
    arrived = arrived.reshape(orbit_count, 2, thin_x, parts_z, length, rows_z)
    rotated = jnp.einsum(
        "ncxqyz,ducy->ndxqzu", arrived, inverse, preferred_element_type=jnp.float32
    ).astype(jnp.bfloat16)
    rotated = rotated.reshape(orbit_count, 2, thin_x, length, length)
    real_field = jnp.einsum(
        "ndxzu,fwdz->nfxuw", rotated, inverse, preferred_element_type=jnp.float32
    )
    partial_density = jnp.sum(
        occupations[:, None, None, None] * jnp.sum(real_field * real_field, axis=1), axis=0
    )
    density = lax.psum(partial_density.astype(jnp.bfloat16), "band").astype(jnp.float32)
    scaled = (potential[None, None] * real_field).astype(jnp.bfloat16)
    back_z = jnp.einsum(
        "nfxuw,dzfw->ndxuz", scaled, forward, preferred_element_type=jnp.float32
    ).astype(jnp.bfloat16)
    folded = jnp.einsum(
        "ndxuz,cydu->ncxyz", back_z, forward, preferred_element_type=jnp.float32
    ).astype(jnp.bfloat16)
    folded = folded.reshape(orbit_count, 1, 1, 2, thin_x, length, length)
    returned = lax.all_to_all(
        lax.all_to_all(folded, "gy", split_axis=5, concat_axis=1, tiled=True),
        "gz",
        split_axis=6,
        concat_axis=2,
        tiled=True,
    )
    local_g = jnp.einsum("npqcxyz,cpqxk->nyzk", returned, fwd_x, preferred_element_type=jnp.float32)
    coefficients = (intersections * coupling[None, :, None]).astype(jnp.bfloat16)
    coef_real = coefficients[0]
    coef_imag = coefficients[1]
    real_sum = jnp.einsum("pn,pyzx->nyzx", coef_real, real_beta, preferred_element_type=jnp.float32)
    real_sum = real_sum - jnp.einsum(
        "pn,pyzx->nyzx", coef_imag, imag_beta, preferred_element_type=jnp.float32
    )
    imag_sum = jnp.einsum("pn,pyzx->nyzx", coef_imag, real_beta, preferred_element_type=jnp.float32)
    imag_sum = imag_sum + jnp.einsum(
        "pn,pyzx->nyzx", coef_real, imag_beta, preferred_element_type=jnp.float32
    )
    nonlocal_part = jnp.concatenate([real_sum, imag_sum], axis=3)
    energy = (
        kinetic_scale
        * 0.5
        * (freq_y[:, None, None] ** 2 + freq_z[None, :, None] ** 2 + freq_x[None, None, :] ** 2)
    )
    energy = jnp.concatenate([energy, energy], axis=2)
    total = energy[None] * masked.astype(jnp.float32) + local_g + nonlocal_part
    applied = jnp.where(mask_full[None], total, jnp.zeros_like(total)).astype(jnp.bfloat16)
    return (applied, density)


def solution(mesh):
    placed = (
        P("band", "gy", "gz", None),
        P(("gy", "gz"), None, None),
        P("gy", "gz", None),
        P(None, "gy", "gz", None),
        P(),
        P(),
        P(),
        P(),
        P("band"),
    )
    return jax.shard_map(
        shards,
        mesh=mesh,
        in_specs=placed,
        out_specs=(P("band", "gy", "gz", None), P(("gy", "gz"), None, None)),
        check_vma=False,
    )
```

profile of v0, /device:TPU:32, one launch (start us, length us, event | category | flops | bytes accessed | tf_op | source)
XLA Modules:
  0.0 372.4 jit_solution(13134409530287484070)
XLA Ops:
  13.0 3.2 copy.117
  16.2 7.0 %reshape.426 = bf16[2,4,4,2,8,1024]{5,4,3,2,0,1:T(8,128)(2,1)} reshape(bf16[2,4,4,2,8,32,32]{6,5,4,3,2,0,1:T(8,128)(2,1)} %copy.117) | data formatting | bytes 2097152 | tf_op jit(solution)/shard_map/reshape | solution.py:104
  23.2 4.4 %all-to-all-start = ((bf16[2,4,4,2,8,1024]{5,4,3,2,0,1:T(8,128)(2,1)}), bf16[2,4,4,2,8,1024]{5,4,3,2,0,1:T(8,128)(2,1)}, u32[]{:S(2)}, u32[]{:S(2)}) async-start(bf16[2,4,4,2,8,1024]{5,4,3,2,0,1:T(8,128)(2,1)} %reshape.426), calls=%async_computation | async-start | bytes 2097152 | tf_op jit(solution)/shard_map/all_to_all | solution.py:106
  29.6 12.9 %multiply_convert_fusion = (bf16[32,32,32,128]{3,0,2,1:T(8,128)(2,1)S(1)}, bf16[32,32,32,128]{3,0,2,1:T(8,128)(2,1)S(1)}) fusion(f32[32,128]{1,0:T(8,128)S(1)} %get-tuple-element.20, f32[32,32,32]{0,2,1:T(8,128)S(1)} %get-tuple-element.11, f32[32,128]{1,0:T(8,128)S(1)} %get-tuple-element.19, f32[32,32,32]{0,2,1:T(8,128)S(1)} %get-tuple-element.10, ...), kind=kOutput, calls=%fused_computation.1 | convolution fusion | flops 79691904 | bytes 18120832 | tf_op jit(solution)/shard_map/bc,cyzx->byzx/dot_general | solution.py:40
  51.7 31.1 %psum.14 = f32[2,32,2]{1,2,0:T(2,128)S(1)} all-reduce(f32[2,32,2]{1,2,0:T(2,128)S(1)} %pad_maximum_fusion.11), channel_id=1, replica_groups=mesh['band'=16,'gy'=4,'gz'=4] {'gy','gz'}, use_global_device_ids=true, to_apply=%region_0.1 | all-reduce | flops 128 | bytes 1024 | tf_op jit(solution)/shard_map/psum | solution.py:100
  82.9 4.7 %fusion.67 = f32[2,32,32,128]{3,0,2,1:T(2,128)S(1)} fusion(bf16[32,32,32,128]{3,0,2,1:T(8,128)(2,1)} %copy-done.4, bf16[2,32,2]{1,2,0:T(2,128)(2,1)S(1)} %multiply_convert_fusion.4), kind=kOutput, calls=%fused_computation.112 | convolution fusion | flops 16777216 | bytes 9437696 | tf_op jit(solution)/shard_map/pn,pyzx->nyzx/dot_general | solution.py:143
  95.5 4.5 %all-to-all-start.1 = ((bf16[2,1,4,2,8,4096]{5,4,3,0,1,2:T(8,128)(2,1)}), bf16[2,1,4,2,8,4096]{5,4,3,0,1,2:T(8,128)(2,1)}, u32[]{:S(2)}, u32[]{:S(2)}) async-start(bf16[2,1,4,2,8,4096]{5,4,3,0,1,2:T(8,128)(2,1)} %reshape.427), calls=%async_computation.1 | async-start | bytes 2097152 | tf_op jit(solution)/shard_map/all_to_all | solution.py:105
  103.3 5.6 %fusion.68 = f32[2,32,32,128]{3,0,2,1:T(2,128)} fusion(bf16[32,32,32,128]{3,0,2,1:T(8,128)(2,1)} %copy-done.4, bf16[2,32,2]{1,2,0:T(2,128)(2,1)} %copy-done.8), kind=kOutput, calls=%fused_computation.113 | convolution fusion | flops 16777216 | bytes 9437696 | tf_op jit(solution)/shard_map/pn,pyzx->nyzx/dot_general | solution.py:147
  108.9 4.4 %all-to-all-done.1 = bf16[2,1,4,2,8,4096]{5,4,3,0,1,2:T(8,128)(2,1)} async-done(((bf16[2,1,4,2,8,4096]{5,4,3,0,1,2:T(8,128)(2,1)}), bf16[2,1,4,2,8,4096]{5,4,3,0,1,2:T(8,128)(2,1)}, u32[]{:S(2)}, u32[]{:S(2)}) %all-to-all-start.1) | async-done | bytes 1048608 | tf_op jit(solution)/shard_map/all_to_all | solution.py:105
  113.3 5.6 %reshape.428 = bf16[2,2,8,4,128,32]{5,4,2,1,0,3:T(8,128)(2,1)} reshape(bf16[2,1,1,2,8,4,4096]{6,4,3,0,5,2,1:T(8,128)(2,1)} %bitcast.19) | data formatting | bytes 2097152 | tf_op jit(solution)/shard_map/reshape | solution.py:112
  118.9 3.4 bitcast_convert_fusion.2
  122.3 3.6 fusion.7
  125.9 3.2 fusion.13
  132.0 4.2 %all-to-all-start.2 = ((bf16[2,1,1,2,8,128,128]{6,4,0,3,2,1,5:T(8,128)(2,1)}), bf16[2,1,1,2,8,128,128]{6,4,0,3,2,1,5:T(8,128)(2,1)}, u32[]{:S(2)}, u32[]{:S(2)}) async-start(bf16[2,1,1,2,8,128,128]{6,4,0,3,2,1,5:T(8,128)(2,1)} %copy.79), calls=%async_computation.2 | async-start | bytes 2097152 | tf_op jit(solution)/shard_map/all_to_all | solution.py:133
  138.3 5.6 %fusion.66 = f32[2,32,32,128]{3,0,2,1:T(2,128)} fusion(bf16[32,32,32,128]{3,0,2,1:T(8,128)(2,1)} %copy-done.2, bf16[2,32,2]{1,2,0:T(2,128)(2,1)S(1)} %copy-done.9), kind=kOutput, calls=%fused_computation.111 | convolution fusion | flops 16777216 | bytes 9437696 | tf_op jit(solution)/shard_map/pn,pyzx->nyzx/dot_general | solution.py:148
  143.8 6.9 %all-to-all-done.2 = bf16[2,1,1,2,8,128,128]{6,4,0,3,2,1,5:T(8,128)(2,1)} async-done(((bf16[2,1,1,2,8,128,128]{6,4,0,3,2,1,5:T(8,128)(2,1)}), bf16[2,1,1,2,8,128,128]{6,4,0,3,2,1,5:T(8,128)(2,1)}, u32[]{:S(2)}, u32[]{:S(2)}) %all-to-all-start.2) | async-done | bytes 1048608 | tf_op jit(solution)/shard_map/all_to_all | solution.py:133
  150.8 8.6 %copy.80 = bf16[2,1,1,2,8,4,32,128]{6,4,3,5,0,7,2,1:T(8,128)(2,1)} copy(bf16[2,1,1,2,8,4,32,128]{7,4,0,3,6,5,2,1:T(8,128)(2,1)} %bitcast.38) | data formatting | bytes 2097152 | tf_op jit(solution)/shard_map/all_to_all | solution.py:133
  159.3 6.0 %bitcast_bitcast_fusion = bf16[128,1,2,4,2,8,32]{6,5,4,3,2,1,0:T(8,128)(2,1)} fusion(bf16[2,1,1,2,8,4,32,128]{6,4,3,5,0,7,2,1:T(8,128)(2,1)} %copy.80), kind=kLoop, calls=%fused_computation.122 | loop fusion | bytes 2097152
  165.3 6.4 %reshape.429 = bf16[4,2,65536]{2,1,0:T(2,128)(2,1)} reshape(bf16[128,1,2,4,2,8,32]{6,5,4,3,2,1,0:T(8,128)(2,1)} %bitcast_bitcast_fusion) | data formatting | bytes 2097152
  171.7 4.2 %all-to-all-start.3 = ((bf16[4,2,65536]{2,1,0:T(2,128)(2,1)}), bf16[4,2,65536]{2,1,0:T(2,128)(2,1)}, u32[]{:S(2)}, u32[]{:S(2)}) async-start(bf16[4,2,65536]{2,1,0:T(2,128)(2,1)} %reshape.429), calls=%async_computation.3 | async-start | bytes 2097152 | tf_op jit(solution)/shard_map/all_to_all | solution.py:132
  185.1 156.5 %all-reduce.2.cloned.1.call-done = bf16[8,128,128]{1,2,0:T(8,128)(2,1)} async-done(((bf16[8,128,128]{1,2,0:T(8,128)(2,1)}), bf16[8,128,128]{1,2,0:T(8,128)(2,1)}) %all-reduce.2.cloned.1.call-update) | async-done | bytes 262160 | tf_op jit(solution)/shard_map/psum | solution.py:123
  343.5 5.1 %reshape.430 = bf16[128,1,2,4,2,8,32]{6,5,4,3,2,1,0:T(8,128)(2,1)} reshape(bf16[4,2,65536]{2,1,0:T(2,128)(2,1)} %all-to-all-done.3) | data formatting | bytes 2097152
  348.6 10.4 %copy.82 = bf16[2,4,1,2,8,32,4,32]{7,6,4,5,0,1,3,2:T(4,128)(2,1)} copy(bf16[2,4,1,2,8,32,4,32]{5,4,3,1,0,7,6,2:T(8,128)(2,1)} %bitcast.202) | data formatting | bytes 2097152 | tf_op jit(solution)/shard_map/all_to_all | solution.py:132
  359.1 6.5 %fusion.5 = bf16[2,32,32,256]{3,2,1,0:T(8,128)(2,1)} fusion(f32[2,32,32,128]{3,2,1,0:T(8,128)} %copy_add_fusion, f32[2,32,32,128]{3,2,1,0:T(8,128)S(1)} %copy-done.5, bf16[2,32,32,256]{3,2,1,0:T(8,128)(2,1)S(1)} %broadcast_select_fusion, bf16[2,4,1,2,8,32,4,32]{7,6,4,5,0,1,3,2:T(4,128)(2,1)} %copy.82, f32[32,32,256]{2,1,0:T(8,128)} %pad_maximum_fusion, ...), kind=kOutput, calls=%fused_computation.9 | convolution fusion | flops 272105472 | bytes 6684672 | tf_op jit(solution)/shard_map/npqcxyz,cpqxk->nyzk/dot_general | solution.py:139
  (76 shorter events, 44.0 us)
Async XLA Ops:
  7.2 22.4 %copy-start = (bf16[4,32,32,128]{3,2,1,0:T(8,128)(2,1)S(1)}, bf16[4,32,32,128]{3,2,1,0:T(8,128)(2,1)}, u32[]{:S(2)}) copy-start(bf16[4,32,32,128]{3,2,1,0:T(8,128)(2,1)} %param.12) | copy-start | bytes 3145732
  12.9 15.9 %copy-start.12 = (f32[8,3]{0,1:T(4,128)S(1)}, f32[8,3]{0,1:T(4,128)}, u32[]{:S(2)}) copy-start(f32[8,3]{0,1:T(4,128)} %param.13) | copy-start | bytes 292
  12.9 15.9 %copy-start.13 = (s32[32]{0:T(128)S(1)}, s32[32]{0:T(128)}, u32[]{:S(2)}) copy-start(s32[32]{0:T(128)} %param.14) | copy-start | bytes 388
  12.9 16.6 %copy-start.14 = (s32[32]{0:T(128)S(1)}, s32[32]{0:T(128)}, u32[]{:S(2)}) copy-start(s32[32]{0:T(128)} %param.15) | copy-start | bytes 388
  23.2 66.6 %all-to-all-start = ((bf16[2,4,4,2,8,1024]{5,4,3,2,0,1:T(8,128)(2,1)}), bf16[2,4,4,2,8,1024]{5,4,3,2,0,1:T(8,128)(2,1)}, u32[]{:S(2)}, u32[]{:S(2)}) async-start(bf16[2,4,4,2,8,1024]{5,4,3,2,0,1:T(8,128)(2,1)} %reshape.426), calls=%async_computation | async-start | bytes 2097152 | tf_op jit(solution)/shard_map/all_to_all | solution.py:106
  29.6 13.0 %copy-start.6 = (bf16[2,32,32,128]{3,2,1,0:T(8,128)(2,1)S(1)}, bf16[2,32,32,128]{3,2,1,0:T(8,128)(2,1)}, u32[]{:S(2)}) copy-start(bf16[2,32,32,128]{3,2,1,0:T(8,128)(2,1)} %get-tuple-element.8) | copy-start | bytes 1572868
  42.5 4.6 %copy-start.4 = (bf16[32,32,32,128]{3,0,2,1:T(8,128)(2,1)}, bf16[32,32,32,128]{3,0,2,1:T(8,128)(2,1)S(1)}, u32[]{:S(2)}) copy-start(bf16[32,32,32,128]{3,0,2,1:T(8,128)(2,1)S(1)} %get-tuple-element.4) | copy-start | bytes 25165828
  42.5 6.9 %copy-start.2 = (bf16[32,32,32,128]{3,0,2,1:T(8,128)(2,1)}, bf16[32,32,32,128]{3,0,2,1:T(8,128)(2,1)S(1)}, u32[]{:S(2)}) copy-start(bf16[32,32,32,128]{3,0,2,1:T(8,128)(2,1)S(1)} %get-tuple-element.5) | copy-start | bytes 25165828
  42.5 2.3 copy-start.7
  47.1 35.7 %copy-start.11 = (f32[32]{0:T(128)S(1)}, f32[32]{0:T(128)}, u32[]{:S(2)}) copy-start(f32[32]{0:T(128)} %param.16) | copy-start | bytes 388
  82.8 5.8 %copy-start.3 = (bf16[32,32,32,128]{3,0,2,1:T(8,128)(2,1)S(1)}, bf16[32,32,32,128]{3,0,2,1:T(8,128)(2,1)}, u32[]{:S(2)}) copy-start(bf16[32,32,32,128]{3,0,2,1:T(8,128)(2,1)} %copy-done.2) | copy-start | bytes 25165828
  82.9 5.3 %copy-start.8 = (bf16[2,32,2]{1,2,0:T(2,128)(2,1)}, bf16[2,32,2]{1,2,0:T(2,128)(2,1)S(1)}, u32[]{:S(2)}) copy-start(bf16[2,32,2]{1,2,0:T(2,128)(2,1)S(1)} %multiply_convert_fusion.4) | copy-start | bytes 772
  95.5 17.8 %all-to-all-start.1 = ((bf16[2,1,4,2,8,4096]{5,4,3,0,1,2:T(8,128)(2,1)}), bf16[2,1,4,2,8,4096]{5,4,3,0,1,2:T(8,128)(2,1)}, u32[]{:S(2)}, u32[]{:S(2)}) async-start(bf16[2,1,4,2,8,4096]{5,4,3,0,1,2:T(8,128)(2,1)} %reshape.427), calls=%async_computation.1 | async-start | bytes 2097152 | tf_op jit(solution)/shard_map/all_to_all | solution.py:105
  125.9 12.4 %copy-start.9 = (bf16[2,32,2]{1,2,0:T(2,128)(2,1)S(1)}, bf16[2,32,2]{1,2,0:T(2,128)(2,1)}, u32[]{:S(2)}) copy-start(bf16[2,32,2]{1,2,0:T(2,128)(2,1)} %copy-done.8) | copy-start | bytes 772
  132.0 18.8 %all-to-all-start.2 = ((bf16[2,1,1,2,8,128,128]{6,4,0,3,2,1,5:T(8,128)(2,1)}), bf16[2,1,1,2,8,128,128]{6,4,0,3,2,1,5:T(8,128)(2,1)}, u32[]{:S(2)}, u32[]{:S(2)}) async-start(bf16[2,1,1,2,8,128,128]{6,4,0,3,2,1,5:T(8,128)(2,1)} %copy.79), calls=%async_computation.2 | async-start | bytes 2097152 | tf_op jit(solution)/shard_map/all_to_all | solution.py:133
  159.3 20.8 %copy-start.10 = (f32[2]{0:T(128)S(1)}, f32[2]{0:T(128)}, u32[]{:S(2)}) copy-start(f32[2]{0:T(128)} %param.17) | copy-start | bytes 28
  171.7 171.8 %all-to-all-start.3 = ((bf16[4,2,65536]{2,1,0:T(2,128)(2,1)}), bf16[4,2,65536]{2,1,0:T(2,128)(2,1)}, u32[]{:S(2)}, u32[]{:S(2)}) async-start(bf16[4,2,65536]{2,1,0:T(2,128)(2,1)} %reshape.429), calls=%async_computation.3 | async-start | bytes 2097152 | tf_op jit(solution)/shard_map/all_to_all | solution.py:132
  176.0 165.6 %all-reduce.2.cloned.1.call-start = ((), (), s32[]{:S(2)}) async-start(), calls=%async_computation.4 | async-start | bytes 524288 | tf_op jit(solution)/shard_map/psum | solution.py:123
  182.3 176.8 %copy-start.5 = (f32[2,32,32,128]{3,2,1,0:T(8,128)S(1)}, f32[2,32,32,128]{3,2,1,0:T(8,128)}, u32[]{:S(2)}) copy-start(f32[2,32,32,128]{3,2,1,0:T(8,128)} %copy_subtract_fusion) | copy-start | bytes 3145732
  359.1 6.5 %copy-start.1 = (bf16[4,32,32,128]{3,2,1,0:T(8,128)(2,1)S(1)}, bf16[4,32,32,128]{3,2,1,0:T(8,128)(2,1)}, u32[]{:S(2)}) copy-start(bf16[4,32,32,128]{3,2,1,0:T(8,128)(2,1)} %param.12) | copy-start | bytes 3145732
Sparse Core Ops, SparseCore 0:
  182.4 159.1 all-reduce.1
where the time goes:
time: 374 us; the launch traced here: 372 us
  waiting for transfers between devices  168 us (45%)
  local copies, waits for them, and re-layouts  68.5 us (18%)
  matrix products  57.3 us (15%)
  blocking collectives  31.1 us (8%)
  starting transfers between devices  17.7 us (5%)
  other arithmetic  15.7 us (4%)
  between operations  14.3 us (4%)
    psum x1, waiting for transfers between devices, shards(): lax.psum(partial_density.astype(jnp.bfloat16), 'band').astype(jnp.float32)  157 us
    psum x1, blocking collectives, shards(): intersections = lax.psum(partial_intersections, ('gy', 'gz'))  31.1 us
    unnamed x35, local copies, waits for them, and re-layouts  21.9 us
    dot_general x1, matrix products, projector_parts(): jnp.einsum('bc,cyzx->byzx', kind_hot, channels, preferred_element_type=jn...  12.9 us
    all_to_all x1, local copies, waits for them, and re-layouts, shards(): lax.all_to_all(lax.all_to_all(folded, 'gy', split_axis=5, concat_axis=1,...  10.4 us
    reshape x2, local copies, waits for them, and re-layouts, shards(): spread.reshape(orbit_count, parts_y, parts_z, 2, thin_x, rows_y * rows_z)  10.2 us
    all_to_all x1, local copies, waits for them, and re-layouts, shards(): lax.all_to_all(folded, 'gy', split_axis=5, concat_axis=1, tiled=True)  8.56 us
  transfers between devices with their start and end apart: 5, of which 3 were waited for; matrix products, arithmetic and copies ran while one was open for 15% of the time, Pallas kernels for 0%

commit v1 on v0

v1 whole, which is shorter than its diff:
```python
import functools
import math

import jax
import jax.numpy as jnp
import ml_dtypes
import numpy as np
from jax import lax
from jax.experimental import pallas as pl
from jax.experimental.pallas import tpu as pltpu
from jax.sharding import PartitionSpec as P

kinetic_scale = 1.0 / 1024.0
vmem_bytes = 48 * 1024 * 1024
bf16 = jnp.bfloat16
f32 = jnp.float32


def dft_table(length, sign_value):
    grid_index = np.arange(length)
    product = grid_index[:, None] * grid_index[None, :] % length
    phase_angle = np.float32(2.0 * math.pi / length) * product.astype(np.float32)
    cosine_part = np.cos(phase_angle) / np.float32(math.sqrt(length))
    sine_part = sign_value * np.sin(phase_angle) / np.float32(math.sqrt(length))
    upper_rows = np.stack([cosine_part, -sine_part], axis=1)
    lower_rows = np.stack([sine_part, cosine_part], axis=1)
    return np.stack([upper_rows, lower_rows], axis=0).astype(np.float32)


def rounded(table, rows):
    return jnp.asarray(np.ascontiguousarray(table).reshape(rows, -1).astype(ml_dtypes.bfloat16))


def frequencies(first_index, span, length):
    grid_index = first_index + jnp.arange(span, dtype=jnp.int32)
    return jnp.where(grid_index >= length // 2, grid_index - length, grid_index).astype(f32)


def axis_phase(coordinate, freq):
    phase_angle = 2.0 * math.pi * (coordinate[:, None] * freq[None, :])
    return (jnp.cos(phase_angle), jnp.sin(phase_angle))


def dot(left, right):
    return jnp.dot(left, right, preferred_element_type=f32)


def dot_nt(left, right):
    return lax.dot_general(left, right, (((1,), (1,)), ((), ())), preferred_element_type=f32)


def dot_tn(left, right):
    return lax.dot_general(left, right, (((0,), (0,)), ((), ())), preferred_element_type=f32)


def spread_kernel(orbitals_ref, mask_ref, table_ref, out_ref):
    length = mask_ref.shape[2]
    dests = out_ref.shape[0]
    thin = length // dests
    mask = jnp.where(mask_ref[...] != 0, 1.0, 0.0).astype(bf16)
    mask = jnp.concatenate([mask, mask], axis=2)
    lane = lax.broadcasted_iota(jnp.int32, (length, 128), 1)
    for pair in range(0, mask_ref.shape[0], 2):
        rows = []
        for y in (pair, pair + 1):
            both = jnp.concatenate([orbitals_ref[0, y] * mask[y], orbitals_ref[1, y] * mask[y]], axis=0)
            rows += [both, both]
        spread = dot_nt(table_ref[...], jnp.concatenate(rows, axis=0))
        tiles = []
        for half in range(2):
            cols = slice(half * 128, half * 128 + 128)
            tile = jnp.where(lane < 64, spread[:length, cols], spread[length:, cols])
            tiles.append(tile.reshape(dests, thin, 128))
        out_ref[:, pair * thin : (pair + 2) * thin, :] = jnp.concatenate(tiles, axis=1).astype(bf16)


def overlap_kernel(orbitals_ref, mask_ref, channels_ref, phase_ref, wave_ref, out_ref, sums_ref):
    step = pl.program_id(0)
    rows = mask_ref.shape[0] * mask_ref.shape[1]
    length = mask_ref.shape[2]
    atoms = wave_ref.shape[0] // 2
    kinds = channels_ref.shape[0]
    mask = jnp.where(mask_ref[...] != 0, 1.0, 0.0).astype(bf16)
    orbs = [orbitals_ref[n].reshape(rows, 2 * length) for n in range(2)]
    columns = []
    for c in range(kinds):
        radial = (channels_ref[c] * mask).reshape(rows, length)
        radial = jnp.concatenate([radial, radial], axis=1)
        columns += [radial * orbs[0], radial * orbs[1]]
    part = dot(phase_ref[...], jnp.concatenate(columns, axis=1))

    @pl.when(step == 0)
    def first():
        sums_ref[...] = part

    @pl.when(step > 0)
    def later():
        sums_ref[...] += part

    @pl.when(step == pl.num_programs(0) - 1)
    def last():
        cos_x, sin_x = wave_ref[:atoms], wave_ref[atoms:]
        lane = lax.broadcasted_iota(jnp.int32, (atoms, 128), 1)
        total = jnp.zeros((atoms, 128), f32)
        for pair in range(kinds * 2):
            base = pair * 2 * length
            real_cols = slice(base, base + length)
            imag_cols = slice(base + length, base + 2 * length)
            real = sums_ref[:atoms, real_cols] - sums_ref[atoms:, imag_cols]
            imag = sums_ref[atoms:, real_cols] + sums_ref[:atoms, imag_cols]
            real_over = jnp.sum(real * cos_x - imag * sin_x, axis=1, keepdims=True)
            imag_over = jnp.sum(real * sin_x + imag * cos_x, axis=1, keepdims=True)
            total = jnp.where(lane == 2 * pair, real_over, total)
            total = jnp.where(lane == 2 * pair + 1, imag_over, total)
        high = total.astype(bf16).astype(f32)
        out_ref[...] = jnp.concatenate([high, total - high], axis=0).astype(bf16)


def field_kernel(arrived_ref, potential_ref, weight_ref, z_ref, y_ref, density_ref, scaled_ref, work_ref):
    thin = potential_ref.shape[0]
    length = potential_ref.shape[1]
    parts = arrived_ref.shape[0] // 4
    rows = arrived_ref.shape[1]
    for sy in range(parts):
        columns = jnp.concatenate([arrived_ref[sy * 4 + sz] for sz in range(4)], axis=1)
        halfway = dot(columns, z_ref[...])
        for tile in range(4):
            work_ref[tile, sy * rows : (sy + 1) * rows, :] = halfway[:, tile * 128 : tile * 128 + 128]
    for x in range(thin):
        plane = [work_ref[tile, pl.ds(x, length, stride=thin), :].astype(bf16) for tile in range(4)]
        stacked = jnp.concatenate(
            [
                jnp.concatenate([plane[0], plane[2]], axis=1),
                jnp.concatenate([plane[1], plane[3]], axis=1),
            ],
            axis=0,
        )
        field = dot(y_ref[...], stacked)
        real, imag = field[:length], field[length:]
        square = real * real + imag * imag
        density = weight_ref[0] * square[:, :length] + weight_ref[1] * square[:, length:]
        density_ref[x * length : (x + 1) * length, :] = density.astype(bf16)
        potential = potential_ref[x]
        potential = jnp.concatenate([potential, potential], axis=1)
        potential = jnp.concatenate([potential, potential], axis=0)
        scaled_ref[x] = (potential * field).astype(bf16)


def fold_kernel(scaled_ref, overlap_ref, z_ref, y_ref, out_ref, work_ref):
    thin = scaled_ref.shape[0]
    length = scaled_ref.shape[1] // 2
    parts = out_ref.shape[0] // 4
    rows = length * thin // parts
    for x in range(thin):
        folded = dot(y_ref[...], scaled_ref[x]).astype(bf16)
        real, imag = folded[:length], folded[length:]
        columns = jnp.concatenate(
            [real[:, :length], imag[:, :length], real[:, length:], imag[:, length:]], axis=1
        )
        halfway = dot(columns, z_ref[...])
        for tile in range(4):
            work_ref[tile, pl.ds(x, length, stride=thin), :] = halfway[:, tile * 128 : tile * 128 + 128]
    for sy in range(parts):
        for sz in range(4):
            block = work_ref[sz, sy * rows : (sy + 1) * rows, :]
            out_ref[sy * 4 + sz, :rows, :] = block.astype(bf16)
    for s in range(out_ref.shape[0]):
        out_ref[s, rows:, :] = overlap_ref[...]


def apply_kernel(
    first_ref,
    returned_ref,
    overlap_ref,
    orbitals_ref,
    mask_ref,
    channels_ref,
    phase_ref,
    wave_ref,
    strength_ref,
    table_ref,
    out_ref,
    factor_ref,
):
    step = pl.program_id(0)
    rows_y, rows_z, length = mask_ref.shape
    atoms = wave_ref.shape[0] // 2
    kinds = channels_ref.shape[0]
    sources = returned_ref.shape[0]
    thin = length // sources

    @pl.when(step == 0)
    def factors():
        cos_x, sin_x = wave_ref[:atoms], wave_ref[atoms:]
        summed = jnp.sum(overlap_ref[...].astype(f32), axis=0)
        coef = (summed[:atoms] + summed[atoms:]) * strength_ref[...]
        for pair in range(kinds * 2):
            coef_real = coef[:, 2 * pair : 2 * pair + 1]
            coef_imag = coef[:, 2 * pair + 1 : 2 * pair + 2]
            real = cos_x * coef_real + sin_x * coef_imag
            imag = cos_x * coef_imag - sin_x * coef_real
            base = pair * 2 * length
            factor_ref[:, base : base + length] = jnp.concatenate([real, imag], axis=0).astype(bf16)
            factor_ref[:, base + length : base + 2 * length] = jnp.concatenate(
                [imag, -real], axis=0
            ).astype(bf16)

    def squared(start, axis):
        index = start + lax.broadcasted_iota(jnp.int32, mask_ref.shape, axis)
        wave = jnp.where(index >= length // 2, index - length, index)
        return wave * wave

    energy = squared(first_ref[0] + step * rows_y, 0) + squared(first_ref[1], 1) + squared(0, 2)
    energy = kinetic_scale * 0.5 * energy.astype(f32)
    inside = mask_ref[...] != 0
    phase = phase_ref[...]
    for pair in range(0, rows_y, 2):
        block = returned_ref[:, pair * thin : (pair + 2) * thin, :].astype(f32)
        planes = jnp.concatenate(
            [
                block[:, :thin].reshape(length, 128).astype(bf16),
                block[:, thin:].reshape(length, 128).astype(bf16),
            ],
            axis=1,
        )
        local = dot_tn(planes, table_ref[...])
        extra = dot_tn(phase[:, pair * rows_z : (pair + 2) * rows_z], factor_ref[...])
        for half in range(2):
            y = pair + half
            top = local[half * 128 : half * 128 + 64, : 2 * length]
            low = local[half * 128 + 64 : half * 128 + 128, 2 * length :]
            both = top + low
            radials = [channels_ref[c, y].astype(f32) for c in range(kinds)]
            for n in range(2):
                for part in range(2):
                    cols = slice(part * length, part * length + length)
                    total = both[n * rows_z : (n + 1) * rows_z, cols]
                    total = total + energy[y] * orbitals_ref[n, y, :, cols].astype(f32)
                    for c in range(kinds):
                        base = ((c * 2 + n) * 2 + part) * length
                        total = total + radials[c] * extra[
                            half * rows_z : (half + 1) * rows_z, base : base + length
                        ]
                    total = jnp.where(inside[y], total, 0.0)
                    out_ref[n, y, :, cols] = total.astype(bf16)


def shards(
    orbitals,
    potential,
    cutoff_mask,
    channels,
    positions,
    proj_atom,
    proj_chan,
    coupling,
    occupations,
):
    rows_y, rows_z, length = cutoff_mask.shape
    parts_y = lax.axis_size("gy")
    parts_z = lax.axis_size("gz")
    parts_band = lax.axis_size("band")
    places = parts_y * parts_z
    thin = length // places
    atoms = positions.shape[0]
    kinds = channels.shape[0]
    block = rows_y * thin
    inverse = dft_table(length, 1.0)
    forward = dft_table(length, -1.0)
    pick = np.eye(2, dtype=np.float32)
    split_inverse = inverse.reshape(2, length, 2, parts_z, rows_z)
    split_forward = forward.reshape(2, parts_z, rows_z, 2, length)
    inv_x = rounded(inverse, 2 * length)
    inv_z = rounded(np.einsum("fzcsl,nm->scnlmfz", split_inverse, pick), 4 * length)
    fwd_z = rounded(np.einsum("cslfz,nm->nfzscml", split_forward, pick), 4 * length)
    fwd_y = rounded(forward, 2 * length)
    fwd_x = rounded(np.einsum("rkcx->xcrk", forward), length)
    first_y = lax.axis_index("gy") * rows_y
    first_z = lax.axis_index("gz") * rows_z

    params = pltpu.CompilerParams(vmem_limit_bytes=vmem_bytes)
    steps = 4
    span = rows_y // steps
    whole = lambda *shape: pl.BlockSpec(shape, lambda i: (0,) * len(shape))
    orbitals_spec = pl.BlockSpec((2, span, rows_z, 2 * length), lambda i: (0, i, 0, 0))
    mask_spec = pl.BlockSpec((span, rows_z, length), lambda i: (i, 0, 0))
    channels_spec = pl.BlockSpec((kinds, span, rows_z, length), lambda i: (0, i, 0, 0))
    phase_spec = pl.BlockSpec((2 * atoms, span * rows_z), lambda i: (0, i))
    blocks_spec = pl.BlockSpec((places, span * thin, 128), lambda i: (0, i, 0))
    tile_spec = pl.BlockSpec((places, 16, 128), lambda i: (0, block // 16, 0))
    smem_spec = pl.BlockSpec(memory_space=pltpu.SMEM)

    spread = pl.pallas_call(
        spread_kernel,
        grid=(steps,),
        in_specs=[orbitals_spec, mask_spec, whole(2 * length, 2 * length)],
        out_specs=blocks_spec,
        out_shape=jax.ShapeDtypeStruct((places, block, 128), bf16),
        compiler_params=params,
        name="spread",
    )(orbitals, cutoff_mask, inv_x)
    arrived = lax.all_to_all(spread, ("gy", "gz"), split_axis=0, concat_axis=0, tiled=True)

    cos_y, sin_y = axis_phase(positions[:, 1], frequencies(first_y, rows_y, length))
    cos_z, sin_z = axis_phase(positions[:, 2], frequencies(first_z, rows_z, length))
    cos_x, sin_x = axis_phase(positions[:, 0], frequencies(0, length, length))
    cos_yz = cos_y[:, :, None] * cos_z[:, None, :] - sin_y[:, :, None] * sin_z[:, None, :]
    sin_yz = sin_y[:, :, None] * cos_z[:, None, :] + cos_y[:, :, None] * sin_z[:, None, :]
    phase = jnp.concatenate([cos_yz, sin_yz], axis=0).astype(bf16).reshape(2 * atoms, rows_y * rows_z)
    wave = jnp.concatenate([cos_x, sin_x], axis=0)
    chosen = (proj_atom[None, :] == jnp.arange(atoms, dtype=jnp.int32)[:, None])[:, None, :] & (
        proj_chan[None, :] == jnp.arange(kinds, dtype=jnp.int32)[:, None]
    )[None, :, :]
    strength = jnp.sum(jnp.where(chosen, coupling[None, None, :], 0.0), axis=2)
    strength = jnp.pad(jnp.repeat(strength, 4, axis=1), ((0, 0), (0, 128 - 4 * kinds)))

    overlap = pl.pallas_call(
        overlap_kernel,
        grid=(steps,),
        in_specs=[orbitals_spec, mask_spec, channels_spec, phase_spec, whole(2 * atoms, length)],
        out_specs=whole(2 * atoms, 128),
        out_shape=jax.ShapeDtypeStruct((2 * atoms, 128), bf16),
        scratch_shapes=[pltpu.VMEM((2 * atoms, kinds * 4 * length), f32)],
        compiler_params=params,
        name="overlap",
    )(orbitals, cutoff_mask, channels, phase, wave)

    density_part, scaled = pl.pallas_call(
        field_kernel,
        grid=(1,),
        in_specs=[
            whole(places, block, 128),
            whole(thin, length, length),
            smem_spec,
            whole(4 * length, 4 * length),
            whole(2 * length, 2 * length),
        ],
        out_specs=[whole(thin * length, length), whole(thin, 2 * length, 2 * length)],
        out_shape=[
            jax.ShapeDtypeStruct((thin * length, length), bf16),
            jax.ShapeDtypeStruct((thin, 2 * length, 2 * length), bf16),
        ],
        scratch_shapes=[pltpu.VMEM((4, length * thin, 128), f32)],
        compiler_params=params,
        name="field",
    )(arrived, potential, occupations, inv_z, inv_x)
    density_parts = lax.all_to_all(
        density_part.reshape(parts_band, -1, length), "band", split_axis=0, concat_axis=0, tiled=True
    )

    folded = pl.pallas_call(
        fold_kernel,
        grid=(1,),
        in_specs=[
            whole(thin, 2 * length, 2 * length),
            whole(2 * atoms, 128),
            whole(4 * length, 4 * length),
            whole(2 * length, 2 * length),
        ],
        out_specs=whole(places, block + 16, 128),
        out_shape=jax.ShapeDtypeStruct((places, block + 16, 128), bf16),
        scratch_shapes=[pltpu.VMEM((4, length * thin, 128), f32)],
        compiler_params=params,
        name="fold",
    )(scaled, overlap, fwd_z, fwd_y)
    returned = lax.all_to_all(folded, ("gy", "gz"), split_axis=0, concat_axis=0, tiled=True)

    density_own = jnp.sum(density_parts.astype(f32), axis=0).astype(bf16)
    density_copies = jnp.broadcast_to(density_own[None], density_parts.shape)
    density = lax.all_to_all(density_copies, "band", split_axis=0, concat_axis=0, tiled=True)

    applied = pl.pallas_call(
        apply_kernel,
        grid=(steps,),
        in_specs=[
            smem_spec,
            blocks_spec,
            tile_spec,
            orbitals_spec,
            mask_spec,
            channels_spec,
            phase_spec,
            whole(2 * atoms, length),
            whole(atoms, 128),
            whole(length, 4 * length),
        ],
        out_specs=orbitals_spec,
        out_shape=jax.ShapeDtypeStruct(orbitals.shape, bf16),
        scratch_shapes=[pltpu.VMEM((2 * atoms, kinds * 4 * length), bf16)],
        compiler_params=params,
        name="apply",
    )(
        jnp.stack([first_y, first_z]).astype(jnp.int32),
        returned,
        returned,
        orbitals,
        cutoff_mask,
        channels,
        phase,
        wave,
        strength,
        fwd_x,
    )
    return (applied, density.astype(f32).reshape(potential.shape))


def solution(mesh):
    placed = (
        P("band", "gy", "gz", None),
        P(("gy", "gz"), None, None),
        P("gy", "gz", None),
        P(None, "gy", "gz", None),
        P(),
        P(),
        P(),
        P(),
        P("band"),
    )
    return jax.shard_map(
        shards,
        mesh=mesh,
        in_specs=placed,
        out_specs=(P("band", "gy", "gz", None), P(("gy", "gz"), None, None)),
        check_vma=False,
    )
```

time: 374 us -> 102 us (0.27)
  the two profiles are of different devices: /device:TPU:32 before, /device:TPU:1 now
where the time goes in v1:
time: 102 us; the launch traced here: 101 us
  waiting for transfers between devices  47 us (46%)
  starting transfers between devices  30.5 us (30%)
  Pallas kernels  13.6 us (13%)
  local copies, waits for them, and re-layouts  7.54 us (7%)
  other arithmetic  1.45 us (1%)
    all_to_all x1, waiting for transfers between devices, shards(): lax.all_to_all(spread, ('gy', 'gz'), split_axis=0, concat_axis=0, tiled=T...  15.2 us
    all_to_all x1, waiting for transfers between devices, shards(): lax.all_to_all(folded, ('gy', 'gz'), split_axis=0, concat_axis=0, tiled=T...  14.7 us
    all_to_all x1, waiting for transfers between devices, shards(): lax.all_to_all(density_part.reshape(parts_band, -1, length), 'band', spli...  10.9 us
    all_to_all x1, starting transfers between devices, shards(): lax.all_to_all(density_part.reshape(parts_band, -1, length), 'band', spli...  10.6 us
    all_to_all x1, starting transfers between devices, shards(): lax.all_to_all(folded, ('gy', 'gz'), split_axis=0, concat_axis=0, tiled=T...  9.21 us
    all_to_all x1, starting transfers between devices, shards(): lax.all_to_all(spread, ('gy', 'gz'), split_axis=0, concat_axis=0, tiled=T...  7.06 us
    unnamed x43, local copies, waits for them, and re-layouts  6.44 us
    all_to_all x1, waiting for transfers between devices, shards(): lax.all_to_all(density_copies, 'band', split_axis=0, concat_axis=0, tiled...  6.16 us
  transfers between devices with their start and end apart: 4, of which 4 were waited for; matrix products, arithmetic and copies ran while one was open for 2% of the time, Pallas kernels for 4%

profile of v1, /device:TPU:1, one launch (start us, length us, event | category | flops | bytes accessed | tf_op | source)
XLA Modules:
  0.0 101.0 jit_solution(3411290593216303436)
XLA Ops:
  0.6 1.2 %copy-done = bf16[2,32,32,256]{3,2,1,0:T(8,128)(2,1)S(1)} copy-done((bf16[2,32,32,256]{3,2,1,0:T(8,128)(2,1)S(1)}, bf16[2,32,32,256]{3,2,1,0:T(8,128)(2,1)}, u32[]{:S(2)}) %copy-start) | copy-done | bytes 1048600
  1.9 1.0 %copy-done.2 = s32[32,32,128]{2,1,0:T(8,128)S(1)} copy-done((s32[32,32,128]{2,1,0:T(8,128)S(1)}, s32[32,32,128]{2,1,0:T(8,128)}, u32[]{:S(2)}) %copy-start.2) | copy-done | bytes 524312
  2.9 0.9 copy-done.12
  3.8 2.5 %spread.1 = bf16[16,256,128]{2,1,0:T(8,128)(2,1)} custom-call(bf16[2,32,32,256]{3,2,1,0:T(8,128)(2,1)S(1)} %copy-done, s32[32,32,128]{2,1,0:T(8,128)S(1)} %copy-done.2, bf16[256,256]{1,0:T(8,128)(2,1)S(1)} %copy-done.12), custom_call_target="tpu_custom_call" | custom-call | tf_op jit(solution)/shard_map/spread/pallas_call | solution.py:293
  6.3 7.1 %all-to-all-start = ((bf16[16,256,128]{2,1,0:T(8,128)(2,1)}), bf16[16,256,128]{2,1,0:T(8,128)(2,1)S(1)}, u32[]{:S(2)}, u32[]{:S(2)}) async-start(bf16[16,256,128]{2,1,0:T(8,128)(2,1)} %spread.1), calls=%async_computation | async-start | bytes 2097152 | tf_op jit(solution)/shard_map/all_to_all | solution.py:302
  13.5 15.2 %all-to-all-done.arrived_ref = bf16[16,256,128]{2,1,0:T(8,128)(2,1)S(1)} async-done(((bf16[16,256,128]{2,1,0:T(8,128)(2,1)}), bf16[16,256,128]{2,1,0:T(8,128)(2,1)S(1)}, u32[]{:S(2)}, u32[]{:S(2)}) %all-to-all-start) | async-done | bytes 1048608 | tf_op jit(solution)/shard_map/all_to_all | solution.py:302
  28.7 2.6 %field.1 = (bf16[1024,128]{1,0:T(8,128)(2,1)}, bf16[8,256,256]{2,1,0:T(8,128)(2,1)S(1)}) custom-call(bf16[16,256,128]{2,1,0:T(8,128)(2,1)S(1)} %all-to-all-done.arrived_ref, f32[8,128,128]{2,1,0:T(8,128)S(1)} %copy-done.9, f32[2]{0:T(128)S(1)} %copy-done.16, bf16[512,512]{1,0:T(8,128)(2,1)S(1)} %copy-done.10, bf16[256,256]{1,0:T(8,128)(2,1)S(1)} %copy-done.13), custom_call_target="tpu_custom_call" | custom-call | tf_op jit(solution)/shard_map/field/pallas_call | solution.py:328
  31.3 1.0 copy-done.7
  32.2 10.6 %all-to-all-start.2 = ((bf16[16,64,128]{2,1,0:T(8,128)(2,1)}), bf16[16,64,128]{2,1,0:T(8,128)(2,1)S(1)}, u32[]{:S(2)}, u32[]{:S(2)}) async-start(bf16[16,64,128]{2,1,0:T(8,128)(2,1)} %bitcast.6), calls=%async_computation.2 | async-start | bytes 524288 | tf_op jit(solution)/shard_map/all_to_all | solution.py:347
  42.9 0.1 add_convert_fusion
  43.1 0.1 add.49
  43.2 0.1 sub.20
  43.4 10.9 %all-to-all-done.2 = bf16[16,64,128]{2,1,0:T(8,128)(2,1)S(1)} async-done(((bf16[16,64,128]{2,1,0:T(8,128)(2,1)}), bf16[16,64,128]{2,1,0:T(8,128)(2,1)S(1)}, u32[]{:S(2)}, u32[]{:S(2)}) %all-to-all-start.2) | async-done | bytes 262176 | tf_op jit(solution)/shard_map/all_to_all | solution.py:347
  54.3 0.8 broadcast_in_dim.15
  55.0 3.6 %all-to-all-start.3 = ((bf16[16,64,128]{2,1,0:T(8,128)(2,1)}), bf16[16,64,128]{2,1,0:T(8,128)(2,1)S(1)}, u32[]{:S(2)}, u32[]{:S(2)}) async-start(bf16[16,64,128]{2,1,0:T(8,128)(2,1)} %broadcast_in_dim.15), calls=%async_computation.3 | async-start | bytes 524288 | tf_op jit(solution)/shard_map/all_to_all | solution.py:370
  58.9 1.4 %overlap.1.overlap_ref = bf16[16,128]{1,0:T(8,128)(2,1)S(1)} custom-call(bf16[2,32,32,256]{3,2,1,0:T(8,128)(2,1)S(1)} %copy-done.1, s32[32,32,128]{2,1,0:T(8,128)S(1)} %copy-done.3, bf16[4,32,32,128]{3,2,1,0:T(8,128)(2,1)S(1)} %copy-done.5, bf16[16,1024]{1,0:T(8,128)(2,1)S(1)} %constant_dynamic-update-slice_fusion.phase_ref, ...), custom_call_target="tpu_custom_call" | custom-call | tf_op jit(solution)/shard_map/overlap/pallas_call | solution.py:317
  60.3 2.3 %fold.1 = bf16[16,272,128]{2,1,0:T(8,128)(2,1)S(1)} custom-call(bf16[8,256,256]{2,1,0:T(8,128)(2,1)S(1)} %copy-done.8, bf16[16,128]{1,0:T(8,128)(2,1)S(1)} %overlap.1.overlap_ref, bf16[512,512]{1,0:T(8,128)(2,1)S(1)} %copy-done.11, bf16[256,256]{1,0:T(8,128)(2,1)S(1)} %copy-done.15), custom_call_target="tpu_custom_call" | custom-call | tf_op jit(solution)/shard_map/fold/pallas_call | solution.py:351
  62.6 1.0 copy-done.4
  63.7 6.2 %all-to-all-done.3 = bf16[16,64,128]{2,1,0:T(8,128)(2,1)S(1)} async-done(((bf16[16,64,128]{2,1,0:T(8,128)(2,1)}), bf16[16,64,128]{2,1,0:T(8,128)(2,1)S(1)}, u32[]{:S(2)}, u32[]{:S(2)}) %all-to-all-start.3) | async-done | bytes 262176 | tf_op jit(solution)/shard_map/all_to_all | solution.py:370
  69.8 9.2 %all-to-all-start.1 = ((bf16[16,272,128]{2,1,0:T(8,128)(2,1)}), bf16[16,272,128]{2,1,0:T(8,128)(2,1)S(1)}, u32[]{:S(2)}, u32[]{:S(2)}) async-start(bf16[16,272,128]{2,1,0:T(8,128)(2,1)} %copy-done.4), calls=%async_computation.1 | async-start | bytes 2228224 | tf_op jit(solution)/shard_map/all_to_all | solution.py:366
  79.3 0.8 bitcast_convert_fusion
  80.2 14.7 %all-to-all-done.1.returned_ref.overlap_ref = bf16[16,272,128]{2,1,0:T(8,128)(2,1)S(1)} async-done(((bf16[16,272,128]{2,1,0:T(8,128)(2,1)}), bf16[16,272,128]{2,1,0:T(8,128)(2,1)S(1)}, u32[]{:S(2)}, u32[]{:S(2)}) %all-to-all-start.1) | async-done | bytes 1114144 | tf_op jit(solution)/shard_map/all_to_all | solution.py:366
  94.9 1.2 %copy-done.6 = bf16[4,32,32,128]{3,2,1,0:T(8,128)(2,1)S(1)} copy-done((bf16[4,32,32,128]{3,2,1,0:T(8,128)(2,1)S(1)}, bf16[4,32,32,128]{3,2,1,0:T(8,128)(2,1)}, u32[]{:S(2)}) %copy-start.6) | copy-done | bytes 1048600
  96.1 4.8 %apply.1 = bf16[2,32,32,256]{3,2,1,0:T(8,128)(2,1)} custom-call(s32[2]{0:T(128)S(1)} %pad_add_fusion.first_ref, bf16[16,272,128]{2,1,0:T(8,128)(2,1)S(1)} %all-to-all-done.1.returned_ref.overlap_ref, bf16[16,272,128]{2,1,0:T(8,128)(2,1)S(1)} %all-to-all-done.1.returned_ref.overlap_ref, bf16[2,32,32,256]{3,2,1,0:T(8,128)(2,1)S(1)} %copy-done.1, ...), custom_call_target="tpu_custom_call" | custom-call | tf_op jit(solution)/shard_map/apply/pallas_call | solution.py:372
  (53 shorter events, 0.7 us)
Async XLA Ops:
  0.6 1.2 %copy-start = (bf16[2,32,32,256]{3,2,1,0:T(8,128)(2,1)S(1)}, bf16[2,32,32,256]{3,2,1,0:T(8,128)(2,1)}, u32[]{:S(2)}) copy-start(bf16[2,32,32,256]{3,2,1,0:T(8,128)(2,1)} %orbitals_ref.5) | copy-start | bytes 3145732
  1.9 1.0 %copy-start.2 = (s32[32,32,128]{2,1,0:T(8,128)S(1)}, s32[32,32,128]{2,1,0:T(8,128)}, u32[]{:S(2)}) copy-start(s32[32,32,128]{2,1,0:T(8,128)} %mask_ref.5) | copy-start | bytes 1572868
  6.3 7.1 %copy-start.17 = (f32[8,3]{0,1:T(4,128)S(1)}, f32[8,3]{0,1:T(4,128)}, u32[]{:S(2)}) copy-start(f32[8,3]{0,1:T(4,128)} %param.18) | copy-start | bytes 292
  6.3 22.3 %copy-start.9 = (f32[8,128,128]{2,1,0:T(8,128)S(1)}, f32[8,128,128]{2,1,0:T(8,128)}, u32[]{:S(2)}) copy-start(f32[8,128,128]{2,1,0:T(8,128)} %potential_ref.1) | copy-start | bytes 1572868
  6.3 22.3 %copy-start.10 = (bf16[512,512]{1,0:T(8,128)(2,1)S(1)}, bf16[512,512]{1,0:T(8,128)(2,1)}, u32[]{:S(2)}) copy-start(bf16[512,512]{1,0:T(8,128)(2,1)} %constant.38.clone.z_ref) | copy-start | bytes 1572868
  6.3 22.3 %copy-start.13 = (bf16[256,256]{1,0:T(8,128)(2,1)S(1)}, bf16[256,256]{1,0:T(8,128)(2,1)}, u32[]{:S(2)}) copy-start(bf16[256,256]{1,0:T(8,128)(2,1)} %constant.37.clone.table_ref.y_ref) | copy-start | bytes 393220
  6.3 22.3 %copy-start.16 = (f32[2]{0:T(128)S(1)}, f32[2]{0:T(128)}, u32[]{:S(2)}) copy-start(f32[2]{0:T(128)} %weight_ref.1) | copy-start | bytes 28
  6.3 22.3 %all-to-all-start = ((bf16[16,256,128]{2,1,0:T(8,128)(2,1)}), bf16[16,256,128]{2,1,0:T(8,128)(2,1)S(1)}, u32[]{:S(2)}, u32[]{:S(2)}) async-start(bf16[16,256,128]{2,1,0:T(8,128)(2,1)} %spread.1), calls=%async_computation | async-start | bytes 2097152 | tf_op jit(solution)/shard_map/all_to_all | solution.py:302
  28.7 30.2 %copy-start.5 = (bf16[4,32,32,128]{3,2,1,0:T(8,128)(2,1)S(1)}, bf16[4,32,32,128]{3,2,1,0:T(8,128)(2,1)}, u32[]{:S(2)}) copy-start(bf16[4,32,32,128]{3,2,1,0:T(8,128)(2,1)} %channels_ref.3) | copy-start | bytes 3145732
  31.3 1.0 copy-start.7
  32.2 26.6 %copy-start.1 = (bf16[2,32,32,256]{3,2,1,0:T(8,128)(2,1)S(1)}, bf16[2,32,32,256]{3,2,1,0:T(8,128)(2,1)}, u32[]{:S(2)}) copy-start(bf16[2,32,32,256]{3,2,1,0:T(8,128)(2,1)} %orbitals_ref.5) | copy-start | bytes 3145732
  32.2 26.6 %copy-start.3 = (s32[32,32,128]{2,1,0:T(8,128)S(1)}, s32[32,32,128]{2,1,0:T(8,128)}, u32[]{:S(2)}) copy-start(s32[32,32,128]{2,1,0:T(8,128)} %mask_ref.5) | copy-start | bytes 1572868
  32.2 22.0 %all-to-all-start.2 = ((bf16[16,64,128]{2,1,0:T(8,128)(2,1)}), bf16[16,64,128]{2,1,0:T(8,128)(2,1)S(1)}, u32[]{:S(2)}, u32[]{:S(2)}) async-start(bf16[16,64,128]{2,1,0:T(8,128)(2,1)} %bitcast.6), calls=%async_computation.2 | async-start | bytes 524288 | tf_op jit(solution)/shard_map/all_to_all | solution.py:347
  55.0 14.8 %all-to-all-start.3 = ((bf16[16,64,128]{2,1,0:T(8,128)(2,1)}), bf16[16,64,128]{2,1,0:T(8,128)(2,1)S(1)}, u32[]{:S(2)}, u32[]{:S(2)}) async-start(bf16[16,64,128]{2,1,0:T(8,128)(2,1)} %broadcast_in_dim.15), calls=%async_computation.3 | async-start | bytes 524288 | tf_op jit(solution)/shard_map/all_to_all | solution.py:370
  58.9 1.4 %copy-start.8 = (bf16[8,256,256]{2,1,0:T(8,128)(2,1)S(1)}, bf16[8,256,256]{2,1,0:T(8,128)(2,1)}, u32[]{:S(2)}) copy-start(bf16[8,256,256]{2,1,0:T(8,128)(2,1)} %copy-done.7) | copy-start | bytes 3145732
  58.9 1.4 %copy-start.11 = (bf16[512,512]{1,0:T(8,128)(2,1)S(1)}, bf16[512,512]{1,0:T(8,128)(2,1)}, u32[]{:S(2)}) copy-start(bf16[512,512]{1,0:T(8,128)(2,1)} %constant.39.clone.z_ref) | copy-start | bytes 1572868
  58.9 1.4 %copy-start.15 = (bf16[256,256]{1,0:T(8,128)(2,1)S(1)}, bf16[256,256]{1,0:T(8,128)(2,1)}, u32[]{:S(2)}) copy-start(bf16[256,256]{1,0:T(8,128)(2,1)} %constant.40.clone.y_ref) | copy-start | bytes 393220
  62.6 1.0 %copy-start.4 = (bf16[16,272,128]{2,1,0:T(8,128)(2,1)}, bf16[16,272,128]{2,1,0:T(8,128)(2,1)S(1)}, u32[]{:S(2)}) copy-start(bf16[16,272,128]{2,1,0:T(8,128)(2,1)S(1)} %fold.1) | copy-start | bytes 3342340
  63.6 15.4 %copy-start.19 = (s32[32]{0:T(128)S(1)}, s32[32]{0:T(128)}, u32[]{:S(2)}) copy-start(s32[32]{0:T(128)} %param.20) | copy-start | bytes 388
  63.6 15.4 %copy-start.20 = (s32[32]{0:T(128)S(1)}, s32[32]{0:T(128)}, u32[]{:S(2)}) copy-start(s32[32]{0:T(128)} %param.19) | copy-start | bytes 388
  63.6 15.4 %copy-start.18 = (f32[32]{0:T(128)S(1)}, f32[32]{0:T(128)}, u32[]{:S(2)}) copy-start(f32[32]{0:T(128)} %param.21) | copy-start | bytes 388
  63.6 31.2 %copy-start.14 = (bf16[128,512]{1,0:T(8,128)(2,1)S(1)}, bf16[128,512]{1,0:T(8,128)(2,1)}, u32[]{:S(2)}) copy-start(bf16[128,512]{1,0:T(8,128)(2,1)} %constant.41.clone.table_ref) | copy-start | bytes 393220
  69.8 25.1 %all-to-all-start.1 = ((bf16[16,272,128]{2,1,0:T(8,128)(2,1)}), bf16[16,272,128]{2,1,0:T(8,128)(2,1)S(1)}, u32[]{:S(2)}, u32[]{:S(2)}) async-start(bf16[16,272,128]{2,1,0:T(8,128)(2,1)} %copy-done.4), calls=%async_computation.1 | async-start | bytes 2228224 | tf_op jit(solution)/shard_map/all_to_all | solution.py:366
  94.9 1.2 %copy-start.6 = (bf16[4,32,32,128]{3,2,1,0:T(8,128)(2,1)S(1)}, bf16[4,32,32,128]{3,2,1,0:T(8,128)(2,1)}, u32[]{:S(2)}) copy-start(bf16[4,32,32,128]{3,2,1,0:T(8,128)(2,1)} %channels_ref.3) | copy-start | bytes 3145732
  (1 other events, 0.9 us)

commit v2 on v1

--- a/solution.py
+++ b/solution.py
@@ -11,7 +11,7 @@
 from jax.sharding import PartitionSpec as P
 
 kinetic_scale = 1.0 / 1024.0
-vmem_bytes = 48 * 1024 * 1024
+vmem_bytes = 60 * 1024 * 1024
 bf16 = jnp.bfloat16
 f32 = jnp.float32
 
@@ -366,6 +366,7 @@
     returned = lax.all_to_all(folded, ("gy", "gz"), split_axis=0, concat_axis=0, tiled=True)
 
     density_own = jnp.sum(density_parts.astype(f32), axis=0).astype(bf16)
+    density_own, returned = lax.optimization_barrier((density_own, returned))
     density_copies = jnp.broadcast_to(density_own[None], density_parts.shape)
     density = lax.all_to_all(density_copies, "band", split_axis=0, concat_axis=0, tiled=True)
 

time: 102 us -> 97.4 us (0.955)
  the two profiles are of different devices: /device:TPU:1 before, /device:TPU:32 now
where the time goes in v2:
time: 97.4 us; the launch traced here: 95.8 us
  waiting for transfers between devices  38.9 us (40%)
  starting transfers between devices  28 us (29%)
  Pallas kernels  22.3 us (23%)
  local copies, waits for them, and re-layouts  3.37 us (3%)
  other arithmetic  2.58 us (3%)
    all_to_all x1, waiting for transfers between devices, shards(): lax.all_to_all(folded, ('gy', 'gz'), split_axis=0, concat_axis=0, tiled=T...  16.9 us
    all_to_all x1, waiting for transfers between devices, shards(): lax.all_to_all(spread, ('gy', 'gz'), split_axis=0, concat_axis=0, tiled=T...  15.7 us
    all_to_all x1, starting transfers between devices, shards(): lax.all_to_all(density_part.reshape(parts_band, -1, length), 'band', spli...  10.7 us
    all_to_all x1, starting transfers between devices, shards(): lax.all_to_all(density_copies, 'band', split_axis=0, concat_axis=0, tiled...  7.9 us
    pallas_call x1, Pallas kernels, shards(): pl.pallas_call(apply_kernel, grid=(steps,), in_specs=[smem_spec, blocks_s...  5.77 us
    all_to_all x1, starting transfers between devices, shards(): lax.all_to_all(spread, ('gy', 'gz'), split_axis=0, concat_axis=0, tiled=T...  5.63 us
    pallas_call x1, Pallas kernels, shards(): pl.pallas_call(fold_kernel, grid=(1,), in_specs=[whole(thin, 2 * length,...  4.68 us
    all_to_all x1, waiting for transfers between devices, shards(): lax.all_to_all(density_copies, 'band', split_axis=0, concat_axis=0, tiled...  4.34 us
  transfers between devices with their start and end apart: 4, of which 4 were waited for; matrix products, arithmetic and copies ran while one was open for 3% of the time, Pallas kernels for 15%

profile of v2, /device:TPU:32, one launch (start us, length us, event | category | flops | bytes accessed | tf_op | source)
XLA Modules:
  0.0 95.8 jit_solution(4788651318349428056)
XLA Ops:
  0.6 4.2 %spread.1 = bf16[16,256,128]{2,1,0:T(8,128)(2,1)} custom-call(bf16[2,32,32,256]{3,2,1,0:T(8,128)(2,1)} %orbitals_ref.5, s32[32,32,128]{2,1,0:T(8,128)} %mask_ref.5, bf16[256,256]{1,0:T(8,128)(2,1)} %constant.37.clone.table_ref.y_ref), custom_call_target="tpu_custom_call" | custom-call | tf_op jit(solution)/shard_map/spread/pallas_call | solution.py:293
  4.8 5.6 %all-to-all-start = ((bf16[16,256,128]{2,1,0:T(8,128)(2,1)}), bf16[16,256,128]{2,1,0:T(8,128)(2,1)S(1)}, u32[]{:S(2)}, u32[]{:S(2)}) async-start(bf16[16,256,128]{2,1,0:T(8,128)(2,1)} %spread.1), calls=%async_computation | async-start | bytes 2097152 | tf_op jit(solution)/shard_map/all_to_all | solution.py:302
  10.5 0.1 fusion.3
  10.6 0.1 add_convert_fusion
  10.8 0.1 sub.20
  10.9 0.1 add.49
  11.0 15.7 %all-to-all-done.arrived_ref = bf16[16,256,128]{2,1,0:T(8,128)(2,1)S(1)} async-done(((bf16[16,256,128]{2,1,0:T(8,128)(2,1)}), bf16[16,256,128]{2,1,0:T(8,128)(2,1)S(1)}, u32[]{:S(2)}, u32[]{:S(2)}) %all-to-all-start) | async-done | bytes 1048608 | tf_op jit(solution)/shard_map/all_to_all | solution.py:302
  26.8 1.0 %copy-done.1 = bf16[16,256,128]{2,1,0:T(8,128)(2,1)} copy-done((bf16[16,256,128]{2,1,0:T(8,128)(2,1)}, bf16[16,256,128]{2,1,0:T(8,128)(2,1)S(1)}, u32[]{:S(2)}) %copy-start.1) | copy-done | bytes 1048600
  27.7 3.9 %field.1 = (bf16[1024,128]{1,0:T(8,128)(2,1)}, bf16[8,256,256]{2,1,0:T(8,128)(2,1)}) custom-call(bf16[16,256,128]{2,1,0:T(8,128)(2,1)} %copy-done.1, f32[8,128,128]{2,1,0:T(8,128)} %potential_ref.1, f32[2]{0:T(128)} %weight_ref.1, bf16[512,512]{1,0:T(8,128)(2,1)} %constant.38.clone.z_ref, bf16[256,256]{1,0:T(8,128)(2,1)} %constant.37.clone.table_ref.y_ref), custom_call_target="tpu_custom_call" | custom-call | tf_op jit(solution)/shard_map/field/pallas_call | solution.py:328
  31.7 10.7 %all-to-all-start.1 = ((bf16[16,64,128]{2,1,0:T(8,128)(2,1)}), bf16[16,64,128]{2,1,0:T(8,128)(2,1)S(1)}, u32[]{:S(2)}, u32[]{:S(2)}) async-start(bf16[16,64,128]{2,1,0:T(8,128)(2,1)} %bitcast.15), calls=%async_computation.1 | async-start | bytes 524288 | tf_op jit(solution)/shard_map/all_to_all | solution.py:347
  42.5 0.6 pad_maximum_fusion.wave_ref
  43.1 0.6 copy-done.2
  43.7 3.7 %overlap.1.overlap_ref = bf16[16,128]{1,0:T(8,128)(2,1)} custom-call(bf16[2,32,32,256]{3,2,1,0:T(8,128)(2,1)} %orbitals_ref.5, s32[32,32,128]{2,1,0:T(8,128)} %mask_ref.5, bf16[4,32,32,128]{3,2,1,0:T(8,128)(2,1)} %channels_ref.3, bf16[16,1024]{1,0:T(8,128)(2,1)} %copy-done.2, f32[16,128]{1,0:T(8,128)} %pad_maximum_fusion.wave_ref), custom_call_target="tpu_custom_call" | custom-call | tf_op jit(solution)/shard_map/overlap/pallas_call | solution.py:317
  47.5 4.7 %fold.1 = bf16[16,272,128]{2,1,0:T(8,128)(2,1)} custom-call(bf16[8,256,256]{2,1,0:T(8,128)(2,1)} %get-tuple-element.7.scaled_ref, bf16[16,128]{1,0:T(8,128)(2,1)} %overlap.1.overlap_ref, bf16[512,512]{1,0:T(8,128)(2,1)} %constant.39.clone.z_ref, bf16[256,256]{1,0:T(8,128)(2,1)} %constant.40.clone.y_ref), custom_call_target="tpu_custom_call" | custom-call | tf_op jit(solution)/shard_map/fold/pallas_call | solution.py:351
  52.1 1.9 %all-to-all-done.1 = bf16[16,64,128]{2,1,0:T(8,128)(2,1)S(1)} async-done(((bf16[16,64,128]{2,1,0:T(8,128)(2,1)}), bf16[16,64,128]{2,1,0:T(8,128)(2,1)S(1)}, u32[]{:S(2)}, u32[]{:S(2)}) %all-to-all-start.1) | async-done | bytes 262176 | tf_op jit(solution)/shard_map/all_to_all | solution.py:347
  54.0 3.7 %all-to-all-start.2 = ((bf16[16,272,128]{2,1,0:T(8,128)(2,1)}), bf16[16,272,128]{2,1,0:T(8,128)(2,1)S(1)}, u32[]{:S(2)}, u32[]{:S(2)}) async-start(bf16[16,272,128]{2,1,0:T(8,128)(2,1)} %fold.1), calls=%async_computation.2 | async-start | bytes 2228224 | tf_op jit(solution)/shard_map/all_to_all | solution.py:366
  57.8 16.9 %all-to-all-done.2.returned_ref.overlap_ref = bf16[16,272,128]{2,1,0:T(8,128)(2,1)S(1)} async-done(((bf16[16,272,128]{2,1,0:T(8,128)(2,1)}), bf16[16,272,128]{2,1,0:T(8,128)(2,1)S(1)}, u32[]{:S(2)}, u32[]{:S(2)}) %all-to-all-start.2) | async-done | bytes 1114144 | tf_op jit(solution)/shard_map/all_to_all | solution.py:366
  74.7 0.8 broadcast_in_dim.15
  75.5 7.9 %all-to-all-start.3 = ((bf16[16,64,128]{2,1,0:T(8,128)(2,1)}), bf16[16,64,128]{2,1,0:T(8,128)(2,1)S(1)}, u32[]{:S(2)}, u32[]{:S(2)}) async-start(bf16[16,64,128]{2,1,0:T(8,128)(2,1)} %broadcast_in_dim.15), calls=%async_computation.3 | async-start | bytes 524288 | tf_op jit(solution)/shard_map/all_to_all | solution.py:371
  83.6 0.6 pad.4.strength_ref
  84.3 0.6 pad_add_fusion.first_ref
  84.9 5.8 %apply.1 = bf16[2,32,32,256]{3,2,1,0:T(8,128)(2,1)} custom-call(s32[2]{0:T(128)} %pad_add_fusion.first_ref, bf16[16,272,128]{2,1,0:T(8,128)(2,1)} %copy-done, bf16[16,272,128]{2,1,0:T(8,128)(2,1)} %copy-done, bf16[2,32,32,256]{3,2,1,0:T(8,128)(2,1)} %orbitals_ref.5, s32[32,32,128]{2,1,0:T(8,128)} %mask_ref.5, bf16[4,32,32,128]{3,2,1,0:T(8,128)(2,1)} %channels_ref.3, ...), custom_call_target="tpu_custom_call" | custom-call | tf_op jit(solution)/shard_map/apply/pallas_call | solution.py:373
  90.6 4.3 %all-to-all-done.3 = bf16[16,64,128]{2,1,0:T(8,128)(2,1)S(1)} async-done(((bf16[16,64,128]{2,1,0:T(8,128)(2,1)}), bf16[16,64,128]{2,1,0:T(8,128)(2,1)S(1)}, u32[]{:S(2)}, u32[]{:S(2)}) %all-to-all-start.3) | async-done | bytes 262176 | tf_op jit(solution)/shard_map/all_to_all | solution.py:371
  95.0 0.8 bitcast_convert_fusion
  (25 shorter events, 0.4 us)
Async XLA Ops:
  4.8 5.7 %copy-start.3 = (f32[8,3]{0,1:T(4,128)S(1)}, f32[8,3]{0,1:T(4,128)}, u32[]{:S(2)}) copy-start(f32[8,3]{0,1:T(4,128)} %param.18) | copy-start | bytes 292
  4.8 22.0 %all-to-all-start = ((bf16[16,256,128]{2,1,0:T(8,128)(2,1)}), bf16[16,256,128]{2,1,0:T(8,128)(2,1)S(1)}, u32[]{:S(2)}, u32[]{:S(2)}) async-start(bf16[16,256,128]{2,1,0:T(8,128)(2,1)} %spread.1), calls=%async_computation | async-start | bytes 2097152 | tf_op jit(solution)/shard_map/all_to_all | solution.py:302
  26.8 1.0 %copy-start.1 = (bf16[16,256,128]{2,1,0:T(8,128)(2,1)}, bf16[16,256,128]{2,1,0:T(8,128)(2,1)S(1)}, u32[]{:S(2)}) copy-start(bf16[16,256,128]{2,1,0:T(8,128)(2,1)S(1)} %all-to-all-done.arrived_ref) | copy-start | bytes 3145732
  31.7 22.4 %all-to-all-start.1 = ((bf16[16,64,128]{2,1,0:T(8,128)(2,1)}), bf16[16,64,128]{2,1,0:T(8,128)(2,1)S(1)}, u32[]{:S(2)}, u32[]{:S(2)}) async-start(bf16[16,64,128]{2,1,0:T(8,128)(2,1)} %bitcast.15), calls=%async_computation.1 | async-start | bytes 524288 | tf_op jit(solution)/shard_map/all_to_all | solution.py:347
  43.1 0.6 copy-start.2
  52.1 31.3 %copy-start.5 = (s32[32]{0:T(128)S(1)}, s32[32]{0:T(128)}, u32[]{:S(2)}) copy-start(s32[32]{0:T(128)} %param.20) | copy-start | bytes 388
  52.1 31.3 %copy-start.6 = (s32[32]{0:T(128)S(1)}, s32[32]{0:T(128)}, u32[]{:S(2)}) copy-start(s32[32]{0:T(128)} %param.19) | copy-start | bytes 388
  52.1 31.3 %copy-start.4 = (f32[32]{0:T(128)S(1)}, f32[32]{0:T(128)}, u32[]{:S(2)}) copy-start(f32[32]{0:T(128)} %param.21) | copy-start | bytes 388
  54.0 20.7 %all-to-all-start.2 = ((bf16[16,272,128]{2,1,0:T(8,128)(2,1)}), bf16[16,272,128]{2,1,0:T(8,128)(2,1)S(1)}, u32[]{:S(2)}, u32[]{:S(2)}) async-start(bf16[16,272,128]{2,1,0:T(8,128)(2,1)} %fold.1), calls=%async_computation.2 | async-start | bytes 2228224 | tf_op jit(solution)/shard_map/all_to_all | solution.py:366
  74.7 10.2 %copy-start = (bf16[16,272,128]{2,1,0:T(8,128)(2,1)}, bf16[16,272,128]{2,1,0:T(8,128)(2,1)S(1)}, u32[]{:S(2)}) copy-start(bf16[16,272,128]{2,1,0:T(8,128)(2,1)S(1)} %all-to-all-done.2.returned_ref.overlap_ref) | copy-start | bytes 3342340
  75.5 19.4 %all-to-all-start.3 = ((bf16[16,64,128]{2,1,0:T(8,128)(2,1)}), bf16[16,64,128]{2,1,0:T(8,128)(2,1)S(1)}, u32[]{:S(2)}, u32[]{:S(2)}) async-start(bf16[16,64,128]{2,1,0:T(8,128)(2,1)} %broadcast_in_dim.15), calls=%async_computation.3 | async-start | bytes 524288 | tf_op jit(solution)/shard_map/all_to_all | solution.py:371

commit v3 on v1

v3 whole, which is shorter than its diff:
```python
import functools
import math

import jax
import jax.numpy as jnp
import ml_dtypes
import numpy as np
from jax import lax
from jax.experimental import pallas as pl
from jax.experimental.pallas import tpu as pltpu
from jax.sharding import PartitionSpec as P

kinetic_scale = 1.0 / 1024.0
vmem_bytes = 63 * 1024 * 1024
bf16 = jnp.bfloat16
f32 = jnp.float32


def dft_table(length, sign_value):
    grid_index = np.arange(length)
    product = grid_index[:, None] * grid_index[None, :] % length
    phase_angle = np.float32(2.0 * math.pi / length) * product.astype(np.float32)
    cosine_part = np.cos(phase_angle) / np.float32(math.sqrt(length))
    sine_part = sign_value * np.sin(phase_angle) / np.float32(math.sqrt(length))
    upper_rows = np.stack([cosine_part, -sine_part], axis=1)
    lower_rows = np.stack([sine_part, cosine_part], axis=1)
    return np.stack([upper_rows, lower_rows], axis=0).astype(np.float32)


def rounded(table, rows):
    return jnp.asarray(np.ascontiguousarray(table).reshape(rows, -1).astype(ml_dtypes.bfloat16))


def frequencies(first_index, span, length):
    grid_index = first_index + jnp.arange(span, dtype=jnp.int32)
    return jnp.where(grid_index >= length // 2, grid_index - length, grid_index).astype(f32)


def axis_phase(coordinate, freq):
    phase_angle = 2.0 * math.pi * (coordinate[:, None] * freq[None, :])
    return (jnp.cos(phase_angle), jnp.sin(phase_angle))


def dot(left, right):
    return jnp.dot(left, right, preferred_element_type=f32)


def dot_nt(left, right):
    return lax.dot_general(left, right, (((1,), (1,)), ((), ())), preferred_element_type=f32)


def dot_tn(left, right):
    return lax.dot_general(left, right, (((0,), (0,)), ((), ())), preferred_element_type=f32)


def root_weights(weight_ref, shape, axis, span):
    index = lax.broadcasted_iota(jnp.int32, shape, axis)
    return jnp.sqrt(jnp.where(index // span % 2 == 0, weight_ref[0], weight_ref[1]))


def spread_kernel(orbitals_ref, mask_ref, weight_ref, table_ref, out_ref, work_ref):
    rows_y, rows_z, length = mask_ref.shape
    mask = jnp.where(mask_ref[...] != 0, 1.0, 0.0).astype(bf16)
    mask = jnp.concatenate([mask, mask], axis=2)
    lane = lax.broadcasted_iota(jnp.int32, (length, 128), 1)
    roots = root_weights(weight_ref, (1, 128), 1, rows_z)
    for pair in range(0, rows_y, 2):
        rows = []
        for y in (pair, pair + 1):
            both = jnp.concatenate([orbitals_ref[0, y] * mask[y], orbitals_ref[1, y] * mask[y]], axis=0)
            rows += [both, both]
        spread = dot_nt(table_ref[...], jnp.concatenate(rows, axis=0))
        for half in range(2):
            cols = slice(half * 128, half * 128 + 128)
            tile = jnp.where(lane < 64, spread[:length, cols], spread[length:, cols])
            work_ref[pl.ds(pair + half, length, stride=rows_y), :] = tile * roots
    out_ref[...] = work_ref[...].reshape(out_ref.shape).astype(bf16)


def overlap_kernel(orbitals_ref, mask_ref, channels_ref, phase_ref, wave_ref, out_ref, sums_ref):
    step = pl.program_id(0)
    rows = mask_ref.shape[0] * mask_ref.shape[1]
    length = mask_ref.shape[2]
    atoms = wave_ref.shape[0] // 2
    kinds = channels_ref.shape[0]
    mask = jnp.where(mask_ref[...] != 0, 1.0, 0.0).astype(bf16)
    orbs = [orbitals_ref[n].reshape(rows, 2 * length) for n in range(2)]
    columns = []
    for c in range(kinds):
        radial = (channels_ref[c] * mask).reshape(rows, length)
        radial = jnp.concatenate([radial, radial], axis=1)
        columns += [radial * orbs[0], radial * orbs[1]]
    part = dot(phase_ref[...], jnp.concatenate(columns, axis=1))

    @pl.when(step == 0)
    def first():
        sums_ref[...] = part

    @pl.when(step > 0)
    def later():
        sums_ref[...] += part

    @pl.when(step == pl.num_programs(0) - 1)
    def last():
        cos_x, sin_x = wave_ref[:atoms], wave_ref[atoms:]
        lane = lax.broadcasted_iota(jnp.int32, (atoms, 128), 1)
        total = jnp.zeros((atoms, 128), f32)
        for pair in range(kinds * 2):
            base = pair * 2 * length
            real_cols = slice(base, base + length)
            imag_cols = slice(base + length, base + 2 * length)
            real = sums_ref[:atoms, real_cols] - sums_ref[atoms:, imag_cols]
            imag = sums_ref[atoms:, real_cols] + sums_ref[:atoms, imag_cols]
            real_over = jnp.sum(real * cos_x - imag * sin_x, axis=1, keepdims=True)
            imag_over = jnp.sum(real * sin_x + imag * cos_x, axis=1, keepdims=True)
            total = jnp.where(lane == 2 * pair, real_over, total)
            total = jnp.where(lane == 2 * pair + 1, imag_over, total)
        out_ref[...] = total


def field_kernel(
    arrived_ref,
    potential_ref,
    inv_z_ref,
    inv_y_ref,
    fwd_z_ref,
    fwd_y_ref,
    density_ref,
    out_ref,
    sums_ref,
):
    step = pl.program_id(0)
    planes, length = potential_ref.shape[:2]
    parts = arrived_ref.shape[0] // 4
    rows = arrived_ref.shape[1] // planes
    columns = jnp.concatenate(
        [jnp.concatenate([arrived_ref[sy * 4 + sz] for sz in range(4)], axis=1) for sy in range(parts)],
        axis=0,
    )
    halfway = dot(columns, inv_z_ref[...]).astype(bf16)
    stacked = []
    for x in range(planes):
        first = [(sy * planes + x) * rows for sy in range(parts)]
        plane = jnp.concatenate([halfway[start : start + rows] for start in first], axis=0)
        real = jnp.concatenate([plane[:, 0:128], plane[:, 256:384]], axis=1)
        imag = jnp.concatenate([plane[:, 128:256], plane[:, 384:512]], axis=1)
        stacked.append(jnp.concatenate([real, imag], axis=0))
    fields = [dot(inv_y_ref[...], block) for block in stacked]
    scaled = []
    for x, field in enumerate(fields):
        real, imag = field[:length], field[length:]
        square = real * real + imag * imag
        density = square[:, :length] + square[:, length:]
        here = slice(x * length, (x + 1) * length)
        sums_ref[here, :] = jnp.where(step == 0, density, sums_ref[here, :] + density)
        potential = jnp.concatenate([potential_ref[x], potential_ref[x]], axis=1)
        potential = jnp.concatenate([potential, potential], axis=0)
        scaled.append((potential * field).astype(bf16))
    folded = [dot(fwd_y_ref[...], block).astype(bf16) for block in scaled]
    back = []
    for block in folded:
        real, imag = block[:length], block[length:]
        back.append(
            jnp.concatenate([real[:, :length], imag[:, :length], real[:, length:], imag[:, length:]], axis=1)
        )
    back = dot(jnp.concatenate(back, axis=0), fwd_z_ref[...]).astype(bf16)
    for x in range(planes):
        for sy in range(parts):
            start = x * length + sy * rows
            for sz in range(4):
                out_ref[sy * 4 + sz, x * rows : (x + 1) * rows, :] = back[
                    start : start + rows, sz * 128 : sz * 128 + 128
                ]

    @pl.when(step == pl.num_programs(0) - 1)
    def last():
        density_ref[...] = sums_ref[...].astype(bf16)


def base_kernel(
    first_ref,
    overlap_ref,
    orbitals_ref,
    mask_ref,
    channels_ref,
    phase_ref,
    wave_ref,
    strength_ref,
    out_ref,
    factor_ref,
):
    step = pl.program_id(0)
    rows_y, rows_z, length = mask_ref.shape
    atoms = wave_ref.shape[0] // 2
    kinds = channels_ref.shape[0]

    @pl.when(step == 0)
    def factors():
        cos_x, sin_x = wave_ref[:atoms], wave_ref[atoms:]
        coef = overlap_ref[...] * strength_ref[...]
        for pair in range(kinds * 2):
            coef_real = coef[:, 2 * pair : 2 * pair + 1]
            coef_imag = coef[:, 2 * pair + 1 : 2 * pair + 2]
            real = cos_x * coef_real + sin_x * coef_imag
            imag = cos_x * coef_imag - sin_x * coef_real
            base = pair * 2 * length
            factor_ref[:, base : base + length] = jnp.concatenate([real, imag], axis=0).astype(bf16)
            factor_ref[:, base + length : base + 2 * length] = jnp.concatenate(
                [imag, -real], axis=0
            ).astype(bf16)

    def squared(start, axis):
        index = start + lax.broadcasted_iota(jnp.int32, mask_ref.shape, axis)
        wave = jnp.where(index >= length // 2, index - length, index)
        return wave * wave

    energy = squared(first_ref[0] + step * rows_y, 0) + squared(first_ref[1], 1) + squared(0, 2)
    energy = kinetic_scale * 0.5 * energy.astype(f32)
    for y in range(rows_y):
        extra = dot_tn(phase_ref[:, y * rows_z : (y + 1) * rows_z], factor_ref[...])
        radials = [channels_ref[c, y].astype(f32) for c in range(kinds)]
        for n in range(2):
            for part in range(2):
                cols = slice(part * length, part * length + length)
                total = energy[y] * orbitals_ref[n, y, :, cols].astype(f32)
                for c in range(kinds):
                    base = ((c * 2 + n) * 2 + part) * length
                    total = total + radials[c] * extra[:, base : base + length]
                out_ref[n, y, :, cols] = total


def apply_kernel(returned_ref, base_ref, mask_ref, weight_ref, table_ref, out_ref, work_ref):
    rows_y, rows_z, length = mask_ref.shape
    scale = 1.0 / root_weights(weight_ref, (2 * rows_z, 1), 0, rows_z)
    work_ref[...] = returned_ref[...].astype(f32).reshape(work_ref.shape)
    inside = mask_ref[...] != 0
    for pair in range(0, rows_y, 2):
        planes = jnp.concatenate(
            [work_ref[pl.ds(y, length, stride=rows_y), :].astype(bf16) for y in (pair, pair + 1)], axis=1
        )
        local = dot_tn(planes, table_ref[...])
        for half in range(2):
            y = pair + half
            both = local[half * 128 : half * 128 + 64, : 2 * length]
            both = scale * (both + local[half * 128 + 64 : half * 128 + 128, 2 * length :])
            keep = jnp.concatenate([inside[y], inside[y]], axis=1)
            for n in range(2):
                total = both[n * rows_z : (n + 1) * rows_z] + base_ref[n, y]
                out_ref[n, y] = jnp.where(keep, total, 0.0).astype(bf16)


def partners(axis, distance):
    return [(i, i ^ distance) for i in range(lax.axis_size(axis))]


def sum_over(part, axis, distances):
    got = [lax.ppermute(part, axis, partners(axis, d)).astype(f32) for d in distances]
    return (part.astype(f32) + got[0]) + (got[1] + got[2])


def shards(
    orbitals,
    potential,
    cutoff_mask,
    channels,
    positions,
    proj_atom,
    proj_chan,
    coupling,
    occupations,
):
    rows_y, rows_z, length = cutoff_mask.shape
    parts_y = lax.axis_size("gy")
    parts_z = lax.axis_size("gz")
    parts_band = lax.axis_size("band")
    places = parts_y * parts_z
    bands = 2
    outer = parts_band // bands
    thin = length // places
    planes = thin // bands
    atoms = positions.shape[0]
    kinds = channels.shape[0]
    groups = [
        [(first * bands + b) * places + place for b in range(bands) for place in range(places)]
        for first in range(outer)
    ]
    inverse = dft_table(length, 1.0)
    forward = dft_table(length, -1.0)
    pick = np.eye(2, dtype=np.float32)
    split_inverse = inverse.reshape(2, length, 2, parts_z, rows_z)
    split_forward = forward.reshape(2, parts_z, rows_z, 2, length)
    order = np.arange(length).reshape(places, bands, planes).transpose(1, 0, 2).reshape(-1)
    inv_x = rounded(inverse[:, order], 2 * length)
    inv_y = rounded(inverse, 2 * length)
    inv_z = rounded(np.einsum("fzcsl,nm->scnlmfz", split_inverse, pick), 4 * length)
    fwd_z = rounded(np.einsum("cslfz,nm->nfzscml", split_forward, pick), 4 * length)
    fwd_y = rounded(forward, 2 * length)
    fwd_x = rounded(np.einsum("rkcx->xcrk", forward[..., order]), length)
    first_y = lax.axis_index("gy") * rows_y
    first_z = lax.axis_index("gz") * rows_z
    band = lax.axis_index("band") % bands

    params = pltpu.CompilerParams(vmem_limit_bytes=vmem_bytes)

    def cost(microseconds):
        return pl.CostEstimate(
            flops=int(microseconds * 1.0e9), bytes_accessed=int(microseconds * 1.0e6), transcendentals=0
        )

    steps = 2
    span = rows_y // steps
    whole = lambda *shape: pl.BlockSpec(shape, lambda i: (0,) * len(shape))
    orbitals_spec = pl.BlockSpec((2, span, rows_z, 2 * length), lambda i: (0, i, 0, 0))
    mask_spec = pl.BlockSpec((span, rows_z, length), lambda i: (i, 0, 0))
    channels_spec = pl.BlockSpec((kinds, span, rows_z, length), lambda i: (0, i, 0, 0))
    phase_spec = pl.BlockSpec((2 * atoms, span * rows_z), lambda i: (0, i))
    chunks_spec = pl.BlockSpec((bands * places, planes, span, 128), lambda i: (0, 0, i, 0))
    chunk_shape = (bands * places, planes, rows_y, 128)
    smem_spec = pl.BlockSpec(memory_space=pltpu.SMEM)

    def exchange(chunks):
        return lax.all_to_all(
            chunks, ("band", "gy", "gz"), split_axis=0, concat_axis=0, tiled=True, axis_index_groups=groups
        )

    spread = pl.pallas_call(
        spread_kernel,
        grid=(steps,),
        in_specs=[orbitals_spec, mask_spec, smem_spec, whole(2 * length, 2 * length)],
        out_specs=chunks_spec,
        out_shape=jax.ShapeDtypeStruct(chunk_shape, bf16),
        scratch_shapes=[pltpu.VMEM((length * span, 128), f32)],
        compiler_params=params,
        cost_estimate=cost(4),
        name="spread",
    )(orbitals, cutoff_mask, occupations, inv_x)
    potential_part = lax.dynamic_slice_in_dim(potential, band * planes, planes, 0)

    spread, positions = lax.optimization_barrier((spread, positions))
    arrived = exchange(spread)

    cos_y, sin_y = axis_phase(positions[:, 1], frequencies(first_y, rows_y, length))
    cos_z, sin_z = axis_phase(positions[:, 2], frequencies(first_z, rows_z, length))
    cos_x, sin_x = axis_phase(positions[:, 0], frequencies(0, length, length))
    cos_yz = cos_y[:, :, None] * cos_z[:, None, :] - sin_y[:, :, None] * sin_z[:, None, :]
    sin_yz = sin_y[:, :, None] * cos_z[:, None, :] + cos_y[:, :, None] * sin_z[:, None, :]
    phase = jnp.concatenate([cos_yz, sin_yz], axis=0).astype(bf16).reshape(2 * atoms, rows_y * rows_z)
    wave = jnp.concatenate([cos_x, sin_x], axis=0)
    chosen = (proj_atom[None, :] == jnp.arange(atoms, dtype=jnp.int32)[:, None])[:, None, :] & (
        proj_chan[None, :] == jnp.arange(kinds, dtype=jnp.int32)[:, None]
    )[None, :, :]
    strength = jnp.sum(jnp.where(chosen, coupling[None, None, :], 0.0), axis=2)
    strength = jnp.pad(jnp.repeat(strength, 4, axis=1), ((0, 0), (0, 128 - 4 * kinds)))

    overlap = pl.pallas_call(
        overlap_kernel,
        grid=(steps,),
        in_specs=[orbitals_spec, mask_spec, channels_spec, phase_spec, whole(2 * atoms, length)],
        out_specs=whole(atoms, 128),
        out_shape=jax.ShapeDtypeStruct((atoms, 128), f32),
        scratch_shapes=[pltpu.VMEM((2 * atoms, kinds * 4 * length), f32)],
        compiler_params=params,
        cost_estimate=cost(3),
        name="overlap",
    )(orbitals, cutoff_mask, channels, phase, wave)
    overlap = sum_over(overlap, "gz", (1, 2, 3))
    arrived, overlap = lax.optimization_barrier((arrived, overlap))
    overlap = sum_over(overlap, "gy", (1, 2, 3))

    rows = planes * rows_y
    band_spec = pl.BlockSpec((places, rows, 128), lambda i: (i, 0, 0))
    density, folded = pl.pallas_call(
        field_kernel,
        grid=(bands,),
        in_specs=[
            band_spec,
            whole(planes, length, length),
            whole(4 * length, 4 * length),
            whole(2 * length, 2 * length),
            whole(4 * length, 4 * length),
            whole(2 * length, 2 * length),
        ],
        out_specs=[whole(planes * length, length), band_spec],
        out_shape=[
            jax.ShapeDtypeStruct((planes * length, length), bf16),
            jax.ShapeDtypeStruct((bands * places, rows, 128), bf16),
        ],
        scratch_shapes=[pltpu.VMEM((planes * length, length), f32)],
        compiler_params=params,
        cost_estimate=cost(6),
        name="field",
    )(arrived.reshape(bands * places, rows, 128), potential_part, inv_z, inv_y, fwd_z, fwd_y)
    returned = exchange(folded.reshape(chunk_shape))

    base = pl.pallas_call(
        base_kernel,
        grid=(steps,),
        in_specs=[
            smem_spec,
            whole(atoms, 128),
            orbitals_spec,
            mask_spec,
            channels_spec,
            phase_spec,
            whole(2 * atoms, length),
            whole(atoms, 128),
        ],
        out_specs=orbitals_spec,
        out_shape=jax.ShapeDtypeStruct(orbitals.shape, f32),
        scratch_shapes=[pltpu.VMEM((2 * atoms, kinds * 4 * length), bf16)],
        compiler_params=params,
        cost_estimate=cost(4),
        name="base",
    )(
        jnp.stack([first_y, first_z]).astype(jnp.int32),
        overlap,
        orbitals,
        cutoff_mask,
        channels,
        phase,
        wave,
        strength,
    )
    half = planes // 2 * length
    upper = lax.axis_index("band") // bands % 2
    mine = lax.dynamic_slice_in_dim(density, upper * half, half, 0)
    theirs = lax.dynamic_slice_in_dim(density, (1 - upper) * half, half, 0)
    near = lax.ppermute(theirs, "band", partners("band", bands))
    mine = (mine.astype(f32) + near.astype(f32)).astype(bf16)
    far = [lax.ppermute(mine, "band", partners("band", d * bands)) for d in (2, 4, 6) if d < outer]
    far, base = lax.optimization_barrier((far, base))
    if far:
        far = [part.astype(f32) for part in far]
        mine = ((mine.astype(f32) + far[0]) + (far[1] + far[2])).astype(bf16)
    copies = [lax.ppermute(mine, "band", partners("band", d)) for d in (1, 2, 3)]
    applied = pl.pallas_call(
        apply_kernel,
        grid=(steps,),
        in_specs=[chunks_spec, orbitals_spec, mask_spec, smem_spec, whole(length, 4 * length)],
        out_specs=orbitals_spec,
        out_shape=jax.ShapeDtypeStruct(orbitals.shape, bf16),
        scratch_shapes=[pltpu.VMEM((length * span, 128), f32)],
        compiler_params=params,
        cost_estimate=cost(4),
        name="apply",
    )(returned, base, cutoff_mask, occupations, fwd_x)
    copies, applied = lax.optimization_barrier((copies, applied))
    odd, high = band != 0, upper != 0
    pieces = [mine] + copies
    pieces = [jnp.where(odd, pieces[j ^ 1], pieces[j]) for j in range(4)]
    pieces = [jnp.where(high, pieces[j ^ 2], pieces[j]) for j in range(4)]
    density = jnp.concatenate([pieces[0], pieces[2], pieces[1], pieces[3]], axis=0)
    return (applied, density.astype(f32).reshape(potential.shape))


def solution(mesh):
    placed = (
        P("band", "gy", "gz", None),
        P(("gy", "gz"), None, None),
        P("gy", "gz", None),
        P(None, "gy", "gz", None),
        P(),
        P(),
        P(),
        P(),
        P("band"),
    )
    return jax.shard_map(
        shards,
        mesh=mesh,
        in_specs=placed,
        out_specs=(P("band", "gy", "gz", None), P(("gy", "gz"), None, None)),
        check_vma=False,
    )
```

time: 102 us -> 80.5 us (0.79)
  the two profiles are of different devices: /device:TPU:1 before, /device:TPU:32 now
where the time goes in v3:
time: 80.5 us; the launch traced here: 79.3 us
  starting transfers between devices  31.7 us (39%)
  waiting for transfers between devices  22.2 us (28%)
  Pallas kernels  18.9 us (23%)
  other arithmetic  3.3 us (4%)
  local copies, waits for them, and re-layouts  2.31 us (3%)
  between operations  0.86 us (1%)
    all_to_all x2, waiting for transfers between devices, exchange(): lax.all_to_all(chunks, ('band', 'gy', 'gz'), split_axis=0, concat_axis=0,...  14.8 us
    all_to_all x2, starting transfers between devices, exchange(): lax.all_to_all(chunks, ('band', 'gy', 'gz'), split_axis=0, concat_axis=0,...  12.2 us
    ppermute x3, starting transfers between devices, shards(): lax.ppermute(mine, 'band', partners('band', d * bands))  7.95 us
    ppermute x6, starting transfers between devices, sum_over(): lax.ppermute(part, axis, partners(axis, d)).astype(f32)  6.04 us
    ppermute x3, starting transfers between devices, shards(): lax.ppermute(mine, 'band', partners('band', d))  5.23 us
    pallas_call x1, Pallas kernels, shards(): pl.pallas_call(field_kernel, grid=(bands,), in_specs=[band_spec, whole(pl...  4.74 us
    pallas_call x1, Pallas kernels, shards(): pl.pallas_call(apply_kernel, grid=(steps,), in_specs=[chunks_spec, orbita...  3.99 us
    pallas_call x1, Pallas kernels, shards(): pl.pallas_call(base_kernel, grid=(steps,), in_specs=[smem_spec, whole(ato...  3.98 us
  transfers between devices with their start and end apart: 15, of which 4 were waited for; matrix products, arithmetic and copies ran while one was open for 4% of the time, Pallas kernels for 16%

profile of v3, /device:TPU:32, one launch (start us, length us, event | category | flops | bytes accessed | tf_op | source)
XLA Modules:
  0.0 79.3 jit_solution(8726306129366827197)
XLA Ops:
  0.7 3.4 %spread.1 = bf16[32,4,32,128]{3,2,1,0:T(8,128)(2,1)} custom-call(bf16[2,32,32,256]{3,2,1,0:T(8,128)(2,1)} %orbitals_ref.5, s32[32,32,128]{2,1,0:T(8,128)} %mask_ref.7, f32[2]{0:T(128)} %weight_ref.3, bf16[256,256]{1,0:T(8,128)(2,1)} %constant.79.clone.table_ref), custom_call_target="tpu_custom_call" | custom-call | flops 4000000000 | bytes 4000000 | tf_op jit(solution)/shard_map/spread/pallas_call | solution.py:326
  4.8 0.6 pad_maximum_fusion.1.wave_ref
  6.0 2.8 %overlap.1 = f32[8,128]{1,0:T(8,128)} custom-call(bf16[2,32,32,256]{3,2,1,0:T(8,128)(2,1)} %orbitals_ref.5, s32[32,32,128]{2,1,0:T(8,128)} %mask_ref.7, bf16[4,32,32,128]{3,2,1,0:T(8,128)(2,1)} %channels_ref.3, bf16[16,1024]{1,0:T(8,128)(2,1)} %copy-done.2, f32[16,128]{1,0:T(8,128)} %pad_maximum_fusion.1.wave_ref), custom_call_target="tpu_custom_call" | custom-call | flops 3000000000 | bytes 3000000 | tf_op jit(solution)/shard_map/overlap/pallas_call | solution.py:355
  8.8 3.1 %collective-permute-start.2 = (f32[8,128]{1,0:T(8,128)}, f32[8,128]{1,0:T(8,128)S(1)}, u32[]{:S(2)}, u32[]{:S(2)}) collective-permute-start(f32[8,128]{1,0:T(8,128)} %overlap.1), channel_id=1, source_target_pairs={{0,3},{1,2},{2,1},{3,0},{4,7},{5,6},{6,5},{7,4},{8,11},{9,10},{10,... | collective-permute-start | bytes 12296 | tf_op jit(solution)/shard_map/ppermute | solution.py:257
  11.9 0.6 collective-permute-start.1
  13.0 7.4 %all-to-all-start = ((bf16[32,4,32,128]{3,2,1,0:T(8,128)(2,1)}), bf16[32,4,32,128]{3,2,1,0:T(8,128)(2,1)}, u32[]{:S(2)}, u32[]{:S(2)}) async-start(bf16[32,4,32,128]{3,2,1,0:T(8,128)(2,1)} %spread.1), calls=%async_computation | async-start | bytes 2097152 | tf_op jit(solution)/shard_map/all_to_all | solution.py:322
  20.6 0.7 constant_dynamic-slice_fusion.1.potential_ref
  21.3 0.7 pad_add_fusion.first_ref
  22.7 14.8 %all-to-all-done = bf16[32,4,32,128]{3,2,1,0:T(8,128)(2,1)} async-done(((bf16[32,4,32,128]{3,2,1,0:T(8,128)(2,1)}), bf16[32,4,32,128]{3,2,1,0:T(8,128)(2,1)}, u32[]{:S(2)}, u32[]{:S(2)}) %all-to-all-start) | async-done | bytes 1048608 | tf_op jit(solution)/shard_map/all_to_all | solution.py:322
  37.5 1.1 %collective-permute-start.8 = (f32[8,128]{1,0:T(8,128)S(1)}, f32[8,128]{1,0:T(8,128)S(1)}, u32[]{:S(2)}, u32[]{:S(2)}) collective-permute-start(f32[8,128]{1,0:T(8,128)S(1)} %add_add_fusion.1), channel_id=1, source_target_pairs={{0,8},{4,12},{8,0},{12,4},{1,9},{5,13},{9,1},{13,5},{2,10},{6,14},... | collective-permute-start | bytes 12296 | tf_op jit(solution)/shard_map/ppermute | solution.py:257
  38.6 0.8 collective-permute-start.7
  39.4 4.7 %field.1 = (bf16[512,128]{1,0:T(8,128)(2,1)}, bf16[32,128,128]{2,1,0:T(8,128)(2,1)}) custom-call(bf16[32,128,128]{2,1,0:T(8,128)(2,1)} %bitcast.3.arrived_ref, f32[4,128,128]{2,1,0:T(8,128)} %constant_dynamic-slice_fusion.1.potential_ref, bf16[512,512]{1,0:T(8,128)(2,1)} %constant.81.clone.inv_z_ref, bf16[256,256]{1,0:T(8,128)(2,1)} %constant.80.clone.inv_y_ref, ...), custom_call_target="tpu_custom_call" | custom-call | flops 6000000000 | bytes 6000000 | tf_op jit(solution)/shard_map/field/pallas_call | solution.py:372
  44.1 4.8 %all-to-all-start.1 = ((bf16[32,4,32,128]{3,2,1,0:T(8,128)(2,1)}), bf16[32,4,32,128]{3,2,1,0:T(8,128)(2,1)}, u32[]{:S(2)}, u32[]{:S(2)}) async-start(bf16[32,4,32,128]{3,2,1,0:T(8,128)(2,1)} %bitcast.14), calls=%async_computation.1 | async-start | bytes 2097152 | tf_op jit(solution)/shard_map/all_to_all | solution.py:322
  49.8 3.5 %collective-permute-done.3 = bf16[256,128]{1,0:T(8,128)(2,1)S(1)} collective-permute-done((bf16[256,128]{1,0:T(8,128)(2,1)S(1)}, bf16[256,128]{1,0:T(8,128)(2,1)S(1)}, u32[]{:S(2)}, u32[]{:S(2)}) %collective-permute-start.3) | collective-permute-done | bytes 65568 | tf_op jit(solution)/shard_map/ppermute | solution.py:428
  53.4 5.5 %collective-permute-start.6 = (bf16[256,128]{1,0:T(8,128)(2,1)S(1)}, bf16[256,128]{1,0:T(8,128)(2,1)S(1)}, u32[]{:S(2)}, u32[]{:S(2)}) collective-permute-start(bf16[256,128]{1,0:T(8,128)(2,1)S(1)} %add_convert_fusion.1), channel_id=1, source_target_pairs={{0,192},{16,208},{32,224},{48,240},{64,128},{80,144},{96,160},{112... | collective-permute-start | bytes 196616 | tf_op jit(solution)/shard_map/ppermute | solution.py:430
  58.9 1.4 %collective-permute-start.5 = (bf16[256,128]{1,0:T(8,128)(2,1)S(1)}, bf16[256,128]{1,0:T(8,128)(2,1)S(1)}, u32[]{:S(2)}, u32[]{:S(2)}) collective-permute-start(bf16[256,128]{1,0:T(8,128)(2,1)S(1)} %add_convert_fusion.1), channel_id=1, source_target_pairs={{0,128},{16,144},{32,160},{48,176},{64,192},{80,208},{96,224},{112... | collective-permute-start | bytes 196616 | tf_op jit(solution)/shard_map/ppermute | solution.py:430
  60.3 1.0 %collective-permute-start.4 = (bf16[256,128]{1,0:T(8,128)(2,1)S(1)}, bf16[256,128]{1,0:T(8,128)(2,1)S(1)}, u32[]{:S(2)}, u32[]{:S(2)}) collective-permute-start(bf16[256,128]{1,0:T(8,128)(2,1)S(1)} %add_convert_fusion.1), channel_id=1, source_target_pairs={{0,64},{16,80},{32,96},{48,112},{64,0},{80,16},{96,32},{112,48},{1... | collective-permute-start | bytes 196616 | tf_op jit(solution)/shard_map/ppermute | solution.py:430
  61.3 4.0 %base.1.base_ref = f32[2,32,32,256]{3,2,1,0:T(8,128)} custom-call(s32[2]{0:T(128)} %pad_add_fusion.first_ref, f32[8,128]{1,0:T(8,128)} %add_add_fusion.overlap_ref, bf16[2,32,32,256]{3,2,1,0:T(8,128)(2,1)} %orbitals_ref.5, s32[32,32,128]{2,1,0:T(8,128)} %mask_ref.7, bf16[4,32,32,128]{3,2,1,0:T(8,128)(2,1)} %channels_ref.3, bf16[16,1024]{1,0:T(8,128)(2,1)} %copy-done.2, ...), custom_call_target="tpu_custom_call" | custom-call | flops 4000000000 | bytes 4000000 | tf_op jit(solution)/shard_map/base/pallas_call | solution.py:395
  65.3 2.0 %collective-permute-done.5 = bf16[256,128]{1,0:T(8,128)(2,1)S(1)} collective-permute-done((bf16[256,128]{1,0:T(8,128)(2,1)S(1)}, bf16[256,128]{1,0:T(8,128)(2,1)S(1)}, u32[]{:S(2)}, u32[]{:S(2)}) %collective-permute-start.5) | collective-permute-done | bytes 65568 | tf_op jit(solution)/shard_map/ppermute | solution.py:430
  67.4 4.3 %collective-permute-start.12 = (bf16[256,128]{1,0:T(8,128)(2,1)S(1)}, bf16[256,128]{1,0:T(8,128)(2,1)S(1)}, u32[]{:S(2)}, u32[]{:S(2)}) collective-permute-start(bf16[256,128]{1,0:T(8,128)(2,1)S(1)} %add_convert_fusion), channel_id=1, source_target_pairs={{0,48},{16,32},{32,16},{48,0},{64,112},{80,96},{96,80},{112,64},{1... | collective-permute-start | bytes 196616 | tf_op jit(solution)/shard_map/ppermute | solution.py:435
  71.7 0.9 %collective-permute-start.11 = (bf16[256,128]{1,0:T(8,128)(2,1)S(1)}, bf16[256,128]{1,0:T(8,128)(2,1)S(1)}, u32[]{:S(2)}, u32[]{:S(2)}) collective-permute-start(bf16[256,128]{1,0:T(8,128)(2,1)S(1)} %add_convert_fusion), channel_id=1, source_target_pairs={{0,32},{16,48},{32,0},{48,16},{64,96},{80,112},{96,64},{112,80},{1... | collective-permute-start | bytes 196616 | tf_op jit(solution)/shard_map/ppermute | solution.py:435
  72.6 4.0 %apply.1 = bf16[2,32,32,256]{3,2,1,0:T(8,128)(2,1)} custom-call(bf16[32,4,32,128]{3,2,1,0:T(8,128)(2,1)} %all-to-all-done.1.returned_ref, f32[2,32,32,256]{3,2,1,0:T(8,128)} %base.1.base_ref, s32[32,32,128]{2,1,0:T(8,128)} %mask_ref.7, f32[2]{0:T(128)} %weight_ref.3, bf16[128,512]{1,0:T(8,128)(2,1)} %constant.84.clone.table_ref), custom_call_target="tpu_custom_call" | custom-call | flops 4000000000 | bytes 4000000 | tf_op jit(solution)/shard_map/apply/pallas_call | solution.py:436
  76.6 1.8 %collective-permute-done.10 = bf16[256,128]{1,0:T(8,128)(2,1)S(1)} collective-permute-done((bf16[256,128]{1,0:T(8,128)(2,1)S(1)}, bf16[256,128]{1,0:T(8,128)(2,1)S(1)}, u32[]{:S(2)}, u32[]{:S(2)}) %collective-permute-start.10) | collective-permute-done | bytes 65568 | tf_op jit(solution)/shard_map/ppermute | solution.py:435
  78.4 0.8 %convert.11 = f32[8,128,128]{2,1,0:T(8,128)} convert(bf16[8,128,128]{2,1,0:T(8,128)(2,1)S(1)} %bitcast.13) | non-fusion elementwise | flops 131072 | bytes 786432 | tf_op jit(solution)/shard_map/convert_element_type | solution.py:453
  (55 shorter events, 3.5 us)
Async XLA Ops:
  0.6 20.0 %copy-start = (f32[8,128,128]{2,1,0:T(8,128)S(1)}, f32[8,128,128]{2,1,0:T(8,128)}, u32[]{:S(2)}) copy-start(f32[8,128,128]{2,1,0:T(8,128)} %param.16) | copy-start | bytes 1572868
  0.7 3.4 %copy-start.4 = (f32[8,3]{0,1:T(4,128)S(1)}, f32[8,3]{0,1:T(4,128)}, u32[]{:S(2)}) copy-start(f32[8,3]{0,1:T(4,128)} %param.19) | copy-start | bytes 292
  5.4 0.6 copy-start.2
  8.8 11.7 %copy-start.6 = (s32[32]{0:T(128)S(1)}, s32[32]{0:T(128)}, u32[]{:S(2)}) copy-start(s32[32]{0:T(128)} %param.21) | copy-start | bytes 388
  8.8 11.7 %copy-start.7 = (s32[32]{0:T(128)S(1)}, s32[32]{0:T(128)}, u32[]{:S(2)}) copy-start(s32[32]{0:T(128)} %param.20) | copy-start | bytes 388
  8.8 11.7 %copy-start.5 = (f32[32]{0:T(128)S(1)}, f32[32]{0:T(128)}, u32[]{:S(2)}) copy-start(f32[32]{0:T(128)} %param.22) | copy-start | bytes 388
  8.8 13.9 %copy-start.3 = (f32[8,128]{1,0:T(8,128)S(1)}, f32[8,128]{1,0:T(8,128)}, u32[]{:S(2)}) copy-start(f32[8,128]{1,0:T(8,128)} %overlap.1) | copy-start | bytes 12292
  8.8 13.9 %collective-permute-start.2 = (f32[8,128]{1,0:T(8,128)}, f32[8,128]{1,0:T(8,128)S(1)}, u32[]{:S(2)}, u32[]{:S(2)}) collective-permute-start(f32[8,128]{1,0:T(8,128)} %overlap.1), channel_id=1, source_target_pairs={{0,3},{1,2},{2,1},{3,0},{4,7},{5,6},{6,5},{7,4},{8,11},{9,10},{10,... | collective-permute-start | bytes 12296 | tf_op jit(solution)/shard_map/ppermute | solution.py:257
  11.9 10.8 %collective-permute-start.1 = (f32[8,128]{1,0:T(8,128)}, f32[8,128]{1,0:T(8,128)S(1)}, u32[]{:S(2)}, u32[]{:S(2)}) collective-permute-start(f32[8,128]{1,0:T(8,128)} %overlap.1), channel_id=1, source_target_pairs={{0,2},{1,3},{2,0},{3,1},{4,6},{5,7},{6,4},{7,5},{8,10},{9,11},{10,... | collective-permute-start | bytes 12296 | tf_op jit(solution)/shard_map/ppermute | solution.py:257
  12.5 10.1 %collective-permute-start = (f32[8,128]{1,0:T(8,128)}, f32[8,128]{1,0:T(8,128)S(1)}, u32[]{:S(2)}, u32[]{:S(2)}) collective-permute-start(f32[8,128]{1,0:T(8,128)} %overlap.1), channel_id=1, source_target_pairs={{0,1},{1,0},{2,3},{3,2},{4,5},{5,4},{6,7},{7,6},{8,9},{9,8},{10,11... | collective-permute-start | bytes 12296 | tf_op jit(solution)/shard_map/ppermute | solution.py:257
  13.0 24.5 %all-to-all-start = ((bf16[32,4,32,128]{3,2,1,0:T(8,128)(2,1)}), bf16[32,4,32,128]{3,2,1,0:T(8,128)(2,1)}, u32[]{:S(2)}, u32[]{:S(2)}) async-start(bf16[32,4,32,128]{3,2,1,0:T(8,128)(2,1)} %spread.1), calls=%async_computation | async-start | bytes 2097152 | tf_op jit(solution)/shard_map/all_to_all | solution.py:322
  37.5 11.7 %collective-permute-start.9 = (f32[8,128]{1,0:T(8,128)S(1)}, f32[8,128]{1,0:T(8,128)S(1)}, u32[]{:S(2)}, u32[]{:S(2)}) collective-permute-start(f32[8,128]{1,0:T(8,128)S(1)} %add_add_fusion.1), channel_id=1, source_target_pairs={{0,12},{4,8},{8,4},{12,0},{1,13},{5,9},{9,5},{13,1},{2,14},{6,10},... | collective-permute-start | bytes 12296 | tf_op jit(solution)/shard_map/ppermute | solution.py:257
  37.5 11.7 %collective-permute-start.8 = (f32[8,128]{1,0:T(8,128)S(1)}, f32[8,128]{1,0:T(8,128)S(1)}, u32[]{:S(2)}, u32[]{:S(2)}) collective-permute-start(f32[8,128]{1,0:T(8,128)S(1)} %add_add_fusion.1), channel_id=1, source_target_pairs={{0,8},{4,12},{8,0},{12,4},{1,9},{5,13},{9,1},{13,5},{2,10},{6,14},... | collective-permute-start | bytes 12296 | tf_op jit(solution)/shard_map/ppermute | solution.py:257
  38.6 10.6 %collective-permute-start.7 = (f32[8,128]{1,0:T(8,128)S(1)}, f32[8,128]{1,0:T(8,128)S(1)}, u32[]{:S(2)}, u32[]{:S(2)}) collective-permute-start(f32[8,128]{1,0:T(8,128)S(1)} %add_add_fusion.1), channel_id=1, source_target_pairs={{0,4},{4,0},{8,12},{12,8},{1,5},{5,1},{9,13},{13,9},{2,6},{6,2},{1... | collective-permute-start | bytes 12296 | tf_op jit(solution)/shard_map/ppermute | solution.py:257
  44.1 4.8 %copy-start.1 = (bf16[512,128]{1,0:T(8,128)(2,1)S(1)}, bf16[512,128]{1,0:T(8,128)(2,1)}, u32[]{:S(2)}) copy-start(bf16[512,128]{1,0:T(8,128)(2,1)} %get-tuple-element.19) | copy-start | bytes 393220
  44.1 28.5 %all-to-all-start.1 = ((bf16[32,4,32,128]{3,2,1,0:T(8,128)(2,1)}), bf16[32,4,32,128]{3,2,1,0:T(8,128)(2,1)}, u32[]{:S(2)}, u32[]{:S(2)}) async-start(bf16[32,4,32,128]{3,2,1,0:T(8,128)(2,1)} %bitcast.14), calls=%async_computation.1 | async-start | bytes 2097152 | tf_op jit(solution)/shard_map/all_to_all | solution.py:322
  49.0 4.4 %collective-permute-start.3 = (bf16[256,128]{1,0:T(8,128)(2,1)S(1)}, bf16[256,128]{1,0:T(8,128)(2,1)S(1)}, u32[]{:S(2)}, u32[]{:S(2)}) collective-permute-start(bf16[256,128]{1,0:T(8,128)(2,1)S(1)} %constant_dynamic-slice_fusion), channel_id=1, source_target_pairs={{0,32},{16,48},{32,0},{48,16},{64,96},{80,112},{96,64},{112,80},{1... | collective-permute-start | bytes 196616 | tf_op jit(solution)/shard_map/ppermute | solution.py:428
  53.4 11.9 %collective-permute-start.6 = (bf16[256,128]{1,0:T(8,128)(2,1)S(1)}, bf16[256,128]{1,0:T(8,128)(2,1)S(1)}, u32[]{:S(2)}, u32[]{:S(2)}) collective-permute-start(bf16[256,128]{1,0:T(8,128)(2,1)S(1)} %add_convert_fusion.1), channel_id=1, source_target_pairs={{0,192},{16,208},{32,224},{48,240},{64,128},{80,144},{96,160},{112... | collective-permute-start | bytes 196616 | tf_op jit(solution)/shard_map/ppermute | solution.py:430
  58.9 8.5 %collective-permute-start.5 = (bf16[256,128]{1,0:T(8,128)(2,1)S(1)}, bf16[256,128]{1,0:T(8,128)(2,1)S(1)}, u32[]{:S(2)}, u32[]{:S(2)}) collective-permute-start(bf16[256,128]{1,0:T(8,128)(2,1)S(1)} %add_convert_fusion.1), channel_id=1, source_target_pairs={{0,128},{16,144},{32,160},{48,176},{64,192},{80,208},{96,224},{112... | collective-permute-start | bytes 196616 | tf_op jit(solution)/shard_map/ppermute | solution.py:430
  60.3 7.0 %collective-permute-start.4 = (bf16[256,128]{1,0:T(8,128)(2,1)S(1)}, bf16[256,128]{1,0:T(8,128)(2,1)S(1)}, u32[]{:S(2)}, u32[]{:S(2)}) collective-permute-start(bf16[256,128]{1,0:T(8,128)(2,1)S(1)} %add_convert_fusion.1), channel_id=1, source_target_pairs={{0,64},{16,80},{32,96},{48,112},{64,0},{80,16},{96,32},{112,48},{1... | collective-permute-start | bytes 196616 | tf_op jit(solution)/shard_map/ppermute | solution.py:430
  67.4 9.2 %collective-permute-start.12 = (bf16[256,128]{1,0:T(8,128)(2,1)S(1)}, bf16[256,128]{1,0:T(8,128)(2,1)S(1)}, u32[]{:S(2)}, u32[]{:S(2)}) collective-permute-start(bf16[256,128]{1,0:T(8,128)(2,1)S(1)} %add_convert_fusion), channel_id=1, source_target_pairs={{0,48},{16,32},{32,16},{48,0},{64,112},{80,96},{96,80},{112,64},{1... | collective-permute-start | bytes 196616 | tf_op jit(solution)/shard_map/ppermute | solution.py:435
  71.7 4.9 %collective-permute-start.11 = (bf16[256,128]{1,0:T(8,128)(2,1)S(1)}, bf16[256,128]{1,0:T(8,128)(2,1)S(1)}, u32[]{:S(2)}, u32[]{:S(2)}) collective-permute-start(bf16[256,128]{1,0:T(8,128)(2,1)S(1)} %add_convert_fusion), channel_id=1, source_target_pairs={{0,32},{16,48},{32,0},{48,16},{64,96},{80,112},{96,64},{112,80},{1... | collective-permute-start | bytes 196616 | tf_op jit(solution)/shard_map/ppermute | solution.py:435
  72.6 5.8 %collective-permute-start.10 = (bf16[256,128]{1,0:T(8,128)(2,1)S(1)}, bf16[256,128]{1,0:T(8,128)(2,1)S(1)}, u32[]{:S(2)}, u32[]{:S(2)}) collective-permute-start(bf16[256,128]{1,0:T(8,128)(2,1)S(1)} %add_convert_fusion), channel_id=1, source_target_pairs={{0,16},{16,0},{32,48},{48,32},{64,80},{80,64},{96,112},{112,96},{1... | collective-permute-start | bytes 196616 | tf_op jit(solution)/shard_map/ppermute | solution.py:435

commit v4 on v3

--- a/solution.py
+++ b/solution.py
@@ -360,7 +360,7 @@
         out_shape=jax.ShapeDtypeStruct((atoms, 128), f32),
         scratch_shapes=[pltpu.VMEM((2 * atoms, kinds * 4 * length), f32)],
         compiler_params=params,
-        cost_estimate=cost(3),
+        cost_estimate=cost(0.1),
         name="overlap",
     )(orbitals, cutoff_mask, channels, phase, wave)
     overlap = sum_over(overlap, "gz", (1, 2, 3))
@@ -409,7 +409,7 @@
         out_shape=jax.ShapeDtypeStruct(orbitals.shape, f32),
         scratch_shapes=[pltpu.VMEM((2 * atoms, kinds * 4 * length), bf16)],
         compiler_params=params,
-        cost_estimate=cost(4),
+        cost_estimate=cost(0.1),
         name="base",
     )(
         jnp.stack([first_y, first_z]).astype(jnp.int32),

time: 80.5 us -> 72 us (0.89)
  waiting for transfers between devices: 22.2 us -> 11.1 us
  starting transfers between devices: 31.7 us -> 33.8 us
    all_to_all x2, waiting for transfers between devices: 14.8 us -> 1.7 us  [exchange(): lax.all_to_all(chunks, ('band', 'gy', 'gz'), split_axis=0, concat_axis=0,...]
    ppermute x6, waiting for transfers between devices: 0.02 us -> 6.6 us  [sum_over(): lax.ppermute(part, axis, partners(axis, d)).astype(f32)]
    ppermute x3, starting transfers between devices: 7.95 us -> 10.2 us  [shards(): lax.ppermute(mine, 'band', partners('band', d * bands))]
    ppermute x3, waiting for transfers between devices: 2.02 us -> 0.01 us  [shards(): lax.ppermute(mine, 'band', partners('band', d * bands))]
    ppermute x1, waiting for transfers between devices: 3.53 us -> 1.7 us  [shards(): near = lax.ppermute(theirs, 'band', partners('band', bands))]
  transfers between devices with their start and end apart: 15 -> 15, of which waited for: 4 -> 7; matrix products, arithmetic and copies ran while one was open for 4% -> 7% of each run, Pallas kernels for 16% -> 15%
where the time goes in v4:
time: 72 us; the launch traced here: 70.9 us
  starting transfers between devices  33.8 us (47%)
  Pallas kernels  18.9 us (26%)
  waiting for transfers between devices  11.1 us (15%)
  other arithmetic  3.89 us (5%)
  local copies, waits for them, and re-layouts  2.31 us (3%)
  between operations  0.82 us (1%)
    all_to_all x2, starting transfers between devices, exchange(): lax.all_to_all(chunks, ('band', 'gy', 'gz'), split_axis=0, concat_axis=0,...  12.4 us
    ppermute x3, starting transfers between devices, shards(): lax.ppermute(mine, 'band', partners('band', d * bands))  10.2 us
    ppermute x6, waiting for transfers between devices, sum_over(): lax.ppermute(part, axis, partners(axis, d)).astype(f32)  6.6 us
    ppermute x6, starting transfers between devices, sum_over(): lax.ppermute(part, axis, partners(axis, d)).astype(f32)  5.95 us
    ppermute x3, starting transfers between devices, shards(): lax.ppermute(mine, 'band', partners('band', d))  5.08 us
    pallas_call x1, Pallas kernels, shards(): pl.pallas_call(field_kernel, grid=(bands,), in_specs=[band_spec, whole(pl...  4.74 us
    pallas_call x1, Pallas kernels, shards(): pl.pallas_call(base_kernel, grid=(steps,), in_specs=[smem_spec, whole(ato...  3.98 us
    pallas_call x1, Pallas kernels, shards(): pl.pallas_call(apply_kernel, grid=(steps,), in_specs=[chunks_spec, orbita...  3.98 us
  transfers between devices with their start and end apart: 15, of which 7 were waited for; matrix products, arithmetic and copies ran while one was open for 7% of the time, Pallas kernels for 15%

profile of v4, /device:TPU:32, one launch (start us, length us, event | category | flops | bytes accessed | tf_op | source)
XLA Modules:
  0.0 70.9 jit_solution(10815055684154342401)
XLA Ops:
  0.6 3.4 %spread.1 = bf16[32,4,32,128]{3,2,1,0:T(8,128)(2,1)} custom-call(bf16[2,32,32,256]{3,2,1,0:T(8,128)(2,1)} %orbitals_ref.5, s32[32,32,128]{2,1,0:T(8,128)} %mask_ref.7, f32[2]{0:T(128)} %weight_ref.3, bf16[256,256]{1,0:T(8,128)(2,1)} %constant.79.clone.table_ref), custom_call_target="tpu_custom_call" | custom-call | flops 4000000000 | bytes 4000000 | tf_op jit(solution)/shard_map/spread/pallas_call | solution.py:326
  4.1 7.6 %all-to-all-start = ((bf16[32,4,32,128]{3,2,1,0:T(8,128)(2,1)}), bf16[32,4,32,128]{3,2,1,0:T(8,128)(2,1)}, u32[]{:S(2)}, u32[]{:S(2)}) async-start(bf16[32,4,32,128]{3,2,1,0:T(8,128)(2,1)} %spread.1), calls=%async_computation | async-start | bytes 2097152 | tf_op jit(solution)/shard_map/all_to_all | solution.py:322
  13.6 2.8 %overlap.1 = f32[8,128]{1,0:T(8,128)} custom-call(bf16[2,32,32,256]{3,2,1,0:T(8,128)(2,1)} %orbitals_ref.5, s32[32,32,128]{2,1,0:T(8,128)} %mask_ref.7, bf16[4,32,32,128]{3,2,1,0:T(8,128)(2,1)} %channels_ref.3, bf16[16,1024]{1,0:T(8,128)(2,1)} %copy-done.1, f32[16,128]{1,0:T(8,128)} %pad_maximum_fusion.1.wave_ref), custom_call_target="tpu_custom_call" | custom-call | flops 100000000 | bytes 100000 | tf_op jit(solution)/shard_map/overlap/pallas_call | solution.py:355
  16.4 2.9 %collective-permute-start.2 = (f32[8,128]{1,0:T(8,128)}, f32[8,128]{1,0:T(8,128)S(1)}, u32[]{:S(2)}, u32[]{:S(2)}) collective-permute-start(f32[8,128]{1,0:T(8,128)} %overlap.1), channel_id=1, source_target_pairs={{0,3},{1,2},{2,1},{3,0},{4,7},{5,6},{6,5},{7,4},{8,11},{9,10},{10,... | collective-permute-start | bytes 12296 | tf_op jit(solution)/shard_map/ppermute | solution.py:257
  19.3 0.9 %collective-permute-start.1 = (f32[8,128]{1,0:T(8,128)}, f32[8,128]{1,0:T(8,128)S(1)}, u32[]{:S(2)}, u32[]{:S(2)}) collective-permute-start(f32[8,128]{1,0:T(8,128)} %overlap.1), channel_id=1, source_target_pairs={{0,2},{1,3},{2,0},{3,1},{4,6},{5,7},{6,4},{7,5},{8,10},{9,11},{10,... | collective-permute-start | bytes 12296 | tf_op jit(solution)/shard_map/ppermute | solution.py:257
  20.5 0.7 %constant_dynamic-slice_fusion.1.potential_ref = f32[4,128,128]{2,1,0:T(8,128)} fusion(f32[8,128,128]{2,1,0:T(8,128)S(1)} %copy-done, s32[]{:T(128)S(6)} %select_n.93), kind=kLoop, calls=%fused_computation.34 | loop fusion | bytes 524292 | tf_op jit(solution)/shard_map/dynamic_slice | solution.py:337
  21.2 1.8 %collective-permute-done.2 = f32[8,128]{1,0:T(8,128)S(1)} collective-permute-done((f32[8,128]{1,0:T(8,128)}, f32[8,128]{1,0:T(8,128)S(1)}, u32[]{:S(2)}, u32[]{:S(2)}) %collective-permute-start.2) | collective-permute-done | bytes 4128 | tf_op jit(solution)/shard_map/ppermute | solution.py:257
  23.0 1.6 %collective-permute-done.1 = f32[8,128]{1,0:T(8,128)S(1)} collective-permute-done((f32[8,128]{1,0:T(8,128)}, f32[8,128]{1,0:T(8,128)S(1)}, u32[]{:S(2)}, u32[]{:S(2)}) %collective-permute-start.1) | collective-permute-done | bytes 4128 | tf_op jit(solution)/shard_map/ppermute | solution.py:257
  24.6 1.7 %collective-permute-done = f32[8,128]{1,0:T(8,128)S(1)} collective-permute-done((f32[8,128]{1,0:T(8,128)}, f32[8,128]{1,0:T(8,128)S(1)}, u32[]{:S(2)}, u32[]{:S(2)}) %collective-permute-start) | collective-permute-done | bytes 4128 | tf_op jit(solution)/shard_map/ppermute | solution.py:257
  27.0 1.7 %all-to-all-done = bf16[32,4,32,128]{3,2,1,0:T(8,128)(2,1)} async-done(((bf16[32,4,32,128]{3,2,1,0:T(8,128)(2,1)}), bf16[32,4,32,128]{3,2,1,0:T(8,128)(2,1)}, u32[]{:S(2)}, u32[]{:S(2)}) %all-to-all-start) | async-done | bytes 1048608 | tf_op jit(solution)/shard_map/all_to_all | solution.py:322
  28.7 4.7 %field.1 = (bf16[512,128]{1,0:T(8,128)(2,1)}, bf16[32,128,128]{2,1,0:T(8,128)(2,1)}) custom-call(bf16[32,128,128]{2,1,0:T(8,128)(2,1)} %bitcast.3.arrived_ref, f32[4,128,128]{2,1,0:T(8,128)} %constant_dynamic-slice_fusion.1.potential_ref, bf16[512,512]{1,0:T(8,128)(2,1)} %constant.81.clone.inv_z_ref, bf16[256,256]{1,0:T(8,128)(2,1)} %constant.80.clone.inv_y_ref, ...), custom_call_target="tpu_custom_call" | custom-call | flops 6000000000 | bytes 6000000 | tf_op jit(solution)/shard_map/field/pallas_call | solution.py:372
  33.5 4.8 %all-to-all-start.1 = ((bf16[32,4,32,128]{3,2,1,0:T(8,128)(2,1)}), bf16[32,4,32,128]{3,2,1,0:T(8,128)(2,1)}, u32[]{:S(2)}, u32[]{:S(2)}) async-start(bf16[32,4,32,128]{3,2,1,0:T(8,128)(2,1)} %bitcast.14), calls=%async_computation.1 | async-start | bytes 2097152 | tf_op jit(solution)/shard_map/all_to_all | solution.py:322
  39.9 1.3 %collective-permute-start.9 = (f32[8,128]{1,0:T(8,128)S(1)}, f32[8,128]{1,0:T(8,128)S(1)}, u32[]{:S(2)}, u32[]{:S(2)}) collective-permute-start(f32[8,128]{1,0:T(8,128)S(1)} %add_add_fusion.1), channel_id=1, source_target_pairs={{0,12},{4,8},{8,4},{12,0},{1,13},{5,9},{9,5},{13,1},{2,14},{6,10},... | collective-permute-start | bytes 12296 | tf_op jit(solution)/shard_map/ppermute | solution.py:257
  41.7 1.7 %collective-permute-done.3 = bf16[256,128]{1,0:T(8,128)(2,1)S(1)} collective-permute-done((bf16[256,128]{1,0:T(8,128)(2,1)S(1)}, bf16[256,128]{1,0:T(8,128)(2,1)S(1)}, u32[]{:S(2)}, u32[]{:S(2)}) %collective-permute-start.3) | collective-permute-done | bytes 65568 | tf_op jit(solution)/shard_map/ppermute | solution.py:428
  43.5 5.5 %collective-permute-start.6 = (bf16[256,128]{1,0:T(8,128)(2,1)S(1)}, bf16[256,128]{1,0:T(8,128)(2,1)S(1)}, u32[]{:S(2)}, u32[]{:S(2)}) collective-permute-start(bf16[256,128]{1,0:T(8,128)(2,1)S(1)} %add_convert_fusion.1), channel_id=1, source_target_pairs={{0,192},{16,208},{32,224},{48,240},{64,128},{80,144},{96,160},{112... | collective-permute-start | bytes 196616 | tf_op jit(solution)/shard_map/ppermute | solution.py:430
  49.0 1.4 %collective-permute-start.5 = (bf16[256,128]{1,0:T(8,128)(2,1)S(1)}, bf16[256,128]{1,0:T(8,128)(2,1)S(1)}, u32[]{:S(2)}, u32[]{:S(2)}) collective-permute-start(bf16[256,128]{1,0:T(8,128)(2,1)S(1)} %add_convert_fusion.1), channel_id=1, source_target_pairs={{0,128},{16,144},{32,160},{48,176},{64,192},{80,208},{96,224},{112... | collective-permute-start | bytes 196616 | tf_op jit(solution)/shard_map/ppermute | solution.py:430
  50.4 1.5 %collective-permute-done.9 = f32[8,128]{1,0:T(8,128)S(1)} collective-permute-done((f32[8,128]{1,0:T(8,128)S(1)}, f32[8,128]{1,0:T(8,128)S(1)}, u32[]{:S(2)}, u32[]{:S(2)}) %collective-permute-start.9) | collective-permute-done | bytes 4128 | tf_op jit(solution)/shard_map/ppermute | solution.py:257
  51.9 3.3 %collective-permute-start.4 = (bf16[256,128]{1,0:T(8,128)(2,1)S(1)}, bf16[256,128]{1,0:T(8,128)(2,1)S(1)}, u32[]{:S(2)}, u32[]{:S(2)}) collective-permute-start(bf16[256,128]{1,0:T(8,128)(2,1)S(1)} %add_convert_fusion.1), channel_id=1, source_target_pairs={{0,64},{16,80},{32,96},{48,112},{64,0},{80,16},{96,32},{112,48},{1... | collective-permute-start | bytes 196616 | tf_op jit(solution)/shard_map/ppermute | solution.py:430
  55.7 4.0 %base.1.base_ref = f32[2,32,32,256]{3,2,1,0:T(8,128)} custom-call(s32[2]{0:T(128)} %pad_add_fusion.first_ref, f32[8,128]{1,0:T(8,128)} %add_add_fusion.overlap_ref, bf16[2,32,32,256]{3,2,1,0:T(8,128)(2,1)} %orbitals_ref.5, s32[32,32,128]{2,1,0:T(8,128)} %mask_ref.7, bf16[4,32,32,128]{3,2,1,0:T(8,128)(2,1)} %channels_ref.3, bf16[16,1024]{1,0:T(8,128)(2,1)} %copy-done.1, ...), custom_call_target="tpu_custom_call" | custom-call | flops 100000000 | bytes 100000 | tf_op jit(solution)/shard_map/base/pallas_call | solution.py:395
  59.8 3.2 %collective-permute-start.12 = (bf16[256,128]{1,0:T(8,128)(2,1)S(1)}, bf16[256,128]{1,0:T(8,128)(2,1)S(1)}, u32[]{:S(2)}, u32[]{:S(2)}) collective-permute-start(bf16[256,128]{1,0:T(8,128)(2,1)S(1)} %add_convert_fusion), channel_id=1, source_target_pairs={{0,48},{16,32},{32,16},{48,0},{64,112},{80,96},{96,80},{112,64},{1... | collective-permute-start | bytes 196616 | tf_op jit(solution)/shard_map/ppermute | solution.py:435
  63.0 1.2 %collective-permute-start.11 = (bf16[256,128]{1,0:T(8,128)(2,1)S(1)}, bf16[256,128]{1,0:T(8,128)(2,1)S(1)}, u32[]{:S(2)}, u32[]{:S(2)}) collective-permute-start(bf16[256,128]{1,0:T(8,128)(2,1)S(1)} %add_convert_fusion), channel_id=1, source_target_pairs={{0,32},{16,48},{32,0},{48,16},{64,96},{80,112},{96,64},{112,80},{1... | collective-permute-start | bytes 196616 | tf_op jit(solution)/shard_map/ppermute | solution.py:435
  64.9 4.0 %apply.1 = bf16[2,32,32,256]{3,2,1,0:T(8,128)(2,1)} custom-call(bf16[32,4,32,128]{3,2,1,0:T(8,128)(2,1)} %all-to-all-done.1.returned_ref, f32[2,32,32,256]{3,2,1,0:T(8,128)} %base.1.base_ref, s32[32,32,128]{2,1,0:T(8,128)} %mask_ref.7, f32[2]{0:T(128)} %weight_ref.3, bf16[128,512]{1,0:T(8,128)(2,1)} %constant.84.clone.table_ref), custom_call_target="tpu_custom_call" | custom-call | flops 4000000000 | bytes 4000000 | tf_op jit(solution)/shard_map/apply/pallas_call | solution.py:436
  68.9 1.1 %collective-permute-done.10 = bf16[256,128]{1,0:T(8,128)(2,1)S(1)} collective-permute-done((bf16[256,128]{1,0:T(8,128)(2,1)S(1)}, bf16[256,128]{1,0:T(8,128)(2,1)S(1)}, u32[]{:S(2)}, u32[]{:S(2)}) %collective-permute-start.10) | collective-permute-done | bytes 65568 | tf_op jit(solution)/shard_map/ppermute | solution.py:435
  70.0 0.8 %convert.11 = f32[8,128,128]{2,1,0:T(8,128)} convert(bf16[8,128,128]{2,1,0:T(8,128)(2,1)S(1)} %bitcast.13) | non-fusion elementwise | flops 131072 | bytes 786432 | tf_op jit(solution)/shard_map/convert_element_type | solution.py:453
  (53 shorter events, 6.4 us)
Async XLA Ops:
  0.6 19.9 %copy-start = (f32[8,128,128]{2,1,0:T(8,128)S(1)}, f32[8,128,128]{2,1,0:T(8,128)}, u32[]{:S(2)}) copy-start(f32[8,128,128]{2,1,0:T(8,128)} %param.16) | copy-start | bytes 1572868
  4.0 7.7 %copy-start.3 = (f32[8,3]{0,1:T(4,128)S(1)}, f32[8,3]{0,1:T(4,128)}, u32[]{:S(2)}) copy-start(f32[8,3]{0,1:T(4,128)} %param.19) | copy-start | bytes 292
  4.1 24.7 %all-to-all-start = ((bf16[32,4,32,128]{3,2,1,0:T(8,128)(2,1)}), bf16[32,4,32,128]{3,2,1,0:T(8,128)(2,1)}, u32[]{:S(2)}, u32[]{:S(2)}) async-start(bf16[32,4,32,128]{3,2,1,0:T(8,128)(2,1)} %spread.1), calls=%async_computation | async-start | bytes 2097152 | tf_op jit(solution)/shard_map/all_to_all | solution.py:322
  11.6 8.8 %copy-start.5 = (s32[32]{0:T(128)S(1)}, s32[32]{0:T(128)}, u32[]{:S(2)}) copy-start(s32[32]{0:T(128)} %param.21) | copy-start | bytes 388
  11.6 8.8 %copy-start.6 = (s32[32]{0:T(128)S(1)}, s32[32]{0:T(128)}, u32[]{:S(2)}) copy-start(s32[32]{0:T(128)} %param.20) | copy-start | bytes 388
  13.0 0.6 copy-start.1
  16.4 6.6 %collective-permute-start.2 = (f32[8,128]{1,0:T(8,128)}, f32[8,128]{1,0:T(8,128)S(1)}, u32[]{:S(2)}, u32[]{:S(2)}) collective-permute-start(f32[8,128]{1,0:T(8,128)} %overlap.1), channel_id=1, source_target_pairs={{0,3},{1,2},{2,1},{3,0},{4,7},{5,6},{6,5},{7,4},{8,11},{9,10},{10,... | collective-permute-start | bytes 12296 | tf_op jit(solution)/shard_map/ppermute | solution.py:257
  19.3 5.3 %collective-permute-start.1 = (f32[8,128]{1,0:T(8,128)}, f32[8,128]{1,0:T(8,128)S(1)}, u32[]{:S(2)}, u32[]{:S(2)}) collective-permute-start(f32[8,128]{1,0:T(8,128)} %overlap.1), channel_id=1, source_target_pairs={{0,2},{1,3},{2,0},{3,1},{4,6},{5,7},{6,4},{7,5},{8,10},{9,11},{10,... | collective-permute-start | bytes 12296 | tf_op jit(solution)/shard_map/ppermute | solution.py:257
  20.2 6.2 %collective-permute-start = (f32[8,128]{1,0:T(8,128)}, f32[8,128]{1,0:T(8,128)S(1)}, u32[]{:S(2)}, u32[]{:S(2)}) collective-permute-start(f32[8,128]{1,0:T(8,128)} %overlap.1), channel_id=1, source_target_pairs={{0,1},{1,0},{2,3},{3,2},{4,5},{5,4},{6,7},{7,6},{8,9},{9,8},{10,11... | collective-permute-start | bytes 12296 | tf_op jit(solution)/shard_map/ppermute | solution.py:257
  33.5 4.8 %copy-start.4 = (f32[32]{0:T(128)S(1)}, f32[32]{0:T(128)}, u32[]{:S(2)}) copy-start(f32[32]{0:T(128)} %param.22) | copy-start | bytes 388
  33.5 5.6 %copy-start.2 = (bf16[512,128]{1,0:T(8,128)(2,1)S(1)}, bf16[512,128]{1,0:T(8,128)(2,1)}, u32[]{:S(2)}) copy-start(bf16[512,128]{1,0:T(8,128)(2,1)} %get-tuple-element.19) | copy-start | bytes 393220
  33.5 31.4 %all-to-all-start.1 = ((bf16[32,4,32,128]{3,2,1,0:T(8,128)(2,1)}), bf16[32,4,32,128]{3,2,1,0:T(8,128)(2,1)}, u32[]{:S(2)}, u32[]{:S(2)}) async-start(bf16[32,4,32,128]{3,2,1,0:T(8,128)(2,1)} %bitcast.14), calls=%async_computation.1 | async-start | bytes 2097152 | tf_op jit(solution)/shard_map/all_to_all | solution.py:322
  39.1 4.4 %collective-permute-start.3 = (bf16[256,128]{1,0:T(8,128)(2,1)S(1)}, bf16[256,128]{1,0:T(8,128)(2,1)S(1)}, u32[]{:S(2)}, u32[]{:S(2)}) collective-permute-start(bf16[256,128]{1,0:T(8,128)(2,1)S(1)} %constant_dynamic-slice_fusion), channel_id=1, source_target_pairs={{0,32},{16,48},{32,0},{48,16},{64,96},{80,112},{96,64},{112,80},{1... | collective-permute-start | bytes 196616 | tf_op jit(solution)/shard_map/ppermute | solution.py:428
  39.9 12.0 %collective-permute-start.9 = (f32[8,128]{1,0:T(8,128)S(1)}, f32[8,128]{1,0:T(8,128)S(1)}, u32[]{:S(2)}, u32[]{:S(2)}) collective-permute-start(f32[8,128]{1,0:T(8,128)S(1)} %add_add_fusion.1), channel_id=1, source_target_pairs={{0,12},{4,8},{8,4},{12,0},{1,13},{5,9},{9,5},{13,1},{2,14},{6,10},... | collective-permute-start | bytes 12296 | tf_op jit(solution)/shard_map/ppermute | solution.py:257
  41.2 13.9 %collective-permute-start.8 = (f32[8,128]{1,0:T(8,128)S(1)}, f32[8,128]{1,0:T(8,128)S(1)}, u32[]{:S(2)}, u32[]{:S(2)}) collective-permute-start(f32[8,128]{1,0:T(8,128)S(1)} %add_add_fusion.1), channel_id=1, source_target_pairs={{0,8},{4,12},{8,0},{12,4},{1,9},{5,13},{9,1},{13,5},{2,10},{6,14},... | collective-permute-start | bytes 12296 | tf_op jit(solution)/shard_map/ppermute | solution.py:257
  41.6 13.5 %collective-permute-start.7 = (f32[8,128]{1,0:T(8,128)S(1)}, f32[8,128]{1,0:T(8,128)S(1)}, u32[]{:S(2)}, u32[]{:S(2)}) collective-permute-start(f32[8,128]{1,0:T(8,128)S(1)} %add_add_fusion.1), channel_id=1, source_target_pairs={{0,4},{4,0},{8,12},{12,8},{1,5},{5,1},{9,13},{13,9},{2,6},{6,2},{1... | collective-permute-start | bytes 12296 | tf_op jit(solution)/shard_map/ppermute | solution.py:257
  43.5 16.3 %collective-permute-start.6 = (bf16[256,128]{1,0:T(8,128)(2,1)S(1)}, bf16[256,128]{1,0:T(8,128)(2,1)S(1)}, u32[]{:S(2)}, u32[]{:S(2)}) collective-permute-start(bf16[256,128]{1,0:T(8,128)(2,1)S(1)} %add_convert_fusion.1), channel_id=1, source_target_pairs={{0,192},{16,208},{32,224},{48,240},{64,128},{80,144},{96,160},{112... | collective-permute-start | bytes 196616 | tf_op jit(solution)/shard_map/ppermute | solution.py:430
  49.0 10.8 %collective-permute-start.5 = (bf16[256,128]{1,0:T(8,128)(2,1)S(1)}, bf16[256,128]{1,0:T(8,128)(2,1)S(1)}, u32[]{:S(2)}, u32[]{:S(2)}) collective-permute-start(bf16[256,128]{1,0:T(8,128)(2,1)S(1)} %add_convert_fusion.1), channel_id=1, source_target_pairs={{0,128},{16,144},{32,160},{48,176},{64,192},{80,208},{96,224},{112... | collective-permute-start | bytes 196616 | tf_op jit(solution)/shard_map/ppermute | solution.py:430
  51.9 7.9 %collective-permute-start.4 = (bf16[256,128]{1,0:T(8,128)(2,1)S(1)}, bf16[256,128]{1,0:T(8,128)(2,1)S(1)}, u32[]{:S(2)}, u32[]{:S(2)}) collective-permute-start(bf16[256,128]{1,0:T(8,128)(2,1)S(1)} %add_convert_fusion.1), channel_id=1, source_target_pairs={{0,64},{16,80},{32,96},{48,112},{64,0},{80,16},{96,32},{112,48},{1... | collective-permute-start | bytes 196616 | tf_op jit(solution)/shard_map/ppermute | solution.py:430
  59.8 9.1 %collective-permute-start.12 = (bf16[256,128]{1,0:T(8,128)(2,1)S(1)}, bf16[256,128]{1,0:T(8,128)(2,1)S(1)}, u32[]{:S(2)}, u32[]{:S(2)}) collective-permute-start(bf16[256,128]{1,0:T(8,128)(2,1)S(1)} %add_convert_fusion), channel_id=1, source_target_pairs={{0,48},{16,32},{32,16},{48,0},{64,112},{80,96},{96,80},{112,64},{1... | collective-permute-start | bytes 196616 | tf_op jit(solution)/shard_map/ppermute | solution.py:435
  63.0 5.8 %collective-permute-start.11 = (bf16[256,128]{1,0:T(8,128)(2,1)S(1)}, bf16[256,128]{1,0:T(8,128)(2,1)S(1)}, u32[]{:S(2)}, u32[]{:S(2)}) collective-permute-start(bf16[256,128]{1,0:T(8,128)(2,1)S(1)} %add_convert_fusion), channel_id=1, source_target_pairs={{0,32},{16,48},{32,0},{48,16},{64,96},{80,112},{96,64},{112,80},{1... | collective-permute-start | bytes 196616 | tf_op jit(solution)/shard_map/ppermute | solution.py:435
  64.2 5.8 %collective-permute-start.10 = (bf16[256,128]{1,0:T(8,128)(2,1)S(1)}, bf16[256,128]{1,0:T(8,128)(2,1)S(1)}, u32[]{:S(2)}, u32[]{:S(2)}) collective-permute-start(bf16[256,128]{1,0:T(8,128)(2,1)S(1)} %add_convert_fusion), channel_id=1, source_target_pairs={{0,16},{16,0},{32,48},{48,32},{64,80},{80,64},{96,112},{112,96},{1... | collective-permute-start | bytes 196616 | tf_op jit(solution)/shard_map/ppermute | solution.py:435

commit v5 on v4

--- a/solution.py
+++ b/solution.py
@@ -64,16 +64,17 @@
     mask = jnp.concatenate([mask, mask], axis=2)
     lane = lax.broadcasted_iota(jnp.int32, (length, 128), 1)
     roots = root_weights(weight_ref, (1, 128), 1, rows_z)
+    spreads = []
     for pair in range(0, rows_y, 2):
         rows = []
         for y in (pair, pair + 1):
             both = jnp.concatenate([orbitals_ref[0, y] * mask[y], orbitals_ref[1, y] * mask[y]], axis=0)
             rows += [both, both]
-        spread = dot_nt(table_ref[...], jnp.concatenate(rows, axis=0))
-        for half in range(2):
-            cols = slice(half * 128, half * 128 + 128)
-            tile = jnp.where(lane < 64, spread[:length, cols], spread[length:, cols])
-            work_ref[pl.ds(pair + half, length, stride=rows_y), :] = tile * roots
+        spreads.append(dot_nt(table_ref[...], jnp.concatenate(rows, axis=0)))
+    for y in range(rows_y):
+        spread = spreads[y // 2][:, y % 2 * 128 : y % 2 * 128 + 128]
+        tile = jnp.where(lane < 64, spread[:length], spread[length:])
+        work_ref[pl.ds(y, length, stride=rows_y), :] = tile * roots
     out_ref[...] = work_ref[...].reshape(out_ref.shape).astype(bf16)
 
 
@@ -115,17 +116,20 @@
             imag_over = jnp.sum(real * sin_x + imag * cos_x, axis=1, keepdims=True)
             total = jnp.where(lane == 2 * pair, real_over, total)
             total = jnp.where(lane == 2 * pair + 1, imag_over, total)
-        out_ref[...] = total
+        high = total.astype(bf16).astype(f32)
+        out_ref[...] = jnp.concatenate([high, total - high], axis=0).astype(bf16)
 
 
 def field_kernel(
     arrived_ref,
     potential_ref,
+    overlap_ref,
     inv_z_ref,
     inv_y_ref,
     fwd_z_ref,
     fwd_y_ref,
-    density_ref,
+    mine_ref,
+    theirs_ref,
     out_ref,
     sums_ref,
 ):
@@ -164,21 +168,30 @@
             jnp.concatenate([real[:, :length], imag[:, :length], real[:, length:], imag[:, length:]], axis=1)
         )
     back = dot(jnp.concatenate(back, axis=0), fwd_z_ref[...]).astype(bf16)
+    span = rows // 2
     for x in range(planes):
         for sy in range(parts):
-            start = x * length + sy * rows
-            for sz in range(4):
-                out_ref[sy * 4 + sz, x * rows : (x + 1) * rows, :] = back[
-                    start : start + rows, sz * 128 : sz * 128 + 128
-                ]
+            for half in range(2):
+                start = x * length + sy * rows + half * span
+                row = (half * planes + x) * span
+                for sz in range(4):
+                    out_ref[sy * 4 + sz, row : row + span, :] = back[
+                        start : start + span, sz * 128 : sz * 128 + 128
+                    ]
+    for place in range(out_ref.shape[0]):
+        out_ref[place, planes * rows :, :] = overlap_ref[...]
 
     @pl.when(step == pl.num_programs(0) - 1)
     def last():
-        density_ref[...] = sums_ref[...].astype(bf16)
-
-
-def base_kernel(
-    first_ref,
+        half = planes // 2 * length
+        low, high = sums_ref[:half, :].astype(bf16), sums_ref[half:, :].astype(bf16)
+        upper = lax.axis_index("band") // 2 % 2
+        mine_ref[...] = jnp.where(upper == 0, low, high)
+        theirs_ref[...] = jnp.where(upper == 0, high, low)
+
+
+def apply_kernel(
+    returned_ref,
     overlap_ref,
     orbitals_ref,
     mask_ref,
@@ -186,18 +199,29 @@
     phase_ref,
     wave_ref,
     strength_ref,
+    weight_ref,
+    table_ref,
     out_ref,
     factor_ref,
+    work_ref,
 ):
     step = pl.program_id(0)
     rows_y, rows_z, length = mask_ref.shape
     atoms = wave_ref.shape[0] // 2
     kinds = channels_ref.shape[0]
 
+    work_ref[...] = returned_ref[...].astype(f32).reshape(work_ref.shape)
+    planes = [work_ref[pl.ds(y, length, stride=rows_y), :].astype(bf16) for y in range(rows_y)]
+    local = [dot_tn(jnp.concatenate(planes[y : y + 2], axis=1), table_ref[...]) for y in range(0, rows_y, 2)]
+
     @pl.when(step == 0)
     def factors():
         cos_x, sin_x = wave_ref[:atoms], wave_ref[atoms:]
-        coef = overlap_ref[...] * strength_ref[...]
+        sources = overlap_ref.shape[0] // 2
+        even = jnp.sum(overlap_ref[:sources].astype(f32), axis=0)
+        odd = jnp.sum(overlap_ref[sources:].astype(f32), axis=0)
+        summed = jnp.where(lax.axis_index("band") % 2 == 0, even, odd)
+        coef = (summed[:atoms] + summed[atoms:]) * strength_ref[...]
         for pair in range(kinds * 2):
             coef_real = coef[:, 2 * pair : 2 * pair + 1]
             coef_imag = coef[:, 2 * pair + 1 : 2 * pair + 2]
@@ -209,53 +233,35 @@
                 [imag, -real], axis=0
             ).astype(bf16)
 
+    extra = dot_tn(phase_ref[...], factor_ref[...])
+
     def squared(start, axis):
         index = start + lax.broadcasted_iota(jnp.int32, mask_ref.shape, axis)
         wave = jnp.where(index >= length // 2, index - length, index)
         return wave * wave
 
-    energy = squared(first_ref[0] + step * rows_y, 0) + squared(first_ref[1], 1) + squared(0, 2)
+    first_y = lax.axis_index("gy") * (rows_y * pl.num_programs(0)) + step * rows_y
+    energy = squared(first_y, 0) + squared(lax.axis_index("gz") * rows_z, 1) + squared(0, 2)
     energy = kinetic_scale * 0.5 * energy.astype(f32)
+    inside = mask_ref[...] != 0
+    scale = 1.0 / root_weights(weight_ref, (2 * rows_z, 1), 0, rows_z)
     for y in range(rows_y):
-        extra = dot_tn(phase_ref[:, y * rows_z : (y + 1) * rows_z], factor_ref[...])
+        block = local[y // 2][y % 2 * 128 : y % 2 * 128 + 128]
+        both = scale * (block[:64, : 2 * length] + block[64:, 2 * length :])
         radials = [channels_ref[c, y].astype(f32) for c in range(kinds)]
         for n in range(2):
             for part in range(2):
                 cols = slice(part * length, part * length + length)
-                total = energy[y] * orbitals_ref[n, y, :, cols].astype(f32)
+                total = both[n * rows_z : (n + 1) * rows_z, cols]
+                total = total + energy[y] * orbitals_ref[n, y, :, cols].astype(f32)
                 for c in range(kinds):
                     base = ((c * 2 + n) * 2 + part) * length
-                    total = total + radials[c] * extra[:, base : base + length]
-                out_ref[n, y, :, cols] = total
-
-
-def apply_kernel(returned_ref, base_ref, mask_ref, weight_ref, table_ref, out_ref, work_ref):
-    rows_y, rows_z, length = mask_ref.shape
-    scale = 1.0 / root_weights(weight_ref, (2 * rows_z, 1), 0, rows_z)
-    work_ref[...] = returned_ref[...].astype(f32).reshape(work_ref.shape)
-    inside = mask_ref[...] != 0
-    for pair in range(0, rows_y, 2):
-        planes = jnp.concatenate(
-            [work_ref[pl.ds(y, length, stride=rows_y), :].astype(bf16) for y in (pair, pair + 1)], axis=1
-        )
-        local = dot_tn(planes, table_ref[...])
-        for half in range(2):
-            y = pair + half
-            both = local[half * 128 : half * 128 + 64, : 2 * length]
-            both = scale * (both + local[half * 128 + 64 : half * 128 + 128, 2 * length :])
-            keep = jnp.concatenate([inside[y], inside[y]], axis=1)
-            for n in range(2):
-                total = both[n * rows_z : (n + 1) * rows_z] + base_ref[n, y]
-                out_ref[n, y] = jnp.where(keep, total, 0.0).astype(bf16)
+                    total = total + radials[c] * extra[y * rows_z : (y + 1) * rows_z, base : base + length]
+                out_ref[n, y, :, cols] = jnp.where(inside[y], total, 0.0).astype(bf16)
 
 
 def partners(axis, distance):
     return [(i, i ^ distance) for i in range(lax.axis_size(axis))]
-
-
-def sum_over(part, axis, distances):
-    got = [lax.ppermute(part, axis, partners(axis, d)).astype(f32) for d in distances]
-    return (part.astype(f32) + got[0]) + (got[1] + got[2])
 
 
 def shards(
@@ -356,100 +362,83 @@
         overlap_kernel,
         grid=(steps,),
         in_specs=[orbitals_spec, mask_spec, channels_spec, phase_spec, whole(2 * atoms, length)],
-        out_specs=whole(atoms, 128),
-        out_shape=jax.ShapeDtypeStruct((atoms, 128), f32),
+        out_specs=whole(2 * atoms, 128),
+        out_shape=jax.ShapeDtypeStruct((2 * atoms, 128), bf16),
         scratch_shapes=[pltpu.VMEM((2 * atoms, kinds * 4 * length), f32)],
         compiler_params=params,
         cost_estimate=cost(0.1),
         name="overlap",
     )(orbitals, cutoff_mask, channels, phase, wave)
-    overlap = sum_over(overlap, "gz", (1, 2, 3))
-    arrived, overlap = lax.optimization_barrier((arrived, overlap))
-    overlap = sum_over(overlap, "gy", (1, 2, 3))
+    arrived, strength, overlap = lax.optimization_barrier((arrived, strength, overlap))
 
     rows = planes * rows_y
-    band_spec = pl.BlockSpec((places, rows, 128), lambda i: (i, 0, 0))
-    density, folded = pl.pallas_call(
+    half = planes // 2 * length
+    mine, theirs, folded = pl.pallas_call(
         field_kernel,
         grid=(bands,),
         in_specs=[
-            band_spec,
+            pl.BlockSpec((places, rows, 128), lambda i: (i, 0, 0)),
             whole(planes, length, length),
+            whole(2 * atoms, 128),
             whole(4 * length, 4 * length),
             whole(2 * length, 2 * length),
             whole(4 * length, 4 * length),
             whole(2 * length, 2 * length),
         ],
-        out_specs=[whole(planes * length, length), band_spec],
+        out_specs=[
+            whole(half, length),
+            whole(half, length),
+            pl.BlockSpec((places, rows + 2 * atoms, 128), lambda i: (i, 0, 0)),
+        ],
         out_shape=[
-            jax.ShapeDtypeStruct((planes * length, length), bf16),
-            jax.ShapeDtypeStruct((bands * places, rows, 128), bf16),
+            jax.ShapeDtypeStruct((half, length), bf16),
+            jax.ShapeDtypeStruct((half, length), bf16),
+            jax.ShapeDtypeStruct((bands * places, rows + 2 * atoms, 128), bf16),
         ],
         scratch_shapes=[pltpu.VMEM((planes * length, length), f32)],
         compiler_params=params,
         cost_estimate=cost(6),
         name="field",
-    )(arrived.reshape(bands * places, rows, 128), potential_part, inv_z, inv_y, fwd_z, fwd_y)
-    returned = exchange(folded.reshape(chunk_shape))
-
-    base = pl.pallas_call(
-        base_kernel,
+    )(arrived.reshape(bands * places, rows, 128), potential_part, overlap, inv_z, inv_y, fwd_z, fwd_y)
+    returned = exchange(folded)
+
+    upper = lax.axis_index("band") // bands % 2
+    near = lax.ppermute(theirs, "band", partners("band", bands))
+    mine = (mine.astype(f32) + near.astype(f32)).astype(bf16)
+    for distance in (2, 6):
+        if distance < outer:
+            got = lax.ppermute(mine, "band", partners("band", distance * bands))
+            mine = (mine.astype(f32) + got.astype(f32)).astype(bf16)
+    near = lax.ppermute(mine, "band", partners("band", bands))
+    mine = jnp.where(upper == 0, jnp.stack([mine, near]), jnp.stack([near, mine]))
+    other = lax.ppermute(mine, "band", partners("band", 1))
+    applied = pl.pallas_call(
+        apply_kernel,
         grid=(steps,),
         in_specs=[
-            smem_spec,
-            whole(atoms, 128),
+            pl.BlockSpec((bands * places, planes * span, 128), lambda i: (0, i, 0)),
+            pl.BlockSpec((bands * places, 2 * atoms, 128), lambda i: (0, rows // (2 * atoms), 0)),
             orbitals_spec,
             mask_spec,
             channels_spec,
             phase_spec,
             whole(2 * atoms, length),
             whole(atoms, 128),
+            smem_spec,
+            whole(length, 4 * length),
         ],
         out_specs=orbitals_spec,
-        out_shape=jax.ShapeDtypeStruct(orbitals.shape, f32),
-        scratch_shapes=[pltpu.VMEM((2 * atoms, kinds * 4 * length), bf16)],
-        compiler_params=params,
-        cost_estimate=cost(0.1),
-        name="base",
-    )(
-        jnp.stack([first_y, first_z]).astype(jnp.int32),
-        overlap,
-        orbitals,
-        cutoff_mask,
-        channels,
-        phase,
-        wave,
-        strength,
-    )
-    half = planes // 2 * length
-    upper = lax.axis_index("band") // bands % 2
-    mine = lax.dynamic_slice_in_dim(density, upper * half, half, 0)
-    theirs = lax.dynamic_slice_in_dim(density, (1 - upper) * half, half, 0)
-    near = lax.ppermute(theirs, "band", partners("band", bands))
-    mine = (mine.astype(f32) + near.astype(f32)).astype(bf16)
-    far = [lax.ppermute(mine, "band", partners("band", d * bands)) for d in (2, 4, 6) if d < outer]
-    far, base = lax.optimization_barrier((far, base))
-    if far:
-        far = [part.astype(f32) for part in far]
-        mine = ((mine.astype(f32) + far[0]) + (far[1] + far[2])).astype(bf16)
-    copies = [lax.ppermute(mine, "band", partners("band", d)) for d in (1, 2, 3)]
-    applied = pl.pallas_call(
-        apply_kernel,
-        grid=(steps,),
-        in_specs=[chunks_spec, orbitals_spec, mask_spec, smem_spec, whole(length, 4 * length)],
-        out_specs=orbitals_spec,
         out_shape=jax.ShapeDtypeStruct(orbitals.shape, bf16),
-        scratch_shapes=[pltpu.VMEM((length * span, 128), f32)],
+        scratch_shapes=[
+            pltpu.VMEM((2 * atoms, kinds * 4 * length), bf16),
+            pltpu.VMEM((length * span, 128), f32),
+        ],
         compiler_params=params,
         cost_estimate=cost(4),
         name="apply",
-    )(returned, base, cutoff_mask, occupations, fwd_x)
-    copies, applied = lax.optimization_barrier((copies, applied))
-    odd, high = band != 0, upper != 0
-    pieces = [mine] + copies
-    pieces = [jnp.where(odd, pieces[j ^ 1], pieces[j]) for j in range(4)]
-    pieces = [jnp.where(high, pieces[j ^ 2], pieces[j]) for j in range(4)]
-    density = jnp.concatenate([pieces[0], pieces[2], pieces[1], pieces[3]], axis=0)
+    )(returned, returned, orbitals, cutoff_mask, channels, phase, wave, strength, occupations, fwd_x)
+    other, applied = lax.optimization_barrier((other, applied))
+    density = jnp.where(band == 0, jnp.stack([mine, other]), jnp.stack([other, mine]))
     return (applied, density.astype(f32).reshape(potential.shape))
 
 

time: 72 us -> 69.5 us (0.965)
  waiting for transfers between devices: 11.1 us -> 20.4 us
  starting transfers between devices: 33.8 us -> 26.4 us
  Pallas kernels: 18.9 us -> 16.9 us
  other arithmetic: 3.89 us -> 2.05 us
    all_to_all x2, waiting for transfers between devices: 1.7 us -> 10.8 us  [exchange(): lax.all_to_all(chunks, ('band', 'gy', 'gz'), split_axis=0, concat_axis=0,...]
    ppermute x12 -> x4, starting transfers between devices: 21.2 us -> 13.9 us  [the longest x2 10.4 us: shards(): got = lax.ppermute(mine, 'band', partners('band', distance * bands))]
    pallas_call x3 -> x2, Pallas kernels: 12.7 us -> 10.7 us  [the longest x1 5.89 us: shards(): pl.pallas_call(apply_kernel, grid=(steps,), in_specs=[pl.BlockSpec((bands...]
    ppermute x12 -> x4, waiting for transfers between devices: 7.72 us -> 9.6 us  [the longest x2 5.38 us: shards(): got = lax.ppermute(mine, 'band', partners('band', distance * bands))]
    ppermute x1, waiting for transfers between devices: 1.7 us -> 0.01 us  [shards(): near = lax.ppermute(theirs, 'band', partners('band', bands))]
    add x2 -> x0, other arithmetic: 1.28 us -> none  [sum_over(): return part.astype(f32) + got[0] + (got[1] + got[2])]
  transfers between devices with their start and end apart: 15 -> 7, of which waited for: 7 -> 4; matrix products, arithmetic and copies ran while one was open for 7% -> 4% of each run, Pallas kernels for 15% -> 13%
where the time goes in v5:
time: 69.5 us; the launch traced here: 68.9 us
  starting transfers between devices  26.4 us (38%)
  waiting for transfers between devices  20.4 us (29%)
  Pallas kernels  16.9 us (24%)
  local copies, waits for them, and re-layouts  2.3 us (3%)
  other arithmetic  2.05 us (3%)
  between operations  0.87 us (1%)
    all_to_all x2, starting transfers between devices, exchange(): lax.all_to_all(chunks, ('band', 'gy', 'gz'), split_axis=0, concat_axis=0,...  12.4 us
    all_to_all x2, waiting for transfers between devices, exchange(): lax.all_to_all(chunks, ('band', 'gy', 'gz'), split_axis=0, concat_axis=0,...  10.8 us
    ppermute x2, starting transfers between devices, shards(): got = lax.ppermute(mine, 'band', partners('band', distance * bands))  10.4 us
    pallas_call x1, Pallas kernels, shards(): pl.pallas_call(apply_kernel, grid=(steps,), in_specs=[pl.BlockSpec((bands...  5.89 us
    ppermute x2, waiting for transfers between devices, shards(): got = lax.ppermute(mine, 'band', partners('band', distance * bands))  5.38 us
    pallas_call x1, Pallas kernels, shards(): pl.pallas_call(field_kernel, grid=(bands,), in_specs=[pl.BlockSpec((place...  4.81 us
    ppermute x1, waiting for transfers between devices, shards(): near = lax.ppermute(mine, 'band', partners('band', bands))  4.22 us
    pallas_call x1, Pallas kernels, shards(): pl.pallas_call(spread_kernel, grid=(steps,), in_specs=[orbitals_spec, mas...  3.4 us
  transfers between devices with their start and end apart: 7, of which 4 were waited for; matrix products, arithmetic and copies ran while one was open for 4% of the time, Pallas kernels for 13%

profile of v5, /device:TPU:32, one launch (start us, length us, event | category | flops | bytes accessed | tf_op | source)
XLA Modules:
  0.0 68.9 jit_solution(9849569550430304477)
XLA Ops:
  0.6 3.4 %spread.1 = bf16[32,4,32,128]{3,2,1,0:T(8,128)(2,1)} custom-call(bf16[2,32,32,256]{3,2,1,0:T(8,128)(2,1)} %orbitals_ref.5, s32[32,32,128]{2,1,0:T(8,128)} %mask_ref.5, f32[2]{0:T(128)} %weight_ref.3, bf16[256,256]{1,0:T(8,128)(2,1)} %constant.74.clone.table_ref), custom_call_target="tpu_custom_call" | custom-call | flops 4000000000 | bytes 4000000 | tf_op jit(solution)/shard_map/spread/pallas_call | solution.py:332
  4.1 7.6 %all-to-all-start = ((bf16[32,4,32,128]{3,2,1,0:T(8,128)(2,1)}), bf16[32,4,32,128]{3,2,1,0:T(8,128)(2,1)}, u32[]{:S(2)}, u32[]{:S(2)}) async-start(bf16[32,4,32,128]{3,2,1,0:T(8,128)(2,1)} %spread.1), calls=%async_computation | async-start | bytes 2097152 | tf_op jit(solution)/shard_map/all_to_all | solution.py:328
  12.0 0.1 fusion.3
  12.1 0.1 add_convert_fusion.3
  12.2 0.1 add.70
  12.4 0.1 sub.25
  12.5 0.6 pad.4.strength_ref
  13.1 0.1 fusion.1
  13.2 0.6 pad_maximum_fusion.wave_ref
  13.8 0.6 copy-done.1
  14.4 2.8 %overlap.1.overlap_ref = bf16[16,128]{1,0:T(8,128)(2,1)} custom-call(bf16[2,32,32,256]{3,2,1,0:T(8,128)(2,1)} %orbitals_ref.5, s32[32,32,128]{2,1,0:T(8,128)} %mask_ref.5, bf16[4,32,32,128]{3,2,1,0:T(8,128)(2,1)} %channels_ref.3, bf16[16,1024]{1,0:T(8,128)(2,1)} %copy-done.1, f32[16,128]{1,0:T(8,128)} %pad_maximum_fusion.wave_ref), custom_call_target="tpu_custom_call" | custom-call | flops 100000000 | bytes 100000 | tf_op jit(solution)/shard_map/overlap/pallas_call | solution.py:361
  17.2 0.7 %constant_dynamic-slice_fusion.potential_ref = f32[4,128,128]{2,1,0:T(8,128)} fusion(f32[8,128,128]{2,1,0:T(8,128)S(1)} %copy-done, s32[]{:T(128)S(6)} %select_n.82), kind=kLoop, calls=%fused_computation.32 | loop fusion | bytes 524292 | tf_op jit(solution)/shard_map/dynamic_slice | solution.py:343
  18.0 10.8 %all-to-all-done = bf16[32,4,32,128]{3,2,1,0:T(8,128)(2,1)} async-done(((bf16[32,4,32,128]{3,2,1,0:T(8,128)(2,1)}), bf16[32,4,32,128]{3,2,1,0:T(8,128)(2,1)}, u32[]{:S(2)}, u32[]{:S(2)}) %all-to-all-start) | async-done | bytes 1048608 | tf_op jit(solution)/shard_map/all_to_all | solution.py:328
  28.8 4.8 %field.1 = (bf16[256,128]{1,0:T(8,128)(2,1)}, bf16[256,128]{1,0:T(8,128)(2,1)}, bf16[32,144,128]{2,1,0:T(8,128)(2,1)}) custom-call(bf16[32,128,128]{2,1,0:T(8,128)(2,1)} %bitcast.4.arrived_ref, f32[4,128,128]{2,1,0:T(8,128)} %constant_dynamic-slice_fusion.potential_ref, bf16[16,128]{1,0:T(8,128)(2,1)} %overlap.1.overlap_ref, ...), custom_call_target="tpu_custom_call" | custom-call | flops 6000000000 | bytes 6000000 | tf_op jit(solution)/shard_map/field/pallas_call | solution.py:376
  33.6 0.1 collective-permute-start
  33.7 4.8 %all-to-all-start.1 = ((bf16[32,144,128]{2,1,0:T(8,128)(2,1)}), bf16[32,144,128]{2,1,0:T(8,128)(2,1)}, u32[]{:S(2)}, u32[]{:S(2)}) async-start(bf16[32,144,128]{2,1,0:T(8,128)(2,1)} %get-tuple-element.18), calls=%async_computation.1 | async-start | bytes 2359296 | tf_op jit(solution)/shard_map/all_to_all | solution.py:328
  38.6 3.4 %collective-permute-start.1 = (bf16[256,128]{1,0:T(8,128)(2,1)S(1)}, bf16[256,128]{1,0:T(8,128)(2,1)S(1)}, u32[]{:S(2)}, u32[]{:S(2)}) collective-permute-start(bf16[256,128]{1,0:T(8,128)(2,1)S(1)} %add_convert_fusion.2), channel_id=1, source_target_pairs={{0,64},{16,80},{32,96},{48,112},{64,0},{80,16},{96,32},{112,48},{1... | collective-permute-start | bytes 196616 | tf_op jit(solution)/shard_map/ppermute | solution.py:410
  41.9 2.5 %collective-permute-done.1 = bf16[256,128]{1,0:T(8,128)(2,1)S(1)} collective-permute-done((bf16[256,128]{1,0:T(8,128)(2,1)S(1)}, bf16[256,128]{1,0:T(8,128)(2,1)S(1)}, u32[]{:S(2)}, u32[]{:S(2)}) %collective-permute-start.1) | collective-permute-done | bytes 65568 | tf_op jit(solution)/shard_map/ppermute | solution.py:410
  44.4 7.1 %collective-permute-start.2 = (bf16[256,128]{1,0:T(8,128)(2,1)S(1)}, bf16[256,128]{1,0:T(8,128)(2,1)S(1)}, u32[]{:S(2)}, u32[]{:S(2)}) collective-permute-start(bf16[256,128]{1,0:T(8,128)(2,1)S(1)} %add_convert_fusion.1), channel_id=1, source_target_pairs={{0,192},{16,208},{32,224},{48,240},{64,128},{80,144},{96,160},{112... | collective-permute-start | bytes 196616 | tf_op jit(solution)/shard_map/ppermute | solution.py:410
  51.5 2.9 %collective-permute-done.2 = bf16[256,128]{1,0:T(8,128)(2,1)S(1)} collective-permute-done((bf16[256,128]{1,0:T(8,128)(2,1)S(1)}, bf16[256,128]{1,0:T(8,128)(2,1)S(1)}, u32[]{:S(2)}, u32[]{:S(2)}) %collective-permute-start.2) | collective-permute-done | bytes 65568 | tf_op jit(solution)/shard_map/ppermute | solution.py:410
  54.6 4.2 %collective-permute-done.3 = bf16[256,128]{1,0:T(8,128)(2,1)S(1)} collective-permute-done((bf16[256,128]{1,0:T(8,128)(2,1)S(1)}, bf16[256,128]{1,0:T(8,128)(2,1)S(1)}, u32[]{:S(2)}, u32[]{:S(2)}) %collective-permute-start.3) | collective-permute-done | bytes 65568 | tf_op jit(solution)/shard_map/ppermute | solution.py:412
  58.8 3.4 %collective-permute-start.4 = (bf16[2,256,128]{2,1,0:T(8,128)(2,1)S(1)}, bf16[2,256,128]{2,1,0:T(8,128)(2,1)S(1)}, u32[]{:S(2)}, u32[]{:S(2)}) collective-permute-start(bf16[2,256,128]{2,1,0:T(8,128)(2,1)S(1)} %maximum_select_fusion.1), channel_id=1, source_target_pairs={{0,16},{16,0},{32,48},{48,32},{64,80},{80,64},{96,112},{112,96},{1... | collective-permute-start | bytes 393224 | tf_op jit(solution)/shard_map/ppermute | solution.py:414
  62.2 5.9 %apply.1 = bf16[2,32,32,256]{3,2,1,0:T(8,128)(2,1)} custom-call(bf16[32,144,128]{2,1,0:T(8,128)(2,1)} %all-to-all-done.1.returned_ref.overlap_ref, bf16[32,144,128]{2,1,0:T(8,128)(2,1)} %all-to-all-done.1.returned_ref.overlap_ref, bf16[2,32,32,256]{3,2,1,0:T(8,128)(2,1)} %orbitals_ref.5, s32[32,32,128]{2,1,0:T(8,128)} %mask_ref.5, ...), custom_call_target="tpu_custom_call" | custom-call | flops 4000000000 | bytes 4000000 | tf_op jit(solution)/shard_map/apply/pallas_call | solution.py:415
  68.1 0.8 %convert.11 = f32[8,128,128]{2,1,0:T(8,128)} convert(bf16[8,128,128]{2,1,0:T(8,128)(2,1)S(1)} %bitcast.15) | non-fusion elementwise | flops 131072 | bytes 786432 | tf_op jit(solution)/shard_map/convert_element_type | solution.py:442
  (34 shorter events, 0.5 us)
Async XLA Ops:
  0.6 16.6 %copy-start = (f32[8,128,128]{2,1,0:T(8,128)S(1)}, f32[8,128,128]{2,1,0:T(8,128)}, u32[]{:S(2)}) copy-start(f32[8,128,128]{2,1,0:T(8,128)} %param.16) | copy-start | bytes 1572868
  4.0 7.7 %copy-start.5 = (s32[32]{0:T(128)S(1)}, s32[32]{0:T(128)}, u32[]{:S(2)}) copy-start(s32[32]{0:T(128)} %param.21) | copy-start | bytes 388
  4.0 7.7 %copy-start.6 = (s32[32]{0:T(128)S(1)}, s32[32]{0:T(128)}, u32[]{:S(2)}) copy-start(s32[32]{0:T(128)} %param.20) | copy-start | bytes 388
  4.1 7.7 %copy-start.4 = (f32[32]{0:T(128)S(1)}, f32[32]{0:T(128)}, u32[]{:S(2)}) copy-start(f32[32]{0:T(128)} %param.22) | copy-start | bytes 388
  4.1 7.9 %copy-start.3 = (f32[8,3]{0,1:T(4,128)S(1)}, f32[8,3]{0,1:T(4,128)}, u32[]{:S(2)}) copy-start(f32[8,3]{0,1:T(4,128)} %param.19) | copy-start | bytes 292
  4.1 24.7 %all-to-all-start = ((bf16[32,4,32,128]{3,2,1,0:T(8,128)(2,1)}), bf16[32,4,32,128]{3,2,1,0:T(8,128)(2,1)}, u32[]{:S(2)}, u32[]{:S(2)}) async-start(bf16[32,4,32,128]{3,2,1,0:T(8,128)(2,1)} %spread.1), calls=%async_computation | async-start | bytes 2097152 | tf_op jit(solution)/shard_map/all_to_all | solution.py:328
  13.8 0.6 copy-start.1
  33.6 4.9 %collective-permute-start = (bf16[256,128]{1,0:T(8,128)(2,1)}, bf16[256,128]{1,0:T(8,128)(2,1)S(1)}, u32[]{:S(2)}, u32[]{:S(2)}) collective-permute-start(bf16[256,128]{1,0:T(8,128)(2,1)} %get-tuple-element.17), channel_id=1, source_target_pairs={{0,32},{16,48},{32,0},{48,16},{64,96},{80,112},{96,64},{112,80},{1... | collective-permute-start | bytes 196616 | tf_op jit(solution)/shard_map/ppermute | solution.py:406
  33.7 4.8 %copy-start.2 = (bf16[256,128]{1,0:T(8,128)(2,1)S(1)}, bf16[256,128]{1,0:T(8,128)(2,1)}, u32[]{:S(2)}) copy-start(bf16[256,128]{1,0:T(8,128)(2,1)} %get-tuple-element.16) | copy-start | bytes 196612
  33.7 28.5 %all-to-all-start.1 = ((bf16[32,144,128]{2,1,0:T(8,128)(2,1)}), bf16[32,144,128]{2,1,0:T(8,128)(2,1)}, u32[]{:S(2)}, u32[]{:S(2)}) async-start(bf16[32,144,128]{2,1,0:T(8,128)(2,1)} %get-tuple-element.18), calls=%async_computation.1 | async-start | bytes 2359296 | tf_op jit(solution)/shard_map/all_to_all | solution.py:328
  38.6 5.8 %collective-permute-start.1 = (bf16[256,128]{1,0:T(8,128)(2,1)S(1)}, bf16[256,128]{1,0:T(8,128)(2,1)S(1)}, u32[]{:S(2)}, u32[]{:S(2)}) collective-permute-start(bf16[256,128]{1,0:T(8,128)(2,1)S(1)} %add_convert_fusion.2), channel_id=1, source_target_pairs={{0,64},{16,80},{32,96},{48,112},{64,0},{80,16},{96,32},{112,48},{1... | collective-permute-start | bytes 196616 | tf_op jit(solution)/shard_map/ppermute | solution.py:410
  44.4 10.0 %collective-permute-start.2 = (bf16[256,128]{1,0:T(8,128)(2,1)S(1)}, bf16[256,128]{1,0:T(8,128)(2,1)S(1)}, u32[]{:S(2)}, u32[]{:S(2)}) collective-permute-start(bf16[256,128]{1,0:T(8,128)(2,1)S(1)} %add_convert_fusion.1), channel_id=1, source_target_pairs={{0,192},{16,208},{32,224},{48,240},{64,128},{80,144},{96,160},{112... | collective-permute-start | bytes 196616 | tf_op jit(solution)/shard_map/ppermute | solution.py:410
  54.4 4.4 %collective-permute-start.3 = (bf16[256,128]{1,0:T(8,128)(2,1)S(1)}, bf16[256,128]{1,0:T(8,128)(2,1)S(1)}, u32[]{:S(2)}, u32[]{:S(2)}) collective-permute-start(bf16[256,128]{1,0:T(8,128)(2,1)S(1)} %add_convert_fusion), channel_id=1, source_target_pairs={{0,32},{16,48},{32,0},{48,16},{64,96},{80,112},{96,64},{112,80},{1... | collective-permute-start | bytes 196616 | tf_op jit(solution)/shard_map/ppermute | solution.py:412
  58.8 9.3 %collective-permute-start.4 = (bf16[2,256,128]{2,1,0:T(8,128)(2,1)S(1)}, bf16[2,256,128]{2,1,0:T(8,128)(2,1)S(1)}, u32[]{:S(2)}, u32[]{:S(2)}) collective-permute-start(bf16[2,256,128]{2,1,0:T(8,128)(2,1)S(1)} %maximum_select_fusion.1), channel_id=1, source_target_pairs={{0,16},{16,0},{32,48},{48,32},{64,80},{80,64},{96,112},{112,96},{1... | collective-permute-start | bytes 393224 | tf_op jit(solution)/shard_map/ppermute | solution.py:414

commit v6 on v5

--- a/solution.py
+++ b/solution.py
@@ -260,6 +260,15 @@
                 out_ref[n, y, :, cols] = jnp.where(inside[y], total, 0.0).astype(bf16)
 
 
+def strength_kernel(atom_ref, kind_ref, coupling_ref, out_ref):
+    row = lax.broadcasted_iota(jnp.int32, out_ref.shape, 0)
+    kind = lax.broadcasted_iota(jnp.int32, out_ref.shape, 1) // 4
+    total = jnp.zeros(out_ref.shape, f32)
+    for p in range(coupling_ref.shape[0]):
+        total += jnp.where((row == atom_ref[p]) & (kind == kind_ref[p]), coupling_ref[p], 0.0)
+    out_ref[...] = total
+
+
 def partners(axis, distance):
     return [(i, i ^ distance) for i in range(lax.axis_size(axis))]
 
@@ -352,12 +361,6 @@
     sin_yz = sin_y[:, :, None] * cos_z[:, None, :] + cos_y[:, :, None] * sin_z[:, None, :]
     phase = jnp.concatenate([cos_yz, sin_yz], axis=0).astype(bf16).reshape(2 * atoms, rows_y * rows_z)
     wave = jnp.concatenate([cos_x, sin_x], axis=0)
-    chosen = (proj_atom[None, :] == jnp.arange(atoms, dtype=jnp.int32)[:, None])[:, None, :] & (
-        proj_chan[None, :] == jnp.arange(kinds, dtype=jnp.int32)[:, None]
-    )[None, :, :]
-    strength = jnp.sum(jnp.where(chosen, coupling[None, None, :], 0.0), axis=2)
-    strength = jnp.pad(jnp.repeat(strength, 4, axis=1), ((0, 0), (0, 128 - 4 * kinds)))
-
     overlap = pl.pallas_call(
         overlap_kernel,
         grid=(steps,),
@@ -369,7 +372,7 @@
         cost_estimate=cost(0.1),
         name="overlap",
     )(orbitals, cutoff_mask, channels, phase, wave)
-    arrived, strength, overlap = lax.optimization_barrier((arrived, strength, overlap))
+    arrived, overlap = lax.optimization_barrier((arrived, overlap))
 
     rows = planes * rows_y
     half = planes // 2 * length
@@ -400,18 +403,24 @@
         cost_estimate=cost(6),
         name="field",
     )(arrived.reshape(bands * places, rows, 128), potential_part, overlap, inv_z, inv_y, fwd_z, fwd_y)
+    folded, coupling = lax.optimization_barrier((folded, coupling))
+    strength = pl.pallas_call(
+        strength_kernel,
+        in_specs=[smem_spec] * 3,
+        out_shape=jax.ShapeDtypeStruct((atoms, 128), f32),
+        compiler_params=params,
+        cost_estimate=cost(5),
+        name="strength",
+    )(proj_atom, proj_chan, coupling)
     returned = exchange(folded)
 
-    upper = lax.axis_index("band") // bands % 2
     near = lax.ppermute(theirs, "band", partners("band", bands))
     mine = (mine.astype(f32) + near.astype(f32)).astype(bf16)
     for distance in (2, 6):
         if distance < outer:
             got = lax.ppermute(mine, "band", partners("band", distance * bands))
             mine = (mine.astype(f32) + got.astype(f32)).astype(bf16)
-    near = lax.ppermute(mine, "band", partners("band", bands))
-    mine = jnp.where(upper == 0, jnp.stack([mine, near]), jnp.stack([near, mine]))
-    other = lax.ppermute(mine, "band", partners("band", 1))
+    copies = [lax.ppermute(mine, "band", partners("band", d)) for d in (1, 2, 3)]
     applied = pl.pallas_call(
         apply_kernel,
         grid=(steps,),
@@ -437,8 +446,12 @@
         cost_estimate=cost(4),
         name="apply",
     )(returned, returned, orbitals, cutoff_mask, channels, phase, wave, strength, occupations, fwd_x)
-    other, applied = lax.optimization_barrier((other, applied))
-    density = jnp.where(band == 0, jnp.stack([mine, other]), jnp.stack([other, mine]))
+    copies, applied = lax.optimization_barrier((copies, applied))
+    place = lax.axis_index("band") % 4
+    pieces = [mine] + copies
+    pieces = [jnp.where(place & 1 != 0, pieces[j ^ 1], pieces[j]) for j in range(4)]
+    pieces = [jnp.where(place & 2 != 0, pieces[j ^ 2], pieces[j]) for j in range(4)]
+    density = jnp.concatenate([pieces[0], pieces[2], pieces[1], pieces[3]], axis=0)
     return (applied, density.astype(f32).reshape(potential.shape))
 
 

time: 69.5 us -> 67.4 us (0.970)
  waiting for transfers between devices: 20.4 us -> 15.7 us
  starting transfers between devices: 26.4 us -> 28 us
  Pallas kernels: 16.9 us -> 18.2 us
  local copies, waits for them, and re-layouts: 2.3 us -> 1.6 us
    ppermute x2 -> x3, waiting for transfers between devices: 4.22 us -> 0.01 us  [shards(): lax.ppermute(mine, 'band', partners('band', d))]
    ppermute x2 -> x3, starting transfers between devices: 3.44 us -> 5.08 us  [shards(): lax.ppermute(mine, 'band', partners('band', d))]
    ppermute x2, waiting for transfers between devices: 5.38 us -> 4.07 us  [shards(): got = lax.ppermute(mine, 'band', partners('band', distance * bands))]
    pallas_call x0 -> x1, Pallas kernels: none -> 1.31 us  [shards(): pl.pallas_call(strength_kernel, in_specs=[smem_spec] * 3, out_shape=jax.S...]
    all_to_all x2, waiting for transfers between devices: 10.8 us -> 11.7 us  [exchange(): lax.all_to_all(chunks, ('band', 'gy', 'gz'), split_axis=0, concat_axis=0,...]
  transfers between devices with their start and end apart: 7 -> 8, of which waited for: 4 -> 3; matrix products, arithmetic and copies ran while one was open for 4% -> 3% of each run, Pallas kernels for 13% -> 15%
where the time goes in v6:
time: 67.4 us; the launch traced here: 66.2 us
  starting transfers between devices  28 us (42%)
  Pallas kernels  18.2 us (27%)
  waiting for transfers between devices  15.7 us (23%)
  other arithmetic  1.94 us (3%)
  local copies, waits for them, and re-layouts  1.6 us (2%)
  between operations  0.8 us (1%)
    all_to_all x2, starting transfers between devices, exchange(): lax.all_to_all(chunks, ('band', 'gy', 'gz'), split_axis=0, concat_axis=0,...  12.4 us
    all_to_all x2, waiting for transfers between devices, exchange(): lax.all_to_all(chunks, ('band', 'gy', 'gz'), split_axis=0, concat_axis=0,...  11.7 us
    ppermute x2, starting transfers between devices, shards(): got = lax.ppermute(mine, 'band', partners('band', distance * bands))  10.4 us
    pallas_call x1, Pallas kernels, shards(): pl.pallas_call(apply_kernel, grid=(steps,), in_specs=[pl.BlockSpec((bands...  5.86 us
    ppermute x3, starting transfers between devices, shards(): lax.ppermute(mine, 'band', partners('band', d))  5.08 us
    pallas_call x1, Pallas kernels, shards(): pl.pallas_call(field_kernel, grid=(bands,), in_specs=[pl.BlockSpec((place...  4.82 us
    ppermute x2, waiting for transfers between devices, shards(): got = lax.ppermute(mine, 'band', partners('band', distance * bands))  4.07 us
    pallas_call x1, Pallas kernels, shards(): pl.pallas_call(spread_kernel, grid=(steps,), in_specs=[orbitals_spec, mas...  3.4 us
  transfers between devices with their start and end apart: 8, of which 3 were waited for; matrix products, arithmetic and copies ran while one was open for 3% of the time, Pallas kernels for 15%

profile of v6, /device:TPU:32, one launch (start us, length us, event | category | flops | bytes accessed | tf_op | source)
XLA Modules:
  0.0 66.2 jit_solution(11778919228211955055)
XLA Ops:
  0.6 3.4 %spread.1 = bf16[32,4,32,128]{3,2,1,0:T(8,128)(2,1)} custom-call(bf16[2,32,32,256]{3,2,1,0:T(8,128)(2,1)} %orbitals_ref.5, s32[32,32,128]{2,1,0:T(8,128)} %mask_ref.5, f32[2]{0:T(128)} %weight_ref.3, bf16[256,256]{1,0:T(8,128)(2,1)} %constant.65.clone.table_ref), custom_call_target="tpu_custom_call" | custom-call | flops 4000000000 | bytes 4000000 | tf_op jit(solution)/shard_map/spread/pallas_call | solution.py:341
  4.0 7.6 %all-to-all-start = ((bf16[32,4,32,128]{3,2,1,0:T(8,128)(2,1)}), bf16[32,4,32,128]{3,2,1,0:T(8,128)(2,1)}, u32[]{:S(2)}, u32[]{:S(2)}) async-start(bf16[32,4,32,128]{3,2,1,0:T(8,128)(2,1)} %spread.1), calls=%async_computation | async-start | bytes 2097152 | tf_op jit(solution)/shard_map/all_to_all | solution.py:337
  11.7 0.1 fusion.3
  11.8 0.1 add_convert_fusion.3
  12.0 0.1 add.66
  12.1 0.1 sub.20
  12.3 0.6 pad_maximum_fusion.1.wave_ref
  13.0 0.6 copy-done.1
  13.6 2.8 %overlap.1.overlap_ref = bf16[16,128]{1,0:T(8,128)(2,1)} custom-call(bf16[2,32,32,256]{3,2,1,0:T(8,128)(2,1)} %orbitals_ref.5, s32[32,32,128]{2,1,0:T(8,128)} %mask_ref.5, bf16[4,32,32,128]{3,2,1,0:T(8,128)(2,1)} %channels_ref.3, bf16[16,1024]{1,0:T(8,128)(2,1)} %copy-done.1, f32[16,128]{1,0:T(8,128)} %pad_maximum_fusion.1.wave_ref), custom_call_target="tpu_custom_call" | custom-call | flops 100000000 | bytes 100000 | tf_op jit(solution)/shard_map/overlap/pallas_call | solution.py:364
  16.4 0.7 %constant_dynamic-slice_fusion.potential_ref = f32[4,128,128]{2,1,0:T(8,128)} fusion(f32[8,128,128]{2,1,0:T(8,128)S(1)} %copy-done, s32[]{:T(128)S(6)} %select_n.79), kind=kLoop, calls=%fused_computation.35 | loop fusion | bytes 524292 | tf_op jit(solution)/shard_map/dynamic_slice | solution.py:352
  17.1 11.6 %all-to-all-done = bf16[32,4,32,128]{3,2,1,0:T(8,128)(2,1)} async-done(((bf16[32,4,32,128]{3,2,1,0:T(8,128)(2,1)}), bf16[32,4,32,128]{3,2,1,0:T(8,128)(2,1)}, u32[]{:S(2)}, u32[]{:S(2)}) %all-to-all-start) | async-done | bytes 1048608 | tf_op jit(solution)/shard_map/all_to_all | solution.py:337
  28.7 4.8 %field.1 = (bf16[256,128]{1,0:T(8,128)(2,1)}, bf16[256,128]{1,0:T(8,128)(2,1)}, bf16[32,144,128]{2,1,0:T(8,128)(2,1)}) custom-call(bf16[32,128,128]{2,1,0:T(8,128)(2,1)} %bitcast.3.arrived_ref, f32[4,128,128]{2,1,0:T(8,128)} %constant_dynamic-slice_fusion.potential_ref, bf16[16,128]{1,0:T(8,128)(2,1)} %overlap.1.overlap_ref, ...), custom_call_target="tpu_custom_call" | custom-call | flops 6000000000 | bytes 6000000 | tf_op jit(solution)/shard_map/field/pallas_call | solution.py:379
  33.6 0.1 collective-permute-start
  33.7 4.8 %all-to-all-start.1 = ((bf16[32,144,128]{2,1,0:T(8,128)(2,1)}), bf16[32,144,128]{2,1,0:T(8,128)(2,1)}, u32[]{:S(2)}, u32[]{:S(2)}) async-start(bf16[32,144,128]{2,1,0:T(8,128)(2,1)} %get-tuple-element.22), calls=%async_computation.1 | async-start | bytes 2359296 | tf_op jit(solution)/shard_map/all_to_all | solution.py:337
  38.5 3.4 %collective-permute-start.1 = (bf16[256,128]{1,0:T(8,128)(2,1)S(1)}, bf16[256,128]{1,0:T(8,128)(2,1)S(1)}, u32[]{:S(2)}, u32[]{:S(2)}) collective-permute-start(bf16[256,128]{1,0:T(8,128)(2,1)S(1)} %add_convert_fusion.2), channel_id=1, source_target_pairs={{0,64},{16,80},{32,96},{48,112},{64,0},{80,16},{96,32},{112,48},{1... | collective-permute-start | bytes 196616 | tf_op jit(solution)/shard_map/ppermute | solution.py:421
  41.9 2.5 %collective-permute-done.1 = bf16[256,128]{1,0:T(8,128)(2,1)S(1)} collective-permute-done((bf16[256,128]{1,0:T(8,128)(2,1)S(1)}, bf16[256,128]{1,0:T(8,128)(2,1)S(1)}, u32[]{:S(2)}, u32[]{:S(2)}) %collective-permute-start.1) | collective-permute-done | bytes 65568 | tf_op jit(solution)/shard_map/ppermute | solution.py:421
  44.4 7.1 %collective-permute-start.2 = (bf16[256,128]{1,0:T(8,128)(2,1)S(1)}, bf16[256,128]{1,0:T(8,128)(2,1)S(1)}, u32[]{:S(2)}, u32[]{:S(2)}) collective-permute-start(bf16[256,128]{1,0:T(8,128)(2,1)S(1)} %add_convert_fusion.1), channel_id=1, source_target_pairs={{0,192},{16,208},{32,224},{48,240},{64,128},{80,144},{96,160},{112... | collective-permute-start | bytes 196616 | tf_op jit(solution)/shard_map/ppermute | solution.py:421
  51.4 1.3 %strength.1.strength_ref = f32[8,128]{1,0:T(8,128)} custom-call(s32[32]{0:T(128)} %atom_ref.1, s32[32]{0:T(128)} %kind_ref.1, f32[32]{0:T(128)} %coupling_ref), custom_call_target="tpu_custom_call" | custom-call | flops 5000000000 | bytes 5000000 | tf_op jit(solution)/shard_map/strength/pallas_call | solution.py:407
  52.8 1.6 %collective-permute-done.2 = bf16[256,128]{1,0:T(8,128)(2,1)S(1)} collective-permute-done((bf16[256,128]{1,0:T(8,128)(2,1)S(1)}, bf16[256,128]{1,0:T(8,128)(2,1)S(1)}, u32[]{:S(2)}, u32[]{:S(2)}) %collective-permute-start.2) | collective-permute-done | bytes 65568 | tf_op jit(solution)/shard_map/ppermute | solution.py:421
  54.4 2.0 %collective-permute-start.5 = (bf16[256,128]{1,0:T(8,128)(2,1)S(1)}, bf16[256,128]{1,0:T(8,128)(2,1)S(1)}, u32[]{:S(2)}, u32[]{:S(2)}) collective-permute-start(bf16[256,128]{1,0:T(8,128)(2,1)S(1)} %add_convert_fusion), channel_id=1, source_target_pairs={{0,48},{16,32},{32,16},{48,0},{64,112},{80,96},{96,80},{112,64},{1... | collective-permute-start | bytes 196616 | tf_op jit(solution)/shard_map/ppermute | solution.py:423
  56.4 2.8 %collective-permute-start.4 = (bf16[256,128]{1,0:T(8,128)(2,1)S(1)}, bf16[256,128]{1,0:T(8,128)(2,1)S(1)}, u32[]{:S(2)}, u32[]{:S(2)}) collective-permute-start(bf16[256,128]{1,0:T(8,128)(2,1)S(1)} %add_convert_fusion), channel_id=1, source_target_pairs={{0,32},{16,48},{32,0},{48,16},{64,96},{80,112},{96,64},{112,80},{1... | collective-permute-start | bytes 196616 | tf_op jit(solution)/shard_map/ppermute | solution.py:423
  59.2 0.3 collective-permute-start.3
  59.5 5.9 %apply.1 = bf16[2,32,32,256]{3,2,1,0:T(8,128)(2,1)} custom-call(bf16[32,144,128]{2,1,0:T(8,128)(2,1)} %all-to-all-done.1.returned_ref.overlap_ref, bf16[32,144,128]{2,1,0:T(8,128)(2,1)} %all-to-all-done.1.returned_ref.overlap_ref, bf16[2,32,32,256]{3,2,1,0:T(8,128)(2,1)} %orbitals_ref.5, s32[32,32,128]{2,1,0:T(8,128)} %mask_ref.5, ...), custom_call_target="tpu_custom_call" | custom-call | flops 4000000000 | bytes 4000000 | tf_op jit(solution)/shard_map/apply/pallas_call | solution.py:424
  65.4 0.8 %convert.11 = f32[8,128,128]{2,1,0:T(8,128)} convert(bf16[8,128,128]{2,1,0:T(8,128)(2,1)S(1)} %bitcast.9) | non-fusion elementwise | flops 131072 | bytes 786432 | tf_op jit(solution)/shard_map/convert_element_type | solution.py:455
  (24 shorter events, 0.3 us)
Async XLA Ops:
  0.6 15.7 %copy-start = (f32[8,128,128]{2,1,0:T(8,128)S(1)}, f32[8,128,128]{2,1,0:T(8,128)}, u32[]{:S(2)}) copy-start(f32[8,128,128]{2,1,0:T(8,128)} %param.16) | copy-start | bytes 1572868
  4.0 7.6 %copy-start.3 = (f32[8,3]{0,1:T(4,128)S(1)}, f32[8,3]{0,1:T(4,128)}, u32[]{:S(2)}) copy-start(f32[8,3]{0,1:T(4,128)} %param.19) | copy-start | bytes 292
  4.0 24.7 %all-to-all-start = ((bf16[32,4,32,128]{3,2,1,0:T(8,128)(2,1)}), bf16[32,4,32,128]{3,2,1,0:T(8,128)(2,1)}, u32[]{:S(2)}, u32[]{:S(2)}) async-start(bf16[32,4,32,128]{3,2,1,0:T(8,128)(2,1)} %spread.1), calls=%async_computation | async-start | bytes 2097152 | tf_op jit(solution)/shard_map/all_to_all | solution.py:337
  13.0 0.6 copy-start.1
  33.6 4.9 %collective-permute-start = (bf16[256,128]{1,0:T(8,128)(2,1)}, bf16[256,128]{1,0:T(8,128)(2,1)S(1)}, u32[]{:S(2)}, u32[]{:S(2)}) collective-permute-start(bf16[256,128]{1,0:T(8,128)(2,1)} %get-tuple-element.20), channel_id=1, source_target_pairs={{0,32},{16,48},{32,0},{48,16},{64,96},{80,112},{96,64},{112,80},{1... | collective-permute-start | bytes 196616 | tf_op jit(solution)/shard_map/ppermute | solution.py:417
  33.7 4.8 %copy-start.2 = (bf16[256,128]{1,0:T(8,128)(2,1)S(1)}, bf16[256,128]{1,0:T(8,128)(2,1)}, u32[]{:S(2)}) copy-start(bf16[256,128]{1,0:T(8,128)(2,1)} %get-tuple-element.19) | copy-start | bytes 196612
  33.7 25.8 %all-to-all-start.1 = ((bf16[32,144,128]{2,1,0:T(8,128)(2,1)}), bf16[32,144,128]{2,1,0:T(8,128)(2,1)}, u32[]{:S(2)}, u32[]{:S(2)}) async-start(bf16[32,144,128]{2,1,0:T(8,128)(2,1)} %get-tuple-element.22), calls=%async_computation.1 | async-start | bytes 2359296 | tf_op jit(solution)/shard_map/all_to_all | solution.py:337
  38.5 5.8 %collective-permute-start.1 = (bf16[256,128]{1,0:T(8,128)(2,1)S(1)}, bf16[256,128]{1,0:T(8,128)(2,1)S(1)}, u32[]{:S(2)}, u32[]{:S(2)}) collective-permute-start(bf16[256,128]{1,0:T(8,128)(2,1)S(1)} %add_convert_fusion.2), channel_id=1, source_target_pairs={{0,64},{16,80},{32,96},{48,112},{64,0},{80,16},{96,32},{112,48},{1... | collective-permute-start | bytes 196616 | tf_op jit(solution)/shard_map/ppermute | solution.py:421
  44.4 10.0 %collective-permute-start.2 = (bf16[256,128]{1,0:T(8,128)(2,1)S(1)}, bf16[256,128]{1,0:T(8,128)(2,1)S(1)}, u32[]{:S(2)}, u32[]{:S(2)}) collective-permute-start(bf16[256,128]{1,0:T(8,128)(2,1)S(1)} %add_convert_fusion.1), channel_id=1, source_target_pairs={{0,192},{16,208},{32,224},{48,240},{64,128},{80,144},{96,160},{112... | collective-permute-start | bytes 196616 | tf_op jit(solution)/shard_map/ppermute | solution.py:421
  54.4 10.9 %collective-permute-start.5 = (bf16[256,128]{1,0:T(8,128)(2,1)S(1)}, bf16[256,128]{1,0:T(8,128)(2,1)S(1)}, u32[]{:S(2)}, u32[]{:S(2)}) collective-permute-start(bf16[256,128]{1,0:T(8,128)(2,1)S(1)} %add_convert_fusion), channel_id=1, source_target_pairs={{0,48},{16,32},{32,16},{48,0},{64,112},{80,96},{96,80},{112,64},{1... | collective-permute-start | bytes 196616 | tf_op jit(solution)/shard_map/ppermute | solution.py:423
  56.4 8.9 %collective-permute-start.4 = (bf16[256,128]{1,0:T(8,128)(2,1)S(1)}, bf16[256,128]{1,0:T(8,128)(2,1)S(1)}, u32[]{:S(2)}, u32[]{:S(2)}) collective-permute-start(bf16[256,128]{1,0:T(8,128)(2,1)S(1)} %add_convert_fusion), channel_id=1, source_target_pairs={{0,32},{16,48},{32,0},{48,16},{64,96},{80,112},{96,64},{112,80},{1... | collective-permute-start | bytes 196616 | tf_op jit(solution)/shard_map/ppermute | solution.py:423
  59.2 6.2 %collective-permute-start.3 = (bf16[256,128]{1,0:T(8,128)(2,1)S(1)}, bf16[256,128]{1,0:T(8,128)(2,1)S(1)}, u32[]{:S(2)}, u32[]{:S(2)}) collective-permute-start(bf16[256,128]{1,0:T(8,128)(2,1)S(1)} %add_convert_fusion), channel_id=1, source_target_pairs={{0,16},{16,0},{32,48},{48,32},{64,80},{80,64},{96,112},{112,96},{1... | collective-permute-start | bytes 196616 | tf_op jit(solution)/shard_map/ppermute | solution.py:423

commit v7 on v5

--- a/solution.py
+++ b/solution.py
@@ -260,6 +260,15 @@
                 out_ref[n, y, :, cols] = jnp.where(inside[y], total, 0.0).astype(bf16)
 
 
+def strength_kernel(atom_ref, kind_ref, coupling_ref, out_ref):
+    row = lax.broadcasted_iota(jnp.int32, out_ref.shape, 0)
+    kind = lax.broadcasted_iota(jnp.int32, out_ref.shape, 1) // 4
+    total = jnp.zeros(out_ref.shape, f32)
+    for p in range(coupling_ref.shape[0]):
+        total += jnp.where((row == atom_ref[p]) & (kind == kind_ref[p]), coupling_ref[p], 0.0)
+    out_ref[...] = total
+
+
 def partners(axis, distance):
     return [(i, i ^ distance) for i in range(lax.axis_size(axis))]
 
@@ -352,12 +361,15 @@
     sin_yz = sin_y[:, :, None] * cos_z[:, None, :] + cos_y[:, :, None] * sin_z[:, None, :]
     phase = jnp.concatenate([cos_yz, sin_yz], axis=0).astype(bf16).reshape(2 * atoms, rows_y * rows_z)
     wave = jnp.concatenate([cos_x, sin_x], axis=0)
-    chosen = (proj_atom[None, :] == jnp.arange(atoms, dtype=jnp.int32)[:, None])[:, None, :] & (
-        proj_chan[None, :] == jnp.arange(kinds, dtype=jnp.int32)[:, None]
-    )[None, :, :]
-    strength = jnp.sum(jnp.where(chosen, coupling[None, None, :], 0.0), axis=2)
-    strength = jnp.pad(jnp.repeat(strength, 4, axis=1), ((0, 0), (0, 128 - 4 * kinds)))
-
+    positions, coupling = lax.optimization_barrier((positions, coupling))
+    strength = pl.pallas_call(
+        strength_kernel,
+        in_specs=[smem_spec] * 3,
+        out_shape=jax.ShapeDtypeStruct((atoms, 128), f32),
+        compiler_params=params,
+        cost_estimate=cost(0.1),
+        name="strength",
+    )(proj_atom, proj_chan, coupling)
     overlap = pl.pallas_call(
         overlap_kernel,
         grid=(steps,),
@@ -369,7 +381,7 @@
         cost_estimate=cost(0.1),
         name="overlap",
     )(orbitals, cutoff_mask, channels, phase, wave)
-    arrived, strength, overlap = lax.optimization_barrier((arrived, strength, overlap))
+    arrived, overlap, strength = lax.optimization_barrier((arrived, overlap, strength))
 
     rows = planes * rows_y
     half = planes // 2 * length
@@ -402,14 +414,14 @@
     )(arrived.reshape(bands * places, rows, 128), potential_part, overlap, inv_z, inv_y, fwd_z, fwd_y)
     returned = exchange(folded)
 
-    upper = lax.axis_index("band") // bands % 2
     near = lax.ppermute(theirs, "band", partners("band", bands))
     mine = (mine.astype(f32) + near.astype(f32)).astype(bf16)
-    for distance in (2, 6):
-        if distance < outer:
-            got = lax.ppermute(mine, "band", partners("band", distance * bands))
-            mine = (mine.astype(f32) + got.astype(f32)).astype(bf16)
-    near = lax.ppermute(mine, "band", partners("band", bands))
+    got = lax.ppermute(mine, "band", partners("band", 2 * bands))
+    mine = (mine.astype(f32) + got.astype(f32)).astype(bf16)
+    far, near, both = [lax.ppermute(mine, "band", partners("band", d * bands)) for d in (6, 1, 7)]
+    mine = (mine.astype(f32) + far.astype(f32)).astype(bf16)
+    near = (near.astype(f32) + both.astype(f32)).astype(bf16)
+    upper = lax.axis_index("band") // bands % 2
     mine = jnp.where(upper == 0, jnp.stack([mine, near]), jnp.stack([near, mine]))
     other = lax.ppermute(mine, "band", partners("band", 1))
     applied = pl.pallas_call(

time: 69.5 us -> 69.3 us (level)
  Pallas kernels: 16.9 us -> 18.2 us
  waiting for transfers between devices: 20.4 us -> 19.4 us
    pallas_call x0 -> x1, Pallas kernels: none -> 1.31 us  [shards(): pl.pallas_call(strength_kernel, in_specs=[smem_spec] * 3, out_shape=jax.S...]
    ppermute x3 -> x4, starting transfers between devices: 10.5 us -> 11.1 us  [the longest x3 7.76 us: shards(): lax.ppermute(mine, 'band', partners('band', d * bands))]
    ppermute x3 -> x4, waiting for transfers between devices: 9.6 us -> 9.02 us  [the longest x3 6.55 us: shards(): lax.ppermute(mine, 'band', partners('band', d * bands))]
  transfers between devices with their start and end apart: 7 -> 8, of which waited for: 4 -> 4; matrix products, arithmetic and copies ran while one was open for 4% -> 3% of each run, Pallas kernels for 13% -> 14%
where the time goes in v7:
time: 69.3 us; the launch traced here: 68.9 us
  starting transfers between devices  26.9 us (39%)
  waiting for transfers between devices  19.4 us (28%)
  Pallas kernels  18.2 us (26%)
  other arithmetic  1.96 us (3%)
  local copies, waits for them, and re-layouts  1.61 us (2%)
  between operations  0.79 us (1%)
    all_to_all x2, starting transfers between devices, exchange(): lax.all_to_all(chunks, ('band', 'gy', 'gz'), split_axis=0, concat_axis=0,...  12.4 us
    all_to_all x2, waiting for transfers between devices, exchange(): lax.all_to_all(chunks, ('band', 'gy', 'gz'), split_axis=0, concat_axis=0,...  10.3 us
    ppermute x3, starting transfers between devices, shards(): lax.ppermute(mine, 'band', partners('band', d * bands))  7.76 us
    ppermute x3, waiting for transfers between devices, shards(): lax.ppermute(mine, 'band', partners('band', d * bands))  6.55 us
    pallas_call x1, Pallas kernels, shards(): pl.pallas_call(apply_kernel, grid=(steps,), in_specs=[pl.BlockSpec((bands...  5.86 us
    pallas_call x1, Pallas kernels, shards(): pl.pallas_call(field_kernel, grid=(bands,), in_specs=[pl.BlockSpec((place...  4.81 us
    pallas_call x1, Pallas kernels, shards(): pl.pallas_call(spread_kernel, grid=(steps,), in_specs=[orbitals_spec, mas...  3.4 us
    ppermute x1, starting transfers between devices, shards(): got = lax.ppermute(mine, 'band', partners('band', 2 * bands))  3.35 us
  transfers between devices with their start and end apart: 8, of which 4 were waited for; matrix products, arithmetic and copies ran while one was open for 3% of the time, Pallas kernels for 14%

profile of v7, /device:TPU:32, one launch (start us, length us, event | category | flops | bytes accessed | tf_op | source)
XLA Modules:
  0.0 68.9 jit_solution(13735246309193507030)
XLA Ops:
  0.6 3.4 %spread.1 = bf16[32,4,32,128]{3,2,1,0:T(8,128)(2,1)} custom-call(bf16[2,32,32,256]{3,2,1,0:T(8,128)(2,1)} %orbitals_ref.5, s32[32,32,128]{2,1,0:T(8,128)} %mask_ref.5, f32[2]{0:T(128)} %weight_ref.3, bf16[256,256]{1,0:T(8,128)(2,1)} %constant.71.clone.table_ref), custom_call_target="tpu_custom_call" | custom-call | flops 4000000000 | bytes 4000000 | tf_op jit(solution)/shard_map/spread/pallas_call | solution.py:341
  4.0 7.6 %all-to-all-start = ((bf16[32,4,32,128]{3,2,1,0:T(8,128)(2,1)}), bf16[32,4,32,128]{3,2,1,0:T(8,128)(2,1)}, u32[]{:S(2)}, u32[]{:S(2)}) async-start(bf16[32,4,32,128]{3,2,1,0:T(8,128)(2,1)} %spread.1), calls=%async_computation | async-start | bytes 2097152 | tf_op jit(solution)/shard_map/all_to_all | solution.py:337
  11.7 0.1 fusion.7
  11.8 0.1 add_convert_fusion.4
  12.0 0.1 add.71
  12.1 0.1 sub.25
  12.2 1.3 %strength.1.strength_ref = f32[8,128]{1,0:T(8,128)} custom-call(s32[32]{0:T(128)} %atom_ref.1, s32[32]{0:T(128)} %kind_ref.1, f32[32]{0:T(128)} %coupling_ref), custom_call_target="tpu_custom_call" | custom-call | flops 100000000 | bytes 100000 | tf_op jit(solution)/shard_map/strength/pallas_call | solution.py:365
  13.5 0.1 fusion.5
  13.7 0.6 pad_maximum_fusion.wave_ref
  14.3 0.6 copy-done.1
  14.9 2.8 %overlap.1.overlap_ref = bf16[16,128]{1,0:T(8,128)(2,1)} custom-call(bf16[2,32,32,256]{3,2,1,0:T(8,128)(2,1)} %orbitals_ref.5, s32[32,32,128]{2,1,0:T(8,128)} %mask_ref.5, bf16[4,32,32,128]{3,2,1,0:T(8,128)(2,1)} %channels_ref.3, bf16[16,1024]{1,0:T(8,128)(2,1)} %copy-done.1, f32[16,128]{1,0:T(8,128)} %pad_maximum_fusion.wave_ref), custom_call_target="tpu_custom_call" | custom-call | flops 100000000 | bytes 100000 | tf_op jit(solution)/shard_map/overlap/pallas_call | solution.py:373
  17.7 0.7 %constant_dynamic-slice_fusion.potential_ref = f32[4,128,128]{2,1,0:T(8,128)} fusion(f32[8,128,128]{2,1,0:T(8,128)S(1)} %copy-done, s32[]{:T(128)S(6)} %select_n.77), kind=kLoop, calls=%fused_computation.34 | loop fusion | bytes 524292 | tf_op jit(solution)/shard_map/dynamic_slice | solution.py:352
  18.4 10.3 %all-to-all-done = bf16[32,4,32,128]{3,2,1,0:T(8,128)(2,1)} async-done(((bf16[32,4,32,128]{3,2,1,0:T(8,128)(2,1)}), bf16[32,4,32,128]{3,2,1,0:T(8,128)(2,1)}, u32[]{:S(2)}, u32[]{:S(2)}) %all-to-all-start) | async-done | bytes 1048608 | tf_op jit(solution)/shard_map/all_to_all | solution.py:337
  28.7 4.8 %field.1 = (bf16[256,128]{1,0:T(8,128)(2,1)}, bf16[256,128]{1,0:T(8,128)(2,1)}, bf16[32,144,128]{2,1,0:T(8,128)(2,1)}) custom-call(bf16[32,128,128]{2,1,0:T(8,128)(2,1)} %bitcast.3.arrived_ref, f32[4,128,128]{2,1,0:T(8,128)} %constant_dynamic-slice_fusion.potential_ref, bf16[16,128]{1,0:T(8,128)(2,1)} %overlap.1.overlap_ref, ...), custom_call_target="tpu_custom_call" | custom-call | flops 6000000000 | bytes 6000000 | tf_op jit(solution)/shard_map/field/pallas_call | solution.py:388
  33.7 4.8 %all-to-all-start.1 = ((bf16[32,144,128]{2,1,0:T(8,128)(2,1)}), bf16[32,144,128]{2,1,0:T(8,128)(2,1)}, u32[]{:S(2)}, u32[]{:S(2)}) async-start(bf16[32,144,128]{2,1,0:T(8,128)(2,1)} %get-tuple-element.20), calls=%async_computation.1 | async-start | bytes 2359296 | tf_op jit(solution)/shard_map/all_to_all | solution.py:337
  38.5 3.4 %collective-permute-start.1 = (bf16[256,128]{1,0:T(8,128)(2,1)S(1)}, bf16[256,128]{1,0:T(8,128)(2,1)S(1)}, u32[]{:S(2)}, u32[]{:S(2)}) collective-permute-start(bf16[256,128]{1,0:T(8,128)(2,1)S(1)} %add_convert_fusion.3), channel_id=1, source_target_pairs={{0,64},{16,80},{32,96},{48,112},{64,0},{80,16},{96,32},{112,48},{1... | collective-permute-start | bytes 196616 | tf_op jit(solution)/shard_map/ppermute | solution.py:419
  41.9 2.5 %collective-permute-done.1 = bf16[256,128]{1,0:T(8,128)(2,1)S(1)} collective-permute-done((bf16[256,128]{1,0:T(8,128)(2,1)S(1)}, bf16[256,128]{1,0:T(8,128)(2,1)S(1)}, u32[]{:S(2)}, u32[]{:S(2)}) %collective-permute-start.1) | collective-permute-done | bytes 65568 | tf_op jit(solution)/shard_map/ppermute | solution.py:419
  44.4 7.1 %collective-permute-start.2 = (bf16[256,128]{1,0:T(8,128)(2,1)S(1)}, bf16[256,128]{1,0:T(8,128)(2,1)S(1)}, u32[]{:S(2)}, u32[]{:S(2)}) collective-permute-start(bf16[256,128]{1,0:T(8,128)(2,1)S(1)} %add_convert_fusion.2), channel_id=1, source_target_pairs={{0,192},{16,208},{32,224},{48,240},{64,128},{80,144},{96,160},{112... | collective-permute-start | bytes 196616 | tf_op jit(solution)/shard_map/ppermute | solution.py:421
  51.4 0.7 %collective-permute-start.3 = (bf16[256,128]{1,0:T(8,128)(2,1)S(1)}, bf16[256,128]{1,0:T(8,128)(2,1)S(1)}, u32[]{:S(2)}, u32[]{:S(2)}) collective-permute-start(bf16[256,128]{1,0:T(8,128)(2,1)S(1)} %add_convert_fusion.2), channel_id=1, source_target_pairs={{0,32},{16,48},{32,0},{48,16},{64,96},{80,112},{96,64},{112,80},{1... | collective-permute-start | bytes 196616 | tf_op jit(solution)/shard_map/ppermute | solution.py:421
  52.1 2.3 %collective-permute-done.2 = bf16[256,128]{1,0:T(8,128)(2,1)S(1)} collective-permute-done((bf16[256,128]{1,0:T(8,128)(2,1)S(1)}, bf16[256,128]{1,0:T(8,128)(2,1)S(1)}, u32[]{:S(2)}, u32[]{:S(2)}) %collective-permute-start.2) | collective-permute-done | bytes 65568 | tf_op jit(solution)/shard_map/ppermute | solution.py:421
  54.5 4.2 %collective-permute-done.4 = bf16[256,128]{1,0:T(8,128)(2,1)S(1)} collective-permute-done((bf16[256,128]{1,0:T(8,128)(2,1)S(1)}, bf16[256,128]{1,0:T(8,128)(2,1)S(1)}, u32[]{:S(2)}, u32[]{:S(2)}) %collective-permute-start.4) | collective-permute-done | bytes 65568 | tf_op jit(solution)/shard_map/ppermute | solution.py:421
  58.8 3.3 %collective-permute-start.5 = (bf16[2,256,128]{2,1,0:T(8,128)(2,1)S(1)}, bf16[2,256,128]{2,1,0:T(8,128)(2,1)S(1)}, u32[]{:S(2)}, u32[]{:S(2)}) collective-permute-start(bf16[2,256,128]{2,1,0:T(8,128)(2,1)S(1)} %maximum_select_fusion.1), channel_id=1, source_target_pairs={{0,16},{16,0},{32,48},{48,32},{64,80},{80,64},{96,112},{112,96},{1... | collective-permute-start | bytes 393224 | tf_op jit(solution)/shard_map/ppermute | solution.py:426
  62.1 5.9 %apply.1 = bf16[2,32,32,256]{3,2,1,0:T(8,128)(2,1)} custom-call(bf16[32,144,128]{2,1,0:T(8,128)(2,1)} %all-to-all-done.1.returned_ref.overlap_ref, bf16[32,144,128]{2,1,0:T(8,128)(2,1)} %all-to-all-done.1.returned_ref.overlap_ref, bf16[2,32,32,256]{3,2,1,0:T(8,128)(2,1)} %orbitals_ref.5, s32[32,32,128]{2,1,0:T(8,128)} %mask_ref.5, ...), custom_call_target="tpu_custom_call" | custom-call | flops 4000000000 | bytes 4000000 | tf_op jit(solution)/shard_map/apply/pallas_call | solution.py:427
  68.0 0.8 %convert.11 = f32[8,128,128]{2,1,0:T(8,128)} convert(bf16[8,128,128]{2,1,0:T(8,128)(2,1)S(1)} %bitcast.18) | non-fusion elementwise | flops 131072 | bytes 786432 | tf_op jit(solution)/shard_map/convert_element_type | solution.py:454
  (26 shorter events, 0.3 us)
Async XLA Ops:
  0.6 17.1 %copy-start = (f32[8,128,128]{2,1,0:T(8,128)S(1)}, f32[8,128,128]{2,1,0:T(8,128)}, u32[]{:S(2)}) copy-start(f32[8,128,128]{2,1,0:T(8,128)} %param.16) | copy-start | bytes 1572868
  4.0 7.6 %copy-start.3 = (f32[8,3]{0,1:T(4,128)S(1)}, f32[8,3]{0,1:T(4,128)}, u32[]{:S(2)}) copy-start(f32[8,3]{0,1:T(4,128)} %param.19) | copy-start | bytes 292
  4.0 24.7 %all-to-all-start = ((bf16[32,4,32,128]{3,2,1,0:T(8,128)(2,1)}), bf16[32,4,32,128]{3,2,1,0:T(8,128)(2,1)}, u32[]{:S(2)}, u32[]{:S(2)}) async-start(bf16[32,4,32,128]{3,2,1,0:T(8,128)(2,1)} %spread.1), calls=%async_computation | async-start | bytes 2097152 | tf_op jit(solution)/shard_map/all_to_all | solution.py:337
  14.3 0.6 copy-start.1
  33.5 4.9 %collective-permute-start = (bf16[256,128]{1,0:T(8,128)(2,1)}, bf16[256,128]{1,0:T(8,128)(2,1)S(1)}, u32[]{:S(2)}, u32[]{:S(2)}) collective-permute-start(bf16[256,128]{1,0:T(8,128)(2,1)} %get-tuple-element.19), channel_id=1, source_target_pairs={{0,32},{16,48},{32,0},{48,16},{64,96},{80,112},{96,64},{112,80},{1... | collective-permute-start | bytes 196616 | tf_op jit(solution)/shard_map/ppermute | solution.py:417
  33.7 4.8 %copy-start.2 = (bf16[256,128]{1,0:T(8,128)(2,1)S(1)}, bf16[256,128]{1,0:T(8,128)(2,1)}, u32[]{:S(2)}) copy-start(bf16[256,128]{1,0:T(8,128)(2,1)} %get-tuple-element.18) | copy-start | bytes 196612
  33.7 28.5 %all-to-all-start.1 = ((bf16[32,144,128]{2,1,0:T(8,128)(2,1)}), bf16[32,144,128]{2,1,0:T(8,128)(2,1)}, u32[]{:S(2)}, u32[]{:S(2)}) async-start(bf16[32,144,128]{2,1,0:T(8,128)(2,1)} %get-tuple-element.20), calls=%async_computation.1 | async-start | bytes 2359296 | tf_op jit(solution)/shard_map/all_to_all | solution.py:337
  38.5 5.8 %collective-permute-start.1 = (bf16[256,128]{1,0:T(8,128)(2,1)S(1)}, bf16[256,128]{1,0:T(8,128)(2,1)S(1)}, u32[]{:S(2)}, u32[]{:S(2)}) collective-permute-start(bf16[256,128]{1,0:T(8,128)(2,1)S(1)} %add_convert_fusion.3), channel_id=1, source_target_pairs={{0,64},{16,80},{32,96},{48,112},{64,0},{80,16},{96,32},{112,48},{1... | collective-permute-start | bytes 196616 | tf_op jit(solution)/shard_map/ppermute | solution.py:419
  44.4 10.1 %collective-permute-start.2 = (bf16[256,128]{1,0:T(8,128)(2,1)S(1)}, bf16[256,128]{1,0:T(8,128)(2,1)S(1)}, u32[]{:S(2)}, u32[]{:S(2)}) collective-permute-start(bf16[256,128]{1,0:T(8,128)(2,1)S(1)} %add_convert_fusion.2), channel_id=1, source_target_pairs={{0,192},{16,208},{32,224},{48,240},{64,128},{80,144},{96,160},{112... | collective-permute-start | bytes 196616 | tf_op jit(solution)/shard_map/ppermute | solution.py:421
  51.4 7.3 %collective-permute-start.4 = (bf16[256,128]{1,0:T(8,128)(2,1)S(1)}, bf16[256,128]{1,0:T(8,128)(2,1)S(1)}, u32[]{:S(2)}, u32[]{:S(2)}) collective-permute-start(bf16[256,128]{1,0:T(8,128)(2,1)S(1)} %add_convert_fusion.2), channel_id=1, source_target_pairs={{0,224},{16,240},{32,192},{48,208},{64,160},{80,176},{96,128},{112... | collective-permute-start | bytes 196616 | tf_op jit(solution)/shard_map/ppermute | solution.py:421
  51.4 7.3 %collective-permute-start.3 = (bf16[256,128]{1,0:T(8,128)(2,1)S(1)}, bf16[256,128]{1,0:T(8,128)(2,1)S(1)}, u32[]{:S(2)}, u32[]{:S(2)}) collective-permute-start(bf16[256,128]{1,0:T(8,128)(2,1)S(1)} %add_convert_fusion.2), channel_id=1, source_target_pairs={{0,32},{16,48},{32,0},{48,16},{64,96},{80,112},{96,64},{112,80},{1... | collective-permute-start | bytes 196616 | tf_op jit(solution)/shard_map/ppermute | solution.py:421
  58.8 9.2 %collective-permute-start.5 = (bf16[2,256,128]{2,1,0:T(8,128)(2,1)S(1)}, bf16[2,256,128]{2,1,0:T(8,128)(2,1)S(1)}, u32[]{:S(2)}, u32[]{:S(2)}) collective-permute-start(bf16[2,256,128]{2,1,0:T(8,128)(2,1)S(1)} %maximum_select_fusion.1), channel_id=1, source_target_pairs={{0,16},{16,0},{32,48},{48,32},{64,80},{80,64},{96,112},{112,96},{1... | collective-permute-start | bytes 393224 | tf_op jit(solution)/shard_map/ppermute | solution.py:426

commit v8 on v6

--- a/solution.py
+++ b/solution.py
@@ -409,18 +409,16 @@
         in_specs=[smem_spec] * 3,
         out_shape=jax.ShapeDtypeStruct((atoms, 128), f32),
         compiler_params=params,
-        cost_estimate=cost(5),
+        cost_estimate=cost(10),
         name="strength",
     )(proj_atom, proj_chan, coupling)
     returned = exchange(folded)
 
     near = lax.ppermute(theirs, "band", partners("band", bands))
     mine = (mine.astype(f32) + near.astype(f32)).astype(bf16)
-    for distance in (2, 6):
-        if distance < outer:
-            got = lax.ppermute(mine, "band", partners("band", distance * bands))
-            mine = (mine.astype(f32) + got.astype(f32)).astype(bf16)
-    copies = [lax.ppermute(mine, "band", partners("band", d)) for d in (1, 2, 3)]
+    got = lax.ppermute(mine, "band", partners("band", 2 * bands))
+    mine = (mine.astype(f32) + got.astype(f32)).astype(bf16)
+    far, near, both = [lax.ppermute(mine, "band", partners("band", d * bands)) for d in (6, 1, 7)]
     applied = pl.pallas_call(
         apply_kernel,
         grid=(steps,),
@@ -446,12 +444,13 @@
         cost_estimate=cost(4),
         name="apply",
     )(returned, returned, orbitals, cutoff_mask, channels, phase, wave, strength, occupations, fwd_x)
-    copies, applied = lax.optimization_barrier((copies, applied))
-    place = lax.axis_index("band") % 4
-    pieces = [mine] + copies
-    pieces = [jnp.where(place & 1 != 0, pieces[j ^ 1], pieces[j]) for j in range(4)]
-    pieces = [jnp.where(place & 2 != 0, pieces[j ^ 2], pieces[j]) for j in range(4)]
-    density = jnp.concatenate([pieces[0], pieces[2], pieces[1], pieces[3]], axis=0)
+    far, near, both, applied = lax.optimization_barrier((far, near, both, applied))
+    mine = (mine.astype(f32) + far.astype(f32)).astype(bf16)
+    near = (near.astype(f32) + both.astype(f32)).astype(bf16)
+    upper = lax.axis_index("band") // bands % 2
+    mine = jnp.where(upper == 0, jnp.stack([mine, near]), jnp.stack([near, mine]))
+    other = lax.ppermute(mine, "band", partners("band", 1))
+    density = jnp.where(band == 0, jnp.stack([mine, other]), jnp.stack([other, mine]))
     return (applied, density.astype(f32).reshape(potential.shape))
 
 

time: 67.4 us -> 72.6 us (1.077)
  the two profiles are of different devices: /device:TPU:32 before, /device:TPU:64 now
where the time goes in v8:
time: 72.6 us; the launch traced here: 72.2 us
  waiting for transfers between devices  27.9 us (38%)
  starting transfers between devices  21.7 us (30%)
  Pallas kernels  18.2 us (25%)
  other arithmetic  1.96 us (3%)
  local copies, waits for them, and re-layouts  1.61 us (2%)
  between operations  0.82 us (1%)
    all_to_all x2, waiting for transfers between devices, exchange(): lax.all_to_all(chunks, ('band', 'gy', 'gz'), split_axis=0, concat_axis=0,...  19.1 us
    all_to_all x2, starting transfers between devices, exchange(): lax.all_to_all(chunks, ('band', 'gy', 'gz'), split_axis=0, concat_axis=0,...  12.4 us
    pallas_call x1, Pallas kernels, shards(): pl.pallas_call(apply_kernel, grid=(steps,), in_specs=[pl.BlockSpec((bands...  5.86 us
    ppermute x3, starting transfers between devices, shards(): lax.ppermute(mine, 'band', partners('band', d * bands))  5.68 us
    ppermute x1, waiting for transfers between devices, shards(): other = lax.ppermute(mine, 'band', partners('band', 1))  4.96 us
    pallas_call x1, Pallas kernels, shards(): pl.pallas_call(field_kernel, grid=(bands,), in_specs=[pl.BlockSpec((place...  4.81 us
    ppermute x1, waiting for transfers between devices, shards(): got = lax.ppermute(mine, 'band', partners('band', 2 * bands))  3.84 us
    pallas_call x1, Pallas kernels, shards(): pl.pallas_call(spread_kernel, grid=(steps,), in_specs=[orbitals_spec, mas...  3.4 us
  transfers between devices with their start and end apart: 8, of which 4 were waited for; matrix products, arithmetic and copies ran while one was open for 3% of the time, Pallas kernels for 14%

profile of v8, /device:TPU:64, one launch (start us, length us, event | category | flops | bytes accessed | tf_op | source)
XLA Modules:
  0.0 72.2 jit_solution(9886279405751997948)
XLA Ops:
  0.6 3.4 %spread.1 = bf16[32,4,32,128]{3,2,1,0:T(8,128)(2,1)} custom-call(bf16[2,32,32,256]{3,2,1,0:T(8,128)(2,1)} %orbitals_ref.5, s32[32,32,128]{2,1,0:T(8,128)} %mask_ref.5, f32[2]{0:T(128)} %weight_ref.3, bf16[256,256]{1,0:T(8,128)(2,1)} %constant.71.clone.table_ref), custom_call_target="tpu_custom_call" | custom-call | flops 4000000000 | bytes 4000000 | tf_op jit(solution)/shard_map/spread/pallas_call | solution.py:341
  4.0 7.6 %all-to-all-start = ((bf16[32,4,32,128]{3,2,1,0:T(8,128)(2,1)}), bf16[32,4,32,128]{3,2,1,0:T(8,128)(2,1)}, u32[]{:S(2)}, u32[]{:S(2)}) async-start(bf16[32,4,32,128]{3,2,1,0:T(8,128)(2,1)} %spread.1), calls=%async_computation | async-start | bytes 2097152 | tf_op jit(solution)/shard_map/all_to_all | solution.py:337
  11.7 0.1 fusion.7
  11.8 0.1 add_convert_fusion.4
  12.0 0.1 add.70
  12.1 0.1 sub.24
  12.4 0.6 pad_maximum_fusion.wave_ref
  13.0 0.6 copy-done.1
  13.6 2.8 %overlap.1.overlap_ref = bf16[16,128]{1,0:T(8,128)(2,1)} custom-call(bf16[2,32,32,256]{3,2,1,0:T(8,128)(2,1)} %orbitals_ref.5, s32[32,32,128]{2,1,0:T(8,128)} %mask_ref.5, bf16[4,32,32,128]{3,2,1,0:T(8,128)(2,1)} %channels_ref.3, bf16[16,1024]{1,0:T(8,128)(2,1)} %copy-done.1, f32[16,128]{1,0:T(8,128)} %pad_maximum_fusion.wave_ref), custom_call_target="tpu_custom_call" | custom-call | flops 100000000 | bytes 100000 | tf_op jit(solution)/shard_map/overlap/pallas_call | solution.py:364
  16.4 0.7 constant_dynamic-slice_fusion.potential_ref
  17.1 11.6 %all-to-all-done = bf16[32,4,32,128]{3,2,1,0:T(8,128)(2,1)} async-done(((bf16[32,4,32,128]{3,2,1,0:T(8,128)(2,1)}), bf16[32,4,32,128]{3,2,1,0:T(8,128)(2,1)}, u32[]{:S(2)}, u32[]{:S(2)}) %all-to-all-start) | async-done | bytes 1048608 | tf_op jit(solution)/shard_map/all_to_all | solution.py:337
  28.7 4.8 %field.1 = (bf16[256,128]{1,0:T(8,128)(2,1)}, bf16[256,128]{1,0:T(8,128)(2,1)}, bf16[32,144,128]{2,1,0:T(8,128)(2,1)}) custom-call(bf16[32,128,128]{2,1,0:T(8,128)(2,1)} %bitcast.3.arrived_ref, f32[4,128,128]{2,1,0:T(8,128)} %constant_dynamic-slice_fusion.potential_ref, bf16[16,128]{1,0:T(8,128)(2,1)} %overlap.1.overlap_ref, ...), custom_call_target="tpu_custom_call" | custom-call | flops 6000000000 | bytes 6000000 | tf_op jit(solution)/shard_map/field/pallas_call | solution.py:379
  33.5 1.9 %collective-permute-start = (bf16[256,128]{1,0:T(8,128)(2,1)}, bf16[256,128]{1,0:T(8,128)(2,1)S(1)}, u32[]{:S(2)}, u32[]{:S(2)}) collective-permute-start(bf16[256,128]{1,0:T(8,128)(2,1)} %get-tuple-element.20), channel_id=1, source_target_pairs={{0,32},{16,48},{32,0},{48,16},{64,96},{80,112},{96,64},{112,80},{1... | collective-permute-start | bytes 196616 | tf_op jit(solution)/shard_map/ppermute | solution.py:417
  35.5 4.8 %all-to-all-start.1 = ((bf16[32,144,128]{2,1,0:T(8,128)(2,1)}), bf16[32,144,128]{2,1,0:T(8,128)(2,1)}, u32[]{:S(2)}, u32[]{:S(2)}) async-start(bf16[32,144,128]{2,1,0:T(8,128)(2,1)} %get-tuple-element.22), calls=%async_computation.1 | async-start | bytes 2359296 | tf_op jit(solution)/shard_map/all_to_all | solution.py:337
  40.4 1.3 %strength.1.strength_ref = f32[8,128]{1,0:T(8,128)} custom-call(s32[32]{0:T(128)} %atom_ref.1, s32[32]{0:T(128)} %kind_ref.1, f32[32]{0:T(128)} %coupling_ref), custom_call_target="tpu_custom_call" | custom-call | flops 10000000000 | bytes 10000000 | tf_op jit(solution)/shard_map/strength/pallas_call | solution.py:407
  41.7 3.8 %collective-permute-done.1 = bf16[256,128]{1,0:T(8,128)(2,1)S(1)} collective-permute-done((bf16[256,128]{1,0:T(8,128)(2,1)S(1)}, bf16[256,128]{1,0:T(8,128)(2,1)S(1)}, u32[]{:S(2)}, u32[]{:S(2)}) %collective-permute-start.1) | collective-permute-done | bytes 65568 | tf_op jit(solution)/shard_map/ppermute | solution.py:419
  45.6 4.1 %collective-permute-start.4 = (bf16[256,128]{1,0:T(8,128)(2,1)S(1)}, bf16[256,128]{1,0:T(8,128)(2,1)S(1)}, u32[]{:S(2)}, u32[]{:S(2)}) collective-permute-start(bf16[256,128]{1,0:T(8,128)(2,1)S(1)} %add_convert_fusion.2), channel_id=1, source_target_pairs={{0,224},{16,240},{32,192},{48,208},{64,160},{80,176},{96,128},{112... | collective-permute-start | bytes 196616 | tf_op jit(solution)/shard_map/ppermute | solution.py:421
  49.7 1.4 %collective-permute-start.3 = (bf16[256,128]{1,0:T(8,128)(2,1)S(1)}, bf16[256,128]{1,0:T(8,128)(2,1)S(1)}, u32[]{:S(2)}, u32[]{:S(2)}) collective-permute-start(bf16[256,128]{1,0:T(8,128)(2,1)S(1)} %add_convert_fusion.2), channel_id=1, source_target_pairs={{0,32},{16,48},{32,0},{48,16},{64,96},{80,112},{96,64},{112,80},{1... | collective-permute-start | bytes 196616 | tf_op jit(solution)/shard_map/ppermute | solution.py:421
  51.1 0.2 collective-permute-start.2
  51.3 7.5 %all-to-all-done.1.returned_ref.overlap_ref = bf16[32,144,128]{2,1,0:T(8,128)(2,1)} async-done(((bf16[32,144,128]{2,1,0:T(8,128)(2,1)}), bf16[32,144,128]{2,1,0:T(8,128)(2,1)}, u32[]{:S(2)}, u32[]{:S(2)}) %all-to-all-start.1) | async-done | bytes 1179680 | tf_op jit(solution)/shard_map/all_to_all | solution.py:337
  58.8 5.9 %apply.1 = bf16[2,32,32,256]{3,2,1,0:T(8,128)(2,1)} custom-call(bf16[32,144,128]{2,1,0:T(8,128)(2,1)} %all-to-all-done.1.returned_ref.overlap_ref, bf16[32,144,128]{2,1,0:T(8,128)(2,1)} %all-to-all-done.1.returned_ref.overlap_ref, bf16[2,32,32,256]{3,2,1,0:T(8,128)(2,1)} %orbitals_ref.5, s32[32,32,128]{2,1,0:T(8,128)} %mask_ref.5, ...), custom_call_target="tpu_custom_call" | custom-call | flops 4000000000 | bytes 4000000 | tf_op jit(solution)/shard_map/apply/pallas_call | solution.py:422
  64.8 1.6 %collective-permute-start.5 = (bf16[2,256,128]{2,1,0:T(8,128)(2,1)S(1)}, bf16[2,256,128]{2,1,0:T(8,128)(2,1)S(1)}, u32[]{:S(2)}, u32[]{:S(2)}) collective-permute-start(bf16[2,256,128]{2,1,0:T(8,128)(2,1)S(1)} %maximum_select_fusion.2), channel_id=1, source_target_pairs={{0,16},{16,0},{32,48},{48,32},{64,80},{80,64},{96,112},{112,96},{1... | collective-permute-start | bytes 393224 | tf_op jit(solution)/shard_map/ppermute | solution.py:452
  66.4 5.0 %collective-permute-done.5 = bf16[2,256,128]{2,1,0:T(8,128)(2,1)S(1)} collective-permute-done((bf16[2,256,128]{2,1,0:T(8,128)(2,1)S(1)}, bf16[2,256,128]{2,1,0:T(8,128)(2,1)S(1)}, u32[]{:S(2)}, u32[]{:S(2)}) %collective-permute-start.5) | collective-permute-done | bytes 131104 | tf_op jit(solution)/shard_map/ppermute | solution.py:452
  71.4 0.8 %convert.11 = f32[8,128,128]{2,1,0:T(8,128)} convert(bf16[8,128,128]{2,1,0:T(8,128)(2,1)S(1)} %bitcast.18) | non-fusion elementwise | flops 131072 | bytes 786432 | tf_op jit(solution)/shard_map/convert_element_type | solution.py:454
  (26 shorter events, 0.4 us)
Async XLA Ops:
  0.6 15.8 %copy-start = (f32[8,128,128]{2,1,0:T(8,128)S(1)}, f32[8,128,128]{2,1,0:T(8,128)}, u32[]{:S(2)}) copy-start(f32[8,128,128]{2,1,0:T(8,128)} %param.16) | copy-start | bytes 1572868
  4.0 7.6 %copy-start.3 = (f32[8,3]{0,1:T(4,128)S(1)}, f32[8,3]{0,1:T(4,128)}, u32[]{:S(2)}) copy-start(f32[8,3]{0,1:T(4,128)} %param.19) | copy-start | bytes 292
  4.0 24.7 %all-to-all-start = ((bf16[32,4,32,128]{3,2,1,0:T(8,128)(2,1)}), bf16[32,4,32,128]{3,2,1,0:T(8,128)(2,1)}, u32[]{:S(2)}, u32[]{:S(2)}) async-start(bf16[32,4,32,128]{3,2,1,0:T(8,128)(2,1)} %spread.1), calls=%async_computation | async-start | bytes 2097152 | tf_op jit(solution)/shard_map/all_to_all | solution.py:337
  13.0 0.6 copy-start.1
  33.5 6.7 %collective-permute-start = (bf16[256,128]{1,0:T(8,128)(2,1)}, bf16[256,128]{1,0:T(8,128)(2,1)S(1)}, u32[]{:S(2)}, u32[]{:S(2)}) collective-permute-start(bf16[256,128]{1,0:T(8,128)(2,1)} %get-tuple-element.20), channel_id=1, source_target_pairs={{0,32},{16,48},{32,0},{48,16},{64,96},{80,112},{96,64},{112,80},{1... | collective-permute-start | bytes 196616 | tf_op jit(solution)/shard_map/ppermute | solution.py:417
  35.5 4.8 %copy-start.2 = (bf16[256,128]{1,0:T(8,128)(2,1)S(1)}, bf16[256,128]{1,0:T(8,128)(2,1)}, u32[]{:S(2)}) copy-start(bf16[256,128]{1,0:T(8,128)(2,1)} %get-tuple-element.19) | copy-start | bytes 196612
  35.5 23.3 %all-to-all-start.1 = ((bf16[32,144,128]{2,1,0:T(8,128)(2,1)}), bf16[32,144,128]{2,1,0:T(8,128)(2,1)}, u32[]{:S(2)}, u32[]{:S(2)}) async-start(bf16[32,144,128]{2,1,0:T(8,128)(2,1)} %get-tuple-element.22), calls=%async_computation.1 | async-start | bytes 2359296 | tf_op jit(solution)/shard_map/all_to_all | solution.py:337
  40.3 5.3 %collective-permute-start.1 = (bf16[256,128]{1,0:T(8,128)(2,1)S(1)}, bf16[256,128]{1,0:T(8,128)(2,1)S(1)}, u32[]{:S(2)}, u32[]{:S(2)}) collective-permute-start(bf16[256,128]{1,0:T(8,128)(2,1)S(1)} %add_convert_fusion.3), channel_id=1, source_target_pairs={{0,64},{16,80},{32,96},{48,112},{64,0},{80,16},{96,32},{112,48},{1... | collective-permute-start | bytes 196616 | tf_op jit(solution)/shard_map/ppermute | solution.py:419
  45.6 19.1 %collective-permute-start.4 = (bf16[256,128]{1,0:T(8,128)(2,1)S(1)}, bf16[256,128]{1,0:T(8,128)(2,1)S(1)}, u32[]{:S(2)}, u32[]{:S(2)}) collective-permute-start(bf16[256,128]{1,0:T(8,128)(2,1)S(1)} %add_convert_fusion.2), channel_id=1, source_target_pairs={{0,224},{16,240},{32,192},{48,208},{64,160},{80,176},{96,128},{112... | collective-permute-start | bytes 196616 | tf_op jit(solution)/shard_map/ppermute | solution.py:421
  49.7 15.0 %collective-permute-start.3 = (bf16[256,128]{1,0:T(8,128)(2,1)S(1)}, bf16[256,128]{1,0:T(8,128)(2,1)S(1)}, u32[]{:S(2)}, u32[]{:S(2)}) collective-permute-start(bf16[256,128]{1,0:T(8,128)(2,1)S(1)} %add_convert_fusion.2), channel_id=1, source_target_pairs={{0,32},{16,48},{32,0},{48,16},{64,96},{80,112},{96,64},{112,80},{1... | collective-permute-start | bytes 196616 | tf_op jit(solution)/shard_map/ppermute | solution.py:421
  51.1 13.6 %collective-permute-start.2 = (bf16[256,128]{1,0:T(8,128)(2,1)S(1)}, bf16[256,128]{1,0:T(8,128)(2,1)S(1)}, u32[]{:S(2)}, u32[]{:S(2)}) collective-permute-start(bf16[256,128]{1,0:T(8,128)(2,1)S(1)} %add_convert_fusion.2), channel_id=1, source_target_pairs={{0,192},{16,208},{32,224},{48,240},{64,128},{80,144},{96,160},{112... | collective-permute-start | bytes 196616 | tf_op jit(solution)/shard_map/ppermute | solution.py:421
  64.8 6.6 %collective-permute-start.5 = (bf16[2,256,128]{2,1,0:T(8,128)(2,1)S(1)}, bf16[2,256,128]{2,1,0:T(8,128)(2,1)S(1)}, u32[]{:S(2)}, u32[]{:S(2)}) collective-permute-start(bf16[2,256,128]{2,1,0:T(8,128)(2,1)S(1)} %maximum_select_fusion.2), channel_id=1, source_target_pairs={{0,16},{16,0},{32,48},{48,32},{64,80},{80,64},{96,112},{112,96},{1... | collective-permute-start | bytes 393224 | tf_op jit(solution)/shard_map/ppermute | solution.py:452

commit v9 on v7

--- a/solution.py
+++ b/solution.py
@@ -78,7 +78,9 @@
     out_ref[...] = work_ref[...].reshape(out_ref.shape).astype(bf16)
 
 
-def overlap_kernel(orbitals_ref, mask_ref, channels_ref, phase_ref, wave_ref, out_ref, sums_ref):
+def overlap_kernel(
+    orbitals_ref, mask_ref, channels_ref, phase_ref, wave_ref, out_ref, profile_ref, sums_ref
+):
     step = pl.program_id(0)
     rows = mask_ref.shape[0] * mask_ref.shape[1]
     length = mask_ref.shape[2]
@@ -87,8 +89,10 @@
     mask = jnp.where(mask_ref[...] != 0, 1.0, 0.0).astype(bf16)
     orbs = [orbitals_ref[n].reshape(rows, 2 * length) for n in range(2)]
     columns = []
+    profile_ref[kinds] = mask
     for c in range(kinds):
-        radial = (channels_ref[c] * mask).reshape(rows, length)
+        profile_ref[c] = channels_ref[c] * mask
+        radial = profile_ref[c].reshape(rows, length)
         radial = jnp.concatenate([radial, radial], axis=1)
         columns += [radial * orbs[0], radial * orbs[1]]
     part = dot(phase_ref[...], jnp.concatenate(columns, axis=1))
@@ -194,8 +198,7 @@
     returned_ref,
     overlap_ref,
     orbitals_ref,
-    mask_ref,
-    channels_ref,
+    profile_ref,
     phase_ref,
     wave_ref,
     strength_ref,
@@ -206,9 +209,10 @@
     work_ref,
 ):
     step = pl.program_id(0)
-    rows_y, rows_z, length = mask_ref.shape
+    kinds = profile_ref.shape[0] - 1
+    grid_shape = profile_ref.shape[1:]
+    rows_y, rows_z, length = grid_shape
     atoms = wave_ref.shape[0] // 2
-    kinds = channels_ref.shape[0]
 
     work_ref[...] = returned_ref[...].astype(f32).reshape(work_ref.shape)
     planes = [work_ref[pl.ds(y, length, stride=rows_y), :].astype(bf16) for y in range(rows_y)]
@@ -236,28 +240,28 @@
     extra = dot_tn(phase_ref[...], factor_ref[...])
 
     def squared(start, axis):
-        index = start + lax.broadcasted_iota(jnp.int32, mask_ref.shape, axis)
+        index = start + lax.broadcasted_iota(jnp.int32, grid_shape, axis)
         wave = jnp.where(index >= length // 2, index - length, index)
         return wave * wave
 
     first_y = lax.axis_index("gy") * (rows_y * pl.num_programs(0)) + step * rows_y
     energy = squared(first_y, 0) + squared(lax.axis_index("gz") * rows_z, 1) + squared(0, 2)
     energy = kinetic_scale * 0.5 * energy.astype(f32)
-    inside = mask_ref[...] != 0
     scale = 1.0 / root_weights(weight_ref, (2 * rows_z, 1), 0, rows_z)
     for y in range(rows_y):
         block = local[y // 2][y % 2 * 128 : y % 2 * 128 + 128]
         both = scale * (block[:64, : 2 * length] + block[64:, 2 * length :])
-        radials = [channels_ref[c, y].astype(f32) for c in range(kinds)]
+        radials = [profile_ref[c, y].astype(f32) for c in range(kinds + 1)]
         for n in range(2):
             for part in range(2):
                 cols = slice(part * length, part * length + length)
                 total = both[n * rows_z : (n + 1) * rows_z, cols]
                 total = total + energy[y] * orbitals_ref[n, y, :, cols].astype(f32)
+                total = total * radials[kinds]
                 for c in range(kinds):
                     base = ((c * 2 + n) * 2 + part) * length
                     total = total + radials[c] * extra[y * rows_z : (y + 1) * rows_z, base : base + length]
-                out_ref[n, y, :, cols] = jnp.where(inside[y], total, 0.0).astype(bf16)
+                out_ref[n, y, :, cols] = total.astype(bf16)
 
 
 def strength_kernel(atom_ref, kind_ref, coupling_ref, out_ref):
@@ -370,12 +374,16 @@
         cost_estimate=cost(0.1),
         name="strength",
     )(proj_atom, proj_chan, coupling)
-    overlap = pl.pallas_call(
+    profile_spec = pl.BlockSpec((kinds + 1, span, rows_z, length), lambda i: (0, i, 0, 0))
+    overlap, profile = pl.pallas_call(
         overlap_kernel,
         grid=(steps,),
         in_specs=[orbitals_spec, mask_spec, channels_spec, phase_spec, whole(2 * atoms, length)],
-        out_specs=whole(2 * atoms, 128),
-        out_shape=jax.ShapeDtypeStruct((2 * atoms, 128), bf16),
+        out_specs=[whole(2 * atoms, 128), profile_spec],
+        out_shape=[
+            jax.ShapeDtypeStruct((2 * atoms, 128), bf16),
+            jax.ShapeDtypeStruct((kinds + 1, rows_y, rows_z, length), bf16),
+        ],
         scratch_shapes=[pltpu.VMEM((2 * atoms, kinds * 4 * length), f32)],
         compiler_params=params,
         cost_estimate=cost(0.1),
@@ -431,8 +439,7 @@
             pl.BlockSpec((bands * places, planes * span, 128), lambda i: (0, i, 0)),
             pl.BlockSpec((bands * places, 2 * atoms, 128), lambda i: (0, rows // (2 * atoms), 0)),
             orbitals_spec,
-            mask_spec,
-            channels_spec,
+            profile_spec,
             phase_spec,
             whole(2 * atoms, length),
             whole(atoms, 128),
@@ -445,10 +452,10 @@
             pltpu.VMEM((2 * atoms, kinds * 4 * length), bf16),
             pltpu.VMEM((length * span, 128), f32),
         ],
-        compiler_params=params,
+        compiler_params=pltpu.CompilerParams(vmem_limit_bytes=52224 * 1024),
         cost_estimate=cost(4),
         name="apply",
-    )(returned, returned, orbitals, cutoff_mask, channels, phase, wave, strength, occupations, fwd_x)
+    )(returned, returned, orbitals, profile, phase, wave, strength, occupations, fwd_x)
     other, applied = lax.optimization_barrier((other, applied))
     density = jnp.where(band == 0, jnp.stack([mine, other]), jnp.stack([other, mine]))
     return (applied, density.astype(f32).reshape(potential.shape))

time: 69.3 us -> 68.5 us (0.988)
  starting transfers between devices: 26.9 us -> 25.3 us
    ppermute x3, starting transfers between devices: 7.76 us -> 6.88 us  [shards(): lax.ppermute(mine, 'band', partners('band', d * bands))]
    ppermute x1, waiting for transfers between devices: 2.47 us -> 3.22 us  [shards(): got = lax.ppermute(mine, 'band', partners('band', 2 * bands))]
    all_to_all x2, starting transfers between devices: 12.4 us -> 11.6 us  [exchange(): lax.all_to_all(chunks, ('band', 'gy', 'gz'), split_axis=0, concat_axis=0,...]
  transfers between devices with their start and end apart: 8 -> 8, of which waited for: 4 -> 5; matrix products, arithmetic and copies ran while one was open for 3% -> 3% of each run, Pallas kernels for 14% -> 15%
where the time goes in v9:
time: 68.5 us; the launch traced here: 68 us
  starting transfers between devices  25.3 us (37%)
  waiting for transfers between devices  20 us (29%)
  Pallas kernels  18.2 us (27%)
  other arithmetic  1.96 us (3%)
  local copies, waits for them, and re-layouts  1.63 us (2%)
  between operations  0.86 us (1%)
    all_to_all x2, starting transfers between devices, exchange(): lax.all_to_all(chunks, ('band', 'gy', 'gz'), split_axis=0, concat_axis=0,...  11.6 us
    all_to_all x2, waiting for transfers between devices, exchange(): lax.all_to_all(chunks, ('band', 'gy', 'gz'), split_axis=0, concat_axis=0,...  9.99 us
    ppermute x3, starting transfers between devices, shards(): lax.ppermute(mine, 'band', partners('band', d * bands))  6.88 us
    ppermute x3, waiting for transfers between devices, shards(): lax.ppermute(mine, 'band', partners('band', d * bands))  6.55 us
    pallas_call x1, Pallas kernels, shards(): pl.pallas_call(apply_kernel, grid=(steps,), in_specs=[pl.BlockSpec((bands...  5.53 us
    pallas_call x1, Pallas kernels, shards(): pl.pallas_call(field_kernel, grid=(bands,), in_specs=[pl.BlockSpec((place...  4.82 us
    pallas_call x1, Pallas kernels, shards(): pl.pallas_call(spread_kernel, grid=(steps,), in_specs=[orbitals_spec, mas...  3.4 us
    ppermute x1, starting transfers between devices, shards(): got = lax.ppermute(mine, 'band', partners('band', 2 * bands))  3.36 us
  transfers between devices with their start and end apart: 8, of which 5 were waited for; matrix products, arithmetic and copies ran while one was open for 3% of the time, Pallas kernels for 15%

profile of v9, /device:TPU:32, one launch (start us, length us, event | category | flops | bytes accessed | tf_op | source)
XLA Modules:
  0.0 68.0 jit_solution(15601876878855203404)
XLA Ops:
  0.6 3.4 %spread.1 = bf16[32,4,32,128]{3,2,1,0:T(8,128)(2,1)} custom-call(bf16[2,32,32,256]{3,2,1,0:T(8,128)(2,1)} %orbitals_ref.5, s32[32,32,128]{2,1,0:T(8,128)} %mask_ref.3, f32[2]{0:T(128)} %weight_ref.3, bf16[256,256]{1,0:T(8,128)(2,1)} %constant.71.clone.table_ref), custom_call_target="tpu_custom_call" | custom-call | flops 4000000000 | bytes 4000000 | tf_op jit(solution)/shard_map/spread/pallas_call | solution.py:345
  4.0 7.6 %all-to-all-start = ((bf16[32,4,32,128]{3,2,1,0:T(8,128)(2,1)}), bf16[32,4,32,128]{3,2,1,0:T(8,128)(2,1)}, u32[]{:S(2)}, u32[]{:S(2)}) async-start(bf16[32,4,32,128]{3,2,1,0:T(8,128)(2,1)} %spread.1), calls=%async_computation | async-start | bytes 2097152 | tf_op jit(solution)/shard_map/all_to_all | solution.py:341
  11.7 0.1 fusion.7
  11.8 0.1 add_convert_fusion.4
  12.0 0.1 add.71
  12.1 0.1 sub.25
  12.2 1.3 %strength.1.strength_ref = f32[8,128]{1,0:T(8,128)} custom-call(s32[32]{0:T(128)} %atom_ref.1, s32[32]{0:T(128)} %kind_ref.1, f32[32]{0:T(128)} %coupling_ref), custom_call_target="tpu_custom_call" | custom-call | flops 100000000 | bytes 100000 | tf_op jit(solution)/shard_map/strength/pallas_call | solution.py:369
  13.7 0.6 pad_maximum_fusion.wave_ref
  14.3 0.6 copy-done.2
  14.9 3.2 %overlap.1 = (bf16[16,128]{1,0:T(8,128)(2,1)}, bf16[5,32,32,128]{3,2,1,0:T(8,128)(2,1)}) custom-call(bf16[2,32,32,256]{3,2,1,0:T(8,128)(2,1)} %orbitals_ref.5, s32[32,32,128]{2,1,0:T(8,128)} %mask_ref.3, bf16[4,32,32,128]{3,2,1,0:T(8,128)(2,1)} %channels_ref.1, bf16[16,1024]{1,0:T(8,128)(2,1)} %copy-done.2, f32[16,128]{1,0:T(8,128)} %pad_maximum_fusion.wave_ref), custom_call_target="tpu_custom_call" | custom-call | flops 100000000 | bytes 100000 | tf_op jit(solution)/shard_map/overlap/pallas_call | solution.py:378
  18.0 0.7 %constant_dynamic-slice_fusion.potential_ref = f32[4,128,128]{2,1,0:T(8,128)} fusion(f32[8,128,128]{2,1,0:T(8,128)S(1)} %copy-done, s32[]{:T(128)S(6)} %select_n.77), kind=kLoop, calls=%fused_computation.34 | loop fusion | bytes 524292 | tf_op jit(solution)/shard_map/dynamic_slice | solution.py:356
  18.8 10.0 %all-to-all-done = bf16[32,4,32,128]{3,2,1,0:T(8,128)(2,1)} async-done(((bf16[32,4,32,128]{3,2,1,0:T(8,128)(2,1)}), bf16[32,4,32,128]{3,2,1,0:T(8,128)(2,1)}, u32[]{:S(2)}, u32[]{:S(2)}) %all-to-all-start) | async-done | bytes 1048608 | tf_op jit(solution)/shard_map/all_to_all | solution.py:341
  28.7 4.8 %field.1 = (bf16[256,128]{1,0:T(8,128)(2,1)}, bf16[256,128]{1,0:T(8,128)(2,1)}, bf16[32,144,128]{2,1,0:T(8,128)(2,1)}) custom-call(bf16[32,128,128]{2,1,0:T(8,128)(2,1)} %bitcast.3.arrived_ref, f32[4,128,128]{2,1,0:T(8,128)} %constant_dynamic-slice_fusion.potential_ref, bf16[16,128]{1,0:T(8,128)(2,1)} %get-tuple-element.20.overlap_ref, ...), custom_call_target="tpu_custom_call" | custom-call | flops 6000000000 | bytes 6000000 | tf_op jit(solution)/shard_map/field/pallas_call | solution.py:396
  33.7 4.1 %all-to-all-start.1 = ((bf16[32,144,128]{2,1,0:T(8,128)(2,1)}), bf16[32,144,128]{2,1,0:T(8,128)(2,1)S(1)}, u32[]{:S(2)}, u32[]{:S(2)}) async-start(bf16[32,144,128]{2,1,0:T(8,128)(2,1)} %get-tuple-element.23), calls=%async_computation.1 | async-start | bytes 2359296 | tf_op jit(solution)/shard_map/all_to_all | solution.py:341
  37.8 0.2 collective-permute-done
  38.1 3.4 %collective-permute-start.1 = (bf16[256,128]{1,0:T(8,128)(2,1)S(1)}, bf16[256,128]{1,0:T(8,128)(2,1)S(1)}, u32[]{:S(2)}, u32[]{:S(2)}) collective-permute-start(bf16[256,128]{1,0:T(8,128)(2,1)S(1)} %add_convert_fusion.3), channel_id=1, source_target_pairs={{0,64},{16,80},{32,96},{48,112},{64,0},{80,16},{96,32},{112,48},{1... | collective-permute-start | bytes 196616 | tf_op jit(solution)/shard_map/ppermute | solution.py:427
  41.4 3.2 %collective-permute-done.1 = bf16[256,128]{1,0:T(8,128)(2,1)S(1)} collective-permute-done((bf16[256,128]{1,0:T(8,128)(2,1)S(1)}, bf16[256,128]{1,0:T(8,128)(2,1)S(1)}, u32[]{:S(2)}, u32[]{:S(2)}) %collective-permute-start.1) | collective-permute-done | bytes 65568 | tf_op jit(solution)/shard_map/ppermute | solution.py:427
  44.7 6.2 %collective-permute-start.2 = (bf16[256,128]{1,0:T(8,128)(2,1)S(1)}, bf16[256,128]{1,0:T(8,128)(2,1)S(1)}, u32[]{:S(2)}, u32[]{:S(2)}) collective-permute-start(bf16[256,128]{1,0:T(8,128)(2,1)S(1)} %add_convert_fusion.2), channel_id=1, source_target_pairs={{0,192},{16,208},{32,224},{48,240},{64,128},{80,144},{96,160},{112... | collective-permute-start | bytes 196616 | tf_op jit(solution)/shard_map/ppermute | solution.py:429
  50.9 0.7 %collective-permute-start.3 = (bf16[256,128]{1,0:T(8,128)(2,1)S(1)}, bf16[256,128]{1,0:T(8,128)(2,1)S(1)}, u32[]{:S(2)}, u32[]{:S(2)}) collective-permute-start(bf16[256,128]{1,0:T(8,128)(2,1)S(1)} %add_convert_fusion.2), channel_id=1, source_target_pairs={{0,32},{16,48},{32,0},{48,16},{64,96},{80,112},{96,64},{112,80},{1... | collective-permute-start | bytes 196616 | tf_op jit(solution)/shard_map/ppermute | solution.py:429
  51.6 2.3 %collective-permute-done.2 = bf16[256,128]{1,0:T(8,128)(2,1)S(1)} collective-permute-done((bf16[256,128]{1,0:T(8,128)(2,1)S(1)}, bf16[256,128]{1,0:T(8,128)(2,1)S(1)}, u32[]{:S(2)}, u32[]{:S(2)}) %collective-permute-start.2) | collective-permute-done | bytes 65568 | tf_op jit(solution)/shard_map/ppermute | solution.py:429
  53.9 4.2 %collective-permute-done.4 = bf16[256,128]{1,0:T(8,128)(2,1)S(1)} collective-permute-done((bf16[256,128]{1,0:T(8,128)(2,1)S(1)}, bf16[256,128]{1,0:T(8,128)(2,1)S(1)}, u32[]{:S(2)}, u32[]{:S(2)}) %collective-permute-start.4) | collective-permute-done | bytes 65568 | tf_op jit(solution)/shard_map/ppermute | solution.py:429
  58.2 3.3 %collective-permute-start.5 = (bf16[2,256,128]{2,1,0:T(8,128)(2,1)S(1)}, bf16[2,256,128]{2,1,0:T(8,128)(2,1)S(1)}, u32[]{:S(2)}, u32[]{:S(2)}) collective-permute-start(bf16[2,256,128]{2,1,0:T(8,128)(2,1)S(1)} %maximum_select_fusion.1), channel_id=1, source_target_pairs={{0,16},{16,0},{32,48},{48,32},{64,80},{80,64},{96,112},{112,96},{1... | collective-permute-start | bytes 393224 | tf_op jit(solution)/shard_map/ppermute | solution.py:434
  61.6 5.5 %apply.1 = bf16[2,32,32,256]{3,2,1,0:T(8,128)(2,1)} custom-call(bf16[32,144,128]{2,1,0:T(8,128)(2,1)S(1)} %all-to-all-done.1.returned_ref.overlap_ref, bf16[32,144,128]{2,1,0:T(8,128)(2,1)S(1)} %all-to-all-done.1.returned_ref.overlap_ref, bf16[2,32,32,256]{3,2,1,0:T(8,128)(2,1)S(1)} %copy-done.1, bf16[5,32,32,128]{3,2,1,0:T(8,128)(2,1)} %get-tuple-element.24.profile_ref, ...), custom_call_target="tpu_custom_call" | custom-call | flops 4000000000 | bytes 4000000 | tf_op jit(solution)/shard_map/apply/pallas_call | solution.py:435
  67.2 0.8 %convert.11 = f32[8,128,128]{2,1,0:T(8,128)} convert(bf16[8,128,128]{2,1,0:T(8,128)(2,1)S(1)} %bitcast.18) | non-fusion elementwise | flops 131072 | bytes 786432 | tf_op jit(solution)/shard_map/convert_element_type | solution.py:461
  (38 shorter events, 0.5 us)
Async XLA Ops:
  0.6 17.4 %copy-start = (f32[8,128,128]{2,1,0:T(8,128)S(1)}, f32[8,128,128]{2,1,0:T(8,128)}, u32[]{:S(2)}) copy-start(f32[8,128,128]{2,1,0:T(8,128)} %param.16) | copy-start | bytes 1572868
  4.0 7.6 %copy-start.9 = (f32[8,3]{0,1:T(4,128)S(1)}, f32[8,3]{0,1:T(4,128)}, u32[]{:S(2)}) copy-start(f32[8,3]{0,1:T(4,128)} %param.19) | copy-start | bytes 292
  4.0 24.7 %all-to-all-start = ((bf16[32,4,32,128]{3,2,1,0:T(8,128)(2,1)}), bf16[32,4,32,128]{3,2,1,0:T(8,128)(2,1)}, u32[]{:S(2)}, u32[]{:S(2)}) async-start(bf16[32,4,32,128]{3,2,1,0:T(8,128)(2,1)} %spread.1), calls=%async_computation | async-start | bytes 2097152 | tf_op jit(solution)/shard_map/all_to_all | solution.py:341
  14.3 0.6 copy-start.2
  33.6 4.5 %collective-permute-start = (bf16[256,128]{1,0:T(8,128)(2,1)}, bf16[256,128]{1,0:T(8,128)(2,1)S(1)}, u32[]{:S(2)}, u32[]{:S(2)}) collective-permute-start(bf16[256,128]{1,0:T(8,128)(2,1)} %get-tuple-element.22), channel_id=1, source_target_pairs={{0,32},{16,48},{32,0},{48,16},{64,96},{80,112},{96,64},{112,80},{1... | collective-permute-start | bytes 196616 | tf_op jit(solution)/shard_map/ppermute | solution.py:425
  33.7 4.4 %copy-start.8 = (bf16[256,128]{1,0:T(8,128)(2,1)S(1)}, bf16[256,128]{1,0:T(8,128)(2,1)}, u32[]{:S(2)}) copy-start(bf16[256,128]{1,0:T(8,128)(2,1)} %get-tuple-element.21) | copy-start | bytes 196612
  33.7 27.9 %all-to-all-start.1 = ((bf16[32,144,128]{2,1,0:T(8,128)(2,1)}), bf16[32,144,128]{2,1,0:T(8,128)(2,1)S(1)}, u32[]{:S(2)}, u32[]{:S(2)}) async-start(bf16[32,144,128]{2,1,0:T(8,128)(2,1)} %get-tuple-element.23), calls=%async_computation.1 | async-start | bytes 2359296 | tf_op jit(solution)/shard_map/all_to_all | solution.py:341
  37.8 23.8 %copy-start.1 = (bf16[2,32,32,256]{3,2,1,0:T(8,128)(2,1)S(1)}, bf16[2,32,32,256]{3,2,1,0:T(8,128)(2,1)}, u32[]{:S(2)}) copy-start(bf16[2,32,32,256]{3,2,1,0:T(8,128)(2,1)} %orbitals_ref.5) | copy-start | bytes 3145732
  37.8 23.8 %copy-start.3 = (bf16[16,1024]{1,0:T(8,128)(2,1)S(1)}, bf16[16,1024]{1,0:T(8,128)(2,1)}, u32[]{:S(2)}) copy-start(bf16[16,1024]{1,0:T(8,128)(2,1)} %copy-done.2) | copy-start | bytes 98308
  37.8 23.8 %copy-start.4 = (f32[16,128]{1,0:T(8,128)S(1)}, f32[16,128]{1,0:T(8,128)}, u32[]{:S(2)}) copy-start(f32[16,128]{1,0:T(8,128)} %pad_maximum_fusion.wave_ref) | copy-start | bytes 24580
  37.8 23.8 %copy-start.5 = (f32[2]{0:T(128)S(1)}, f32[2]{0:T(128)}, u32[]{:S(2)}) copy-start(f32[2]{0:T(128)} %weight_ref.3) | copy-start | bytes 28
  37.8 23.8 %copy-start.6 = (bf16[128,512]{1,0:T(8,128)(2,1)S(1)}, bf16[128,512]{1,0:T(8,128)(2,1)}, u32[]{:S(2)}) copy-start(bf16[128,512]{1,0:T(8,128)(2,1)} %constant.76.clone.table_ref) | copy-start | bytes 393220
  37.8 23.8 %copy-start.7 = (f32[8,128]{1,0:T(8,128)S(1)}, f32[8,128]{1,0:T(8,128)}, u32[]{:S(2)}) copy-start(f32[8,128]{1,0:T(8,128)} %strength.1.strength_ref) | copy-start | bytes 12292
  38.1 6.6 %collective-permute-start.1 = (bf16[256,128]{1,0:T(8,128)(2,1)S(1)}, bf16[256,128]{1,0:T(8,128)(2,1)S(1)}, u32[]{:S(2)}, u32[]{:S(2)}) collective-permute-start(bf16[256,128]{1,0:T(8,128)(2,1)S(1)} %add_convert_fusion.3), channel_id=1, source_target_pairs={{0,64},{16,80},{32,96},{48,112},{64,0},{80,16},{96,32},{112,48},{1... | collective-permute-start | bytes 196616 | tf_op jit(solution)/shard_map/ppermute | solution.py:427
  44.7 9.2 %collective-permute-start.2 = (bf16[256,128]{1,0:T(8,128)(2,1)S(1)}, bf16[256,128]{1,0:T(8,128)(2,1)S(1)}, u32[]{:S(2)}, u32[]{:S(2)}) collective-permute-start(bf16[256,128]{1,0:T(8,128)(2,1)S(1)} %add_convert_fusion.2), channel_id=1, source_target_pairs={{0,192},{16,208},{32,224},{48,240},{64,128},{80,144},{96,160},{112... | collective-permute-start | bytes 196616 | tf_op jit(solution)/shard_map/ppermute | solution.py:429
  50.9 7.3 %collective-permute-start.4 = (bf16[256,128]{1,0:T(8,128)(2,1)S(1)}, bf16[256,128]{1,0:T(8,128)(2,1)S(1)}, u32[]{:S(2)}, u32[]{:S(2)}) collective-permute-start(bf16[256,128]{1,0:T(8,128)(2,1)S(1)} %add_convert_fusion.2), channel_id=1, source_target_pairs={{0,224},{16,240},{32,192},{48,208},{64,160},{80,176},{96,128},{112... | collective-permute-start | bytes 196616 | tf_op jit(solution)/shard_map/ppermute | solution.py:429
  50.9 7.3 %collective-permute-start.3 = (bf16[256,128]{1,0:T(8,128)(2,1)S(1)}, bf16[256,128]{1,0:T(8,128)(2,1)S(1)}, u32[]{:S(2)}, u32[]{:S(2)}) collective-permute-start(bf16[256,128]{1,0:T(8,128)(2,1)S(1)} %add_convert_fusion.2), channel_id=1, source_target_pairs={{0,32},{16,48},{32,0},{48,16},{64,96},{80,112},{96,64},{112,80},{1... | collective-permute-start | bytes 196616 | tf_op jit(solution)/shard_map/ppermute | solution.py:429
  58.2 9.0 %collective-permute-start.5 = (bf16[2,256,128]{2,1,0:T(8,128)(2,1)S(1)}, bf16[2,256,128]{2,1,0:T(8,128)(2,1)S(1)}, u32[]{:S(2)}, u32[]{:S(2)}) collective-permute-start(bf16[2,256,128]{2,1,0:T(8,128)(2,1)S(1)} %maximum_select_fusion.1), channel_id=1, source_target_pairs={{0,16},{16,0},{32,48},{48,32},{64,80},{80,64},{96,112},{112,96},{1... | collective-permute-start | bytes 393224 | tf_op jit(solution)/shard_map/ppermute | solution.py:434

commit v10 on v9

--- a/solution.py
+++ b/solution.py
@@ -128,9 +128,8 @@
     arrived_ref,
     potential_ref,
     overlap_ref,
-    inv_z_ref,
+    z_ref,
     inv_y_ref,
-    fwd_z_ref,
     fwd_y_ref,
     mine_ref,
     theirs_ref,
@@ -145,7 +144,7 @@
         [jnp.concatenate([arrived_ref[sy * 4 + sz] for sz in range(4)], axis=1) for sy in range(parts)],
         axis=0,
     )
-    halfway = dot(columns, inv_z_ref[...]).astype(bf16)
+    halfway = dot(columns, z_ref[0]).astype(bf16)
     stacked = []
     for x in range(planes):
         first = [(sy * planes + x) * rows for sy in range(parts)]
@@ -171,7 +170,7 @@
         back.append(
             jnp.concatenate([real[:, :length], imag[:, :length], real[:, length:], imag[:, length:]], axis=1)
         )
-    back = dot(jnp.concatenate(back, axis=0), fwd_z_ref[...]).astype(bf16)
+    back = dot(jnp.concatenate(back, axis=0), z_ref[1]).astype(bf16)
     span = rows // 2
     for x in range(planes):
         for sy in range(parts):
@@ -311,8 +310,9 @@
     order = np.arange(length).reshape(places, bands, planes).transpose(1, 0, 2).reshape(-1)
     inv_x = rounded(inverse[:, order], 2 * length)
     inv_y = rounded(inverse, 2 * length)
-    inv_z = rounded(np.einsum("fzcsl,nm->scnlmfz", split_inverse, pick), 4 * length)
-    fwd_z = rounded(np.einsum("cslfz,nm->nfzscml", split_forward, pick), 4 * length)
+    inv_z = np.einsum("fzcsl,nm->scnlmfz", split_inverse, pick).reshape(4 * length, 4 * length)
+    fwd_z = np.einsum("cslfz,nm->nfzscml", split_forward, pick).reshape(4 * length, 4 * length)
+    both_z = rounded(np.stack([inv_z, fwd_z]), 8 * length).reshape(2, 4 * length, 4 * length)
     fwd_y = rounded(forward, 2 * length)
     fwd_x = rounded(np.einsum("rkcx->xcrk", forward[..., order]), length)
     first_y = lax.axis_index("gy") * rows_y
@@ -370,7 +370,7 @@
         strength_kernel,
         in_specs=[smem_spec] * 3,
         out_shape=jax.ShapeDtypeStruct((atoms, 128), f32),
-        compiler_params=params,
+        compiler_params=pltpu.CompilerParams(vmem_limit_bytes=16384 * 1024),
         cost_estimate=cost(0.1),
         name="strength",
     )(proj_atom, proj_chan, coupling)
@@ -385,7 +385,7 @@
             jax.ShapeDtypeStruct((kinds + 1, rows_y, rows_z, length), bf16),
         ],
         scratch_shapes=[pltpu.VMEM((2 * atoms, kinds * 4 * length), f32)],
-        compiler_params=params,
+        compiler_params=pltpu.CompilerParams(vmem_limit_bytes=32768 * 1024),
         cost_estimate=cost(0.1),
         name="overlap",
     )(orbitals, cutoff_mask, channels, phase, wave)
@@ -400,9 +400,8 @@
             pl.BlockSpec((places, rows, 128), lambda i: (i, 0, 0)),
             whole(planes, length, length),
             whole(2 * atoms, 128),
-            whole(4 * length, 4 * length),
+            whole(2, 4 * length, 4 * length),
             whole(2 * length, 2 * length),
-            whole(4 * length, 4 * length),
             whole(2 * length, 2 * length),
         ],
         out_specs=[
@@ -416,10 +415,10 @@
             jax.ShapeDtypeStruct((bands * places, rows + 2 * atoms, 128), bf16),
         ],
         scratch_shapes=[pltpu.VMEM((planes * length, length), f32)],
-        compiler_params=params,
+        compiler_params=pltpu.CompilerParams(vmem_limit_bytes=53248 * 1024),
         cost_estimate=cost(6),
         name="field",
-    )(arrived.reshape(bands * places, rows, 128), potential_part, overlap, inv_z, inv_y, fwd_z, fwd_y)
+    )(arrived.reshape(bands * places, rows, 128), potential_part, overlap, both_z, inv_y, fwd_y)
     returned = exchange(folded)
 
     near = lax.ppermute(theirs, "band", partners("band", bands))

time: 68.5 us -> 67.9 us (level)
  Pallas kernels: 18.2 us -> 15.3 us
  local copies, waits for them, and re-layouts: 1.63 us -> 3.69 us
  waiting for transfers between devices: 20 us -> 21 us
    unnamed x21 -> x29, local copies, waits for them, and re-layouts: 0.65 us -> 3.4 us
    pallas_call x1, Pallas kernels: 3.16 us -> 1.27 us  [shards(): pl.pallas_call(overlap_kernel, grid=(steps,), in_specs=[orbitals_spec, ma...]
    all_to_all x2, waiting for transfers between devices: 9.99 us -> 11.1 us  [exchange(): lax.all_to_all(chunks, ('band', 'gy', 'gz'), split_axis=0, concat_axis=0,...]
    pallas_call x1, Pallas kernels: 1.31 us -> 0.59 us  [shards(): pl.pallas_call(strength_kernel, in_specs=[smem_spec] * 3, out_shape=jax.S...]
    dynamic_slice x1, local copies, waits for them, and re-layouts: 0.72 us -> 0.02 us  [shards(): lax.dynamic_slice_in_dim(potential, band * planes, planes, 0)]
  transfers between devices with their start and end apart: 8 -> 8, of which waited for: 5 -> 5; matrix products, arithmetic and copies ran while one was open for 3% -> 1% of each run, Pallas kernels for 15% -> 11%
where the time goes in v10:
time: 67.9 us; the launch traced here: 67.4 us
  starting transfers between devices  25.1 us (37%)
  waiting for transfers between devices  21 us (31%)
  Pallas kernels  15.3 us (23%)
  local copies, waits for them, and re-layouts  3.69 us (5%)
  other arithmetic  1.36 us (2%)
  between operations  0.93 us (1%)
    all_to_all x2, starting transfers between devices, exchange(): lax.all_to_all(chunks, ('band', 'gy', 'gz'), split_axis=0, concat_axis=0,...  11.4 us
    all_to_all x2, waiting for transfers between devices, exchange(): lax.all_to_all(chunks, ('band', 'gy', 'gz'), split_axis=0, concat_axis=0,...  11.1 us
    ppermute x3, starting transfers between devices, shards(): lax.ppermute(mine, 'band', partners('band', d * bands))  6.91 us
    ppermute x3, waiting for transfers between devices, shards(): lax.ppermute(mine, 'band', partners('band', d * bands))  6.55 us
    pallas_call x1, Pallas kernels, shards(): pl.pallas_call(apply_kernel, grid=(steps,), in_specs=[pl.BlockSpec((bands...  5.52 us
    pallas_call x1, Pallas kernels, shards(): pl.pallas_call(field_kernel, grid=(bands,), in_specs=[pl.BlockSpec((place...  4.49 us
    pallas_call x1, Pallas kernels, shards(): pl.pallas_call(spread_kernel, grid=(steps,), in_specs=[orbitals_spec, mas...  3.4 us
    unnamed x29, local copies, waits for them, and re-layouts  3.4 us
  transfers between devices with their start and end apart: 8, of which 5 were waited for; matrix products, arithmetic and copies ran while one was open for 1% of the time, Pallas kernels for 11%

profile of v10, /device:TPU:32, one launch (start us, length us, event | category | flops | bytes accessed | tf_op | source)
XLA Modules:
  0.0 67.4 jit_solution(17381221394674585588)
XLA Ops:
  0.6 3.4 %spread.1 = bf16[32,4,32,128]{3,2,1,0:T(8,128)(2,1)} custom-call(bf16[2,32,32,256]{3,2,1,0:T(8,128)(2,1)} %orbitals_ref.5, s32[32,32,128]{2,1,0:T(8,128)} %mask_ref.3, f32[2]{0:T(128)} %weight_ref.3, bf16[256,256]{1,0:T(8,128)(2,1)} %constant.69.clone.table_ref), custom_call_target="tpu_custom_call" | custom-call | flops 4000000000 | bytes 4000000 | tf_op jit(solution)/shard_map/spread/pallas_call | solution.py:345
  4.1 7.5 %all-to-all-start = ((bf16[32,4,32,128]{3,2,1,0:T(8,128)(2,1)}), bf16[32,4,32,128]{3,2,1,0:T(8,128)(2,1)S(1)}, u32[]{:S(2)}, u32[]{:S(2)}) async-start(bf16[32,4,32,128]{3,2,1,0:T(8,128)(2,1)} %spread.1), calls=%async_computation | async-start | bytes 2097152 | tf_op jit(solution)/shard_map/all_to_all | solution.py:341
  11.6 0.1 fusion.7
  11.7 0.1 add_convert_fusion.4
  11.9 0.1 add.71
  12.0 0.1 sub.25
  12.2 0.6 strength.1.strength_ref
  13.0 1.2 %copy-done.2 = bf16[2,32,32,256]{3,2,1,0:T(8,128)(2,1)S(1)} copy-done((bf16[2,32,32,256]{3,2,1,0:T(8,128)(2,1)S(1)}, bf16[2,32,32,256]{3,2,1,0:T(8,128)(2,1)}, u32[]{:S(2)}) %copy-start.2) | copy-done | bytes 1048600
  14.2 1.0 %copy-done.4 = s32[32,32,128]{2,1,0:T(8,128)S(1)} copy-done((s32[32,32,128]{2,1,0:T(8,128)S(1)}, s32[32,32,128]{2,1,0:T(8,128)}, u32[]{:S(2)}) %copy-start.4) | copy-done | bytes 524312
  15.2 1.3 %overlap.1 = (bf16[16,128]{1,0:T(8,128)(2,1)S(1)}, bf16[5,32,32,128]{3,2,1,0:T(8,128)(2,1)S(1)}) custom-call(bf16[2,32,32,256]{3,2,1,0:T(8,128)(2,1)S(1)} %copy-done.2, s32[32,32,128]{2,1,0:T(8,128)S(1)} %copy-done.4, bf16[4,32,32,128]{3,2,1,0:T(8,128)(2,1)S(1)} %copy-done.1, bf16[16,1024]{1,0:T(8,128)(2,1)S(1)} %constant_dynamic-update-slice_fusion.phase_ref, ...), custom_call_target="tpu_custom_call" | custom-call | flops 100000000 | bytes 100000 | tf_op jit(solution)/shard_map/overlap/pallas_call | solution.py:378
  16.5 1.1 %copy-done.5 = bf16[5,32,32,128]{3,2,1,0:T(8,128)(2,1)} copy-done((bf16[5,32,32,128]{3,2,1,0:T(8,128)(2,1)}, bf16[5,32,32,128]{3,2,1,0:T(8,128)(2,1)S(1)}, u32[]{:S(2)}) %copy-start.5) | copy-done | bytes 1310744
  17.6 11.1 %all-to-all-done = bf16[32,4,32,128]{3,2,1,0:T(8,128)(2,1)S(1)} async-done(((bf16[32,4,32,128]{3,2,1,0:T(8,128)(2,1)}), bf16[32,4,32,128]{3,2,1,0:T(8,128)(2,1)S(1)}, u32[]{:S(2)}, u32[]{:S(2)}) %all-to-all-start) | async-done | bytes 1048608 | tf_op jit(solution)/shard_map/all_to_all | solution.py:341
  28.7 4.5 %field.1 = (bf16[256,128]{1,0:T(8,128)(2,1)S(1)}, bf16[256,128]{1,0:T(8,128)(2,1)S(1)}, bf16[32,144,128]{2,1,0:T(8,128)(2,1)}) custom-call(bf16[32,128,128]{2,1,0:T(8,128)(2,1)S(1)} %bitcast.18, f32[4,128,128]{2,1,0:T(8,128)S(1)} %constant_dynamic-slice_fusion.potential_ref, bf16[16,128]{1,0:T(8,128)(2,1)S(1)} %get-tuple-element.20.overlap_ref, ...), custom_call_target="tpu_custom_call" | custom-call | flops 6000000000 | bytes 6000000 | tf_op jit(solution)/shard_map/field/pallas_call | solution.py:396
  33.3 3.9 %all-to-all-start.1 = ((bf16[32,144,128]{2,1,0:T(8,128)(2,1)}), bf16[32,144,128]{2,1,0:T(8,128)(2,1)S(1)}, u32[]{:S(2)}, u32[]{:S(2)}) async-start(bf16[32,144,128]{2,1,0:T(8,128)(2,1)} %get-tuple-element.23), calls=%async_computation.1 | async-start | bytes 2359296 | tf_op jit(solution)/shard_map/all_to_all | solution.py:341
  37.3 0.2 collective-permute-done
  37.5 3.4 %collective-permute-start.1 = (bf16[256,128]{1,0:T(8,128)(2,1)S(1)}, bf16[256,128]{1,0:T(8,128)(2,1)S(1)}, u32[]{:S(2)}, u32[]{:S(2)}) collective-permute-start(bf16[256,128]{1,0:T(8,128)(2,1)S(1)} %add_convert_fusion.3), channel_id=1, source_target_pairs={{0,64},{16,80},{32,96},{48,112},{64,0},{80,16},{96,32},{112,48},{1... | collective-permute-start | bytes 196616 | tf_op jit(solution)/shard_map/ppermute | solution.py:426
  40.8 3.2 %collective-permute-done.1 = bf16[256,128]{1,0:T(8,128)(2,1)S(1)} collective-permute-done((bf16[256,128]{1,0:T(8,128)(2,1)S(1)}, bf16[256,128]{1,0:T(8,128)(2,1)S(1)}, u32[]{:S(2)}, u32[]{:S(2)}) %collective-permute-start.1) | collective-permute-done | bytes 65568 | tf_op jit(solution)/shard_map/ppermute | solution.py:426
  44.1 6.2 %collective-permute-start.2 = (bf16[256,128]{1,0:T(8,128)(2,1)S(1)}, bf16[256,128]{1,0:T(8,128)(2,1)S(1)}, u32[]{:S(2)}, u32[]{:S(2)}) collective-permute-start(bf16[256,128]{1,0:T(8,128)(2,1)S(1)} %add_convert_fusion.2), channel_id=1, source_target_pairs={{0,192},{16,208},{32,224},{48,240},{64,128},{80,144},{96,160},{112... | collective-permute-start | bytes 196616 | tf_op jit(solution)/shard_map/ppermute | solution.py:428
  50.3 0.7 %collective-permute-start.3 = (bf16[256,128]{1,0:T(8,128)(2,1)S(1)}, bf16[256,128]{1,0:T(8,128)(2,1)S(1)}, u32[]{:S(2)}, u32[]{:S(2)}) collective-permute-start(bf16[256,128]{1,0:T(8,128)(2,1)S(1)} %add_convert_fusion.2), channel_id=1, source_target_pairs={{0,32},{16,48},{32,0},{48,16},{64,96},{80,112},{96,64},{112,80},{1... | collective-permute-start | bytes 196616 | tf_op jit(solution)/shard_map/ppermute | solution.py:428
  51.0 2.3 %collective-permute-done.2 = bf16[256,128]{1,0:T(8,128)(2,1)S(1)} collective-permute-done((bf16[256,128]{1,0:T(8,128)(2,1)S(1)}, bf16[256,128]{1,0:T(8,128)(2,1)S(1)}, u32[]{:S(2)}, u32[]{:S(2)}) %collective-permute-start.2) | collective-permute-done | bytes 65568 | tf_op jit(solution)/shard_map/ppermute | solution.py:428
  53.3 4.2 %collective-permute-done.4 = bf16[256,128]{1,0:T(8,128)(2,1)S(1)} collective-permute-done((bf16[256,128]{1,0:T(8,128)(2,1)S(1)}, bf16[256,128]{1,0:T(8,128)(2,1)S(1)}, u32[]{:S(2)}, u32[]{:S(2)}) %collective-permute-start.4) | collective-permute-done | bytes 65568 | tf_op jit(solution)/shard_map/ppermute | solution.py:428
  57.6 3.3 %collective-permute-start.5 = (bf16[2,256,128]{2,1,0:T(8,128)(2,1)S(1)}, bf16[2,256,128]{2,1,0:T(8,128)(2,1)S(1)}, u32[]{:S(2)}, u32[]{:S(2)}) collective-permute-start(bf16[2,256,128]{2,1,0:T(8,128)(2,1)S(1)} %maximum_select_fusion.1), channel_id=1, source_target_pairs={{0,16},{16,0},{32,48},{48,32},{64,80},{80,64},{96,112},{112,96},{1... | collective-permute-start | bytes 393224 | tf_op jit(solution)/shard_map/ppermute | solution.py:433
  61.0 5.5 %apply.1 = bf16[2,32,32,256]{3,2,1,0:T(8,128)(2,1)} custom-call(bf16[32,144,128]{2,1,0:T(8,128)(2,1)S(1)} %all-to-all-done.1.returned_ref.overlap_ref, bf16[32,144,128]{2,1,0:T(8,128)(2,1)S(1)} %all-to-all-done.1.returned_ref.overlap_ref, bf16[2,32,32,256]{3,2,1,0:T(8,128)(2,1)S(1)} %copy-done.3, bf16[5,32,32,128]{3,2,1,0:T(8,128)(2,1)} %copy-done.5, ...), custom_call_target="tpu_custom_call" | custom-call | flops 4000000000 | bytes 4000000 | tf_op jit(solution)/shard_map/apply/pallas_call | solution.py:434
  66.6 0.8 %convert.11 = f32[8,128,128]{2,1,0:T(8,128)} convert(bf16[8,128,128]{2,1,0:T(8,128)(2,1)S(1)} %bitcast.19) | non-fusion elementwise | flops 131072 | bytes 786432 | tf_op jit(solution)/shard_map/convert_element_type | solution.py:460
  (46 shorter events, 0.5 us)
Async XLA Ops:
  0.6 17.0 %copy-start = (f32[8,128,128]{2,1,0:T(8,128)S(1)}, f32[8,128,128]{2,1,0:T(8,128)}, u32[]{:S(2)}) copy-start(f32[8,128,128]{2,1,0:T(8,128)} %param.15) | copy-start | bytes 1572868
  4.0 7.6 %copy-start.13 = (f32[8,3]{0,1:T(4,128)S(1)}, f32[8,3]{0,1:T(4,128)}, u32[]{:S(2)}) copy-start(f32[8,3]{0,1:T(4,128)} %param.18) | copy-start | bytes 292
  4.0 8.1 %copy-start.6 = (s32[32]{0:T(128)S(1)}, s32[32]{0:T(128)}, u32[]{:S(2)}) copy-start(s32[32]{0:T(128)} %atom_ref.1) | copy-start | bytes 388
  4.1 8.1 %copy-start.7 = (s32[32]{0:T(128)S(1)}, s32[32]{0:T(128)}, u32[]{:S(2)}) copy-start(s32[32]{0:T(128)} %kind_ref.1) | copy-start | bytes 388
  4.1 8.1 %copy-start.8 = (f32[32]{0:T(128)S(1)}, f32[32]{0:T(128)}, u32[]{:S(2)}) copy-start(f32[32]{0:T(128)} %coupling_ref) | copy-start | bytes 388
  4.1 8.9 %copy-start.1 = (bf16[4,32,32,128]{3,2,1,0:T(8,128)(2,1)S(1)}, bf16[4,32,32,128]{3,2,1,0:T(8,128)(2,1)}, u32[]{:S(2)}) copy-start(bf16[4,32,32,128]{3,2,1,0:T(8,128)(2,1)} %channels_ref.1) | copy-start | bytes 3145732
  4.1 24.6 %all-to-all-start = ((bf16[32,4,32,128]{3,2,1,0:T(8,128)(2,1)}), bf16[32,4,32,128]{3,2,1,0:T(8,128)(2,1)S(1)}, u32[]{:S(2)}, u32[]{:S(2)}) async-start(bf16[32,4,32,128]{3,2,1,0:T(8,128)(2,1)} %spread.1), calls=%async_computation | async-start | bytes 2097152 | tf_op jit(solution)/shard_map/all_to_all | solution.py:341
  12.9 1.2 %copy-start.2 = (bf16[2,32,32,256]{3,2,1,0:T(8,128)(2,1)S(1)}, bf16[2,32,32,256]{3,2,1,0:T(8,128)(2,1)}, u32[]{:S(2)}) copy-start(bf16[2,32,32,256]{3,2,1,0:T(8,128)(2,1)} %orbitals_ref.5) | copy-start | bytes 3145732
  14.2 1.0 %copy-start.4 = (s32[32,32,128]{2,1,0:T(8,128)S(1)}, s32[32,32,128]{2,1,0:T(8,128)}, u32[]{:S(2)}) copy-start(s32[32,32,128]{2,1,0:T(8,128)} %mask_ref.3) | copy-start | bytes 1572868
  15.2 13.5 %copy-start.11 = (bf16[256,256]{1,0:T(8,128)(2,1)S(1)}, bf16[256,256]{1,0:T(8,128)(2,1)}, u32[]{:S(2)}) copy-start(bf16[256,256]{1,0:T(8,128)(2,1)} %constant.72.clone.fwd_y_ref) | copy-start | bytes 393220
  15.2 13.5 %copy-start.12 = (bf16[256,256]{1,0:T(8,128)(2,1)S(1)}, bf16[256,256]{1,0:T(8,128)(2,1)}, u32[]{:S(2)}) copy-start(bf16[256,256]{1,0:T(8,128)(2,1)} %constant.70.clone.inv_y_ref) | copy-start | bytes 393220
  16.5 1.1 %copy-start.5 = (bf16[5,32,32,128]{3,2,1,0:T(8,128)(2,1)}, bf16[5,32,32,128]{3,2,1,0:T(8,128)(2,1)S(1)}, u32[]{:S(2)}) copy-start(bf16[5,32,32,128]{3,2,1,0:T(8,128)(2,1)S(1)} %get-tuple-element.24.profile_ref) | copy-start | bytes 3932164
  33.2 4.3 %collective-permute-start = (bf16[256,128]{1,0:T(8,128)(2,1)S(1)}, bf16[256,128]{1,0:T(8,128)(2,1)S(1)}, u32[]{:S(2)}, u32[]{:S(2)}) collective-permute-start(bf16[256,128]{1,0:T(8,128)(2,1)S(1)} %get-tuple-element.22), channel_id=1, source_target_pairs={{0,32},{16,48},{32,0},{48,16},{64,96},{80,112},{96,64},{112,80},{1... | collective-permute-start | bytes 196616 | tf_op jit(solution)/shard_map/ppermute | solution.py:424
  33.3 27.7 %all-to-all-start.1 = ((bf16[32,144,128]{2,1,0:T(8,128)(2,1)}), bf16[32,144,128]{2,1,0:T(8,128)(2,1)S(1)}, u32[]{:S(2)}, u32[]{:S(2)}) async-start(bf16[32,144,128]{2,1,0:T(8,128)(2,1)} %get-tuple-element.23), calls=%async_computation.1 | async-start | bytes 2359296 | tf_op jit(solution)/shard_map/all_to_all | solution.py:341
  37.2 23.8 %copy-start.3 = (bf16[2,32,32,256]{3,2,1,0:T(8,128)(2,1)S(1)}, bf16[2,32,32,256]{3,2,1,0:T(8,128)(2,1)}, u32[]{:S(2)}) copy-start(bf16[2,32,32,256]{3,2,1,0:T(8,128)(2,1)} %orbitals_ref.5) | copy-start | bytes 3145732
  37.2 23.8 %copy-start.9 = (f32[2]{0:T(128)S(1)}, f32[2]{0:T(128)}, u32[]{:S(2)}) copy-start(f32[2]{0:T(128)} %weight_ref.3) | copy-start | bytes 28
  37.3 23.8 %copy-start.10 = (bf16[128,512]{1,0:T(8,128)(2,1)S(1)}, bf16[128,512]{1,0:T(8,128)(2,1)}, u32[]{:S(2)}) copy-start(bf16[128,512]{1,0:T(8,128)(2,1)} %constant.73.clone.table_ref) | copy-start | bytes 393220
  37.5 6.6 %collective-permute-start.1 = (bf16[256,128]{1,0:T(8,128)(2,1)S(1)}, bf16[256,128]{1,0:T(8,128)(2,1)S(1)}, u32[]{:S(2)}, u32[]{:S(2)}) collective-permute-start(bf16[256,128]{1,0:T(8,128)(2,1)S(1)} %add_convert_fusion.3), channel_id=1, source_target_pairs={{0,64},{16,80},{32,96},{48,112},{64,0},{80,16},{96,32},{112,48},{1... | collective-permute-start | bytes 196616 | tf_op jit(solution)/shard_map/ppermute | solution.py:426
  44.1 9.2 %collective-permute-start.2 = (bf16[256,128]{1,0:T(8,128)(2,1)S(1)}, bf16[256,128]{1,0:T(8,128)(2,1)S(1)}, u32[]{:S(2)}, u32[]{:S(2)}) collective-permute-start(bf16[256,128]{1,0:T(8,128)(2,1)S(1)} %add_convert_fusion.2), channel_id=1, source_target_pairs={{0,192},{16,208},{32,224},{48,240},{64,128},{80,144},{96,160},{112... | collective-permute-start | bytes 196616 | tf_op jit(solution)/shard_map/ppermute | solution.py:428
  50.3 7.3 %collective-permute-start.4 = (bf16[256,128]{1,0:T(8,128)(2,1)S(1)}, bf16[256,128]{1,0:T(8,128)(2,1)S(1)}, u32[]{:S(2)}, u32[]{:S(2)}) collective-permute-start(bf16[256,128]{1,0:T(8,128)(2,1)S(1)} %add_convert_fusion.2), channel_id=1, source_target_pairs={{0,224},{16,240},{32,192},{48,208},{64,160},{80,176},{96,128},{112... | collective-permute-start | bytes 196616 | tf_op jit(solution)/shard_map/ppermute | solution.py:428
  50.3 7.3 %collective-permute-start.3 = (bf16[256,128]{1,0:T(8,128)(2,1)S(1)}, bf16[256,128]{1,0:T(8,128)(2,1)S(1)}, u32[]{:S(2)}, u32[]{:S(2)}) collective-permute-start(bf16[256,128]{1,0:T(8,128)(2,1)S(1)} %add_convert_fusion.2), channel_id=1, source_target_pairs={{0,32},{16,48},{32,0},{48,16},{64,96},{80,112},{96,64},{112,80},{1... | collective-permute-start | bytes 196616 | tf_op jit(solution)/shard_map/ppermute | solution.py:428
  57.6 8.9 %collective-permute-start.5 = (bf16[2,256,128]{2,1,0:T(8,128)(2,1)S(1)}, bf16[2,256,128]{2,1,0:T(8,128)(2,1)S(1)}, u32[]{:S(2)}, u32[]{:S(2)}) collective-permute-start(bf16[2,256,128]{2,1,0:T(8,128)(2,1)S(1)} %maximum_select_fusion.1), channel_id=1, source_target_pairs={{0,16},{16,0},{32,48},{48,32},{64,80},{80,64},{96,112},{112,96},{1... | collective-permute-start | bytes 393224 | tf_op jit(solution)/shard_map/ppermute | solution.py:433

commit v11 on v10

--- a/solution.py
+++ b/solution.py
@@ -134,63 +134,68 @@
     mine_ref,
     theirs_ref,
     out_ref,
-    sums_ref,
 ):
-    step = pl.program_id(0)
     planes, length = potential_ref.shape[:2]
-    parts = arrived_ref.shape[0] // 4
+    parts = 4
+    places = 4 * parts
+    bands = arrived_ref.shape[0] // places
     rows = arrived_ref.shape[1] // planes
-    columns = jnp.concatenate(
-        [jnp.concatenate([arrived_ref[sy * 4 + sz] for sz in range(4)], axis=1) for sy in range(parts)],
-        axis=0,
-    )
-    halfway = dot(columns, z_ref[0]).astype(bf16)
-    stacked = []
+    span = rows // 2
+    halfway = []
+    for b in range(bands):
+        columns = jnp.concatenate(
+            [
+                jnp.concatenate([arrived_ref[b * places + sy * 4 + sz] for sz in range(4)], axis=1)
+                for sy in range(parts)
+            ],
+            axis=0,
+        )
+        halfway.append(dot(columns, z_ref[0]).astype(bf16))
+    fields = []
+    for b in range(bands):
+        for x in range(planes):
+            first = [(sy * planes + x) * rows for sy in range(parts)]
+            plane = jnp.concatenate([halfway[b][start : start + rows] for start in first], axis=0)
+            real = jnp.concatenate([plane[:, 0:128], plane[:, 256:384]], axis=1)
+            imag = jnp.concatenate([plane[:, 128:256], plane[:, 384:512]], axis=1)
+            fields.append(dot(inv_y_ref[...], jnp.concatenate([real, imag], axis=0)))
+    density = []
+    scaled = []
     for x in range(planes):
-        first = [(sy * planes + x) * rows for sy in range(parts)]
-        plane = jnp.concatenate([halfway[start : start + rows] for start in first], axis=0)
-        real = jnp.concatenate([plane[:, 0:128], plane[:, 256:384]], axis=1)
-        imag = jnp.concatenate([plane[:, 128:256], plane[:, 384:512]], axis=1)
-        stacked.append(jnp.concatenate([real, imag], axis=0))
-    fields = [dot(inv_y_ref[...], block) for block in stacked]
-    scaled = []
-    for x, field in enumerate(fields):
-        real, imag = field[:length], field[length:]
-        square = real * real + imag * imag
-        density = square[:, :length] + square[:, length:]
-        here = slice(x * length, (x + 1) * length)
-        sums_ref[here, :] = jnp.where(step == 0, density, sums_ref[here, :] + density)
-        potential = jnp.concatenate([potential_ref[x], potential_ref[x]], axis=1)
-        potential = jnp.concatenate([potential, potential], axis=0)
-        scaled.append((potential * field).astype(bf16))
+        square = [fields[b * planes + x] * fields[b * planes + x] for b in range(bands)]
+        square = sum(s[:length] + s[length:] for s in square)
+        density.append((square[:, :length] + square[:, length:]).astype(bf16))
+    for b in range(bands):
+        for x in range(planes):
+            potential = jnp.concatenate([potential_ref[x], potential_ref[x]], axis=1)
+            potential = jnp.concatenate([potential, potential], axis=0)
+            scaled.append((potential * fields[b * planes + x]).astype(bf16))
     folded = [dot(fwd_y_ref[...], block).astype(bf16) for block in scaled]
-    back = []
-    for block in folded:
-        real, imag = block[:length], block[length:]
-        back.append(
-            jnp.concatenate([real[:, :length], imag[:, :length], real[:, length:], imag[:, length:]], axis=1)
-        )
-    back = dot(jnp.concatenate(back, axis=0), z_ref[1]).astype(bf16)
-    span = rows // 2
-    for x in range(planes):
-        for sy in range(parts):
-            for half in range(2):
-                start = x * length + sy * rows + half * span
-                row = (half * planes + x) * span
-                for sz in range(4):
-                    out_ref[sy * 4 + sz, row : row + span, :] = back[
-                        start : start + span, sz * 128 : sz * 128 + 128
-                    ]
+    for b in range(bands):
+        back = []
+        for block in folded[b * planes : (b + 1) * planes]:
+            real, imag = block[:length], block[length:]
+            back.append(
+                jnp.concatenate([real[:, :length], imag[:, :length], real[:, length:], imag[:, length:]], axis=1)
+            )
+        back = dot(jnp.concatenate(back, axis=0), z_ref[1]).astype(bf16)
+        for x in range(planes):
+            for sy in range(parts):
+                for half in range(2):
+                    start = x * length + sy * rows + half * span
+                    row = (half * planes + x) * span
+                    for sz in range(4):
+                        out_ref[b * places + sy * 4 + sz, row : row + span, :] = back[
+                            start : start + span, sz * 128 : sz * 128 + 128
+                        ]
     for place in range(out_ref.shape[0]):
         out_ref[place, planes * rows :, :] = overlap_ref[...]
-
-    @pl.when(step == pl.num_programs(0) - 1)
-    def last():
-        half = planes // 2 * length
-        low, high = sums_ref[:half, :].astype(bf16), sums_ref[half:, :].astype(bf16)
-        upper = lax.axis_index("band") // 2 % 2
-        mine_ref[...] = jnp.where(upper == 0, low, high)
-        theirs_ref[...] = jnp.where(upper == 0, high, low)
+    upper = lax.axis_index("band") // 2 % 2
+    half = planes // 2
+    for x in range(half):
+        here = slice(x * length, (x + 1) * length)
+        mine_ref[here, :] = jnp.where(upper == 0, density[x], density[half + x])
+        theirs_ref[here, :] = jnp.where(upper == 0, density[half + x], density[x])
 
 
 def apply_kernel(
@@ -395,9 +400,9 @@
     half = planes // 2 * length
     mine, theirs, folded = pl.pallas_call(
         field_kernel,
-        grid=(bands,),
+        grid=(1,),
         in_specs=[
-            pl.BlockSpec((places, rows, 128), lambda i: (i, 0, 0)),
+            whole(bands * places, rows, 128),
             whole(planes, length, length),
             whole(2 * atoms, 128),
             whole(2, 4 * length, 4 * length),
@@ -407,14 +412,13 @@
         out_specs=[
             whole(half, length),
             whole(half, length),
-            pl.BlockSpec((places, rows + 2 * atoms, 128), lambda i: (i, 0, 0)),
+            whole(bands * places, rows + 2 * atoms, 128),
         ],
         out_shape=[
             jax.ShapeDtypeStruct((half, length), bf16),
             jax.ShapeDtypeStruct((half, length), bf16),
             jax.ShapeDtypeStruct((bands * places, rows + 2 * atoms, 128), bf16),
         ],
-        scratch_shapes=[pltpu.VMEM((planes * length, length), f32)],
         compiler_params=pltpu.CompilerParams(vmem_limit_bytes=53248 * 1024),
         cost_estimate=cost(6),
         name="field",

time: 67.9 us -> 67.6 us (level)
  no operation moved by 1% of the time
where the time goes in v11:
time: 67.6 us; the launch traced here: 67.1 us
  starting transfers between devices  25.1 us (37%)
  waiting for transfers between devices  21 us (31%)
  Pallas kernels  15 us (22%)
  local copies, waits for them, and re-layouts  3.69 us (5%)
  other arithmetic  1.36 us (2%)
  between operations  0.93 us (1%)
    all_to_all x2, starting transfers between devices, exchange(): lax.all_to_all(chunks, ('band', 'gy', 'gz'), split_axis=0, concat_axis=0,...  11.4 us
    all_to_all x2, waiting for transfers between devices, exchange(): lax.all_to_all(chunks, ('band', 'gy', 'gz'), split_axis=0, concat_axis=0,...  11.1 us
    ppermute x3, starting transfers between devices, shards(): lax.ppermute(mine, 'band', partners('band', d * bands))  6.92 us
    ppermute x3, waiting for transfers between devices, shards(): lax.ppermute(mine, 'band', partners('band', d * bands))  6.55 us
    pallas_call x1, Pallas kernels, shards(): pl.pallas_call(apply_kernel, grid=(steps,), in_specs=[pl.BlockSpec((bands...  5.52 us
    pallas_call x1, Pallas kernels, shards(): pl.pallas_call(field_kernel, grid=(1,), in_specs=[whole(bands * places, r...  4.2 us
    pallas_call x1, Pallas kernels, shards(): pl.pallas_call(spread_kernel, grid=(steps,), in_specs=[orbitals_spec, mas...  3.4 us
    unnamed x29, local copies, waits for them, and re-layouts  3.4 us
  transfers between devices with their start and end apart: 8, of which 5 were waited for; matrix products, arithmetic and copies ran while one was open for 1% of the time, Pallas kernels for 11%

profile of v11, /device:TPU:32, one launch (start us, length us, event | category | flops | bytes accessed | tf_op | source)
XLA Modules:
  0.0 67.1 jit_solution(8151009049854314608)
XLA Ops:
  0.6 3.4 %spread.1 = bf16[32,4,32,128]{3,2,1,0:T(8,128)(2,1)} custom-call(bf16[2,32,32,256]{3,2,1,0:T(8,128)(2,1)} %orbitals_ref.5, s32[32,32,128]{2,1,0:T(8,128)} %mask_ref.3, f32[2]{0:T(128)} %weight_ref.3, bf16[256,256]{1,0:T(8,128)(2,1)} %constant.69.clone.table_ref), custom_call_target="tpu_custom_call" | custom-call | flops 4000000000 | bytes 4000000 | tf_op jit(solution)/shard_map/spread/pallas_call | solution.py:350
  4.1 7.5 %all-to-all-start = ((bf16[32,4,32,128]{3,2,1,0:T(8,128)(2,1)}), bf16[32,4,32,128]{3,2,1,0:T(8,128)(2,1)S(1)}, u32[]{:S(2)}, u32[]{:S(2)}) async-start(bf16[32,4,32,128]{3,2,1,0:T(8,128)(2,1)} %spread.1), calls=%async_computation | async-start | bytes 2097152 | tf_op jit(solution)/shard_map/all_to_all | solution.py:346
  11.6 0.1 fusion.7
  11.7 0.1 add_convert_fusion.4
  11.9 0.1 add.71
  12.0 0.1 sub.25
  12.2 0.6 strength.1.strength_ref
  13.0 1.2 %copy-done.2 = bf16[2,32,32,256]{3,2,1,0:T(8,128)(2,1)S(1)} copy-done((bf16[2,32,32,256]{3,2,1,0:T(8,128)(2,1)S(1)}, bf16[2,32,32,256]{3,2,1,0:T(8,128)(2,1)}, u32[]{:S(2)}) %copy-start.2) | copy-done | bytes 1048600
  14.2 1.0 %copy-done.4 = s32[32,32,128]{2,1,0:T(8,128)S(1)} copy-done((s32[32,32,128]{2,1,0:T(8,128)S(1)}, s32[32,32,128]{2,1,0:T(8,128)}, u32[]{:S(2)}) %copy-start.4) | copy-done | bytes 524312
  15.2 1.3 %overlap.1 = (bf16[16,128]{1,0:T(8,128)(2,1)S(1)}, bf16[5,32,32,128]{3,2,1,0:T(8,128)(2,1)S(1)}) custom-call(bf16[2,32,32,256]{3,2,1,0:T(8,128)(2,1)S(1)} %copy-done.2, s32[32,32,128]{2,1,0:T(8,128)S(1)} %copy-done.4, bf16[4,32,32,128]{3,2,1,0:T(8,128)(2,1)S(1)} %copy-done.1, bf16[16,1024]{1,0:T(8,128)(2,1)S(1)} %constant_dynamic-update-slice_fusion.phase_ref, ...), custom_call_target="tpu_custom_call" | custom-call | flops 100000000 | bytes 100000 | tf_op jit(solution)/shard_map/overlap/pallas_call | solution.py:383
  16.5 1.1 %copy-done.5 = bf16[5,32,32,128]{3,2,1,0:T(8,128)(2,1)} copy-done((bf16[5,32,32,128]{3,2,1,0:T(8,128)(2,1)}, bf16[5,32,32,128]{3,2,1,0:T(8,128)(2,1)S(1)}, u32[]{:S(2)}) %copy-start.5) | copy-done | bytes 1310744
  17.6 11.1 %all-to-all-done = bf16[32,4,32,128]{3,2,1,0:T(8,128)(2,1)S(1)} async-done(((bf16[32,4,32,128]{3,2,1,0:T(8,128)(2,1)}), bf16[32,4,32,128]{3,2,1,0:T(8,128)(2,1)S(1)}, u32[]{:S(2)}, u32[]{:S(2)}) %all-to-all-start) | async-done | bytes 1048608 | tf_op jit(solution)/shard_map/all_to_all | solution.py:346
  28.7 4.2 %field.1 = (bf16[256,128]{1,0:T(8,128)(2,1)S(1)}, bf16[256,128]{1,0:T(8,128)(2,1)S(1)}, bf16[32,144,128]{2,1,0:T(8,128)(2,1)}) custom-call(bf16[32,128,128]{2,1,0:T(8,128)(2,1)S(1)} %bitcast.18, f32[4,128,128]{2,1,0:T(8,128)S(1)} %constant_dynamic-slice_fusion.potential_ref, bf16[16,128]{1,0:T(8,128)(2,1)S(1)} %get-tuple-element.20.overlap_ref, ...), custom_call_target="tpu_custom_call" | custom-call | flops 6000000000 | bytes 6000000 | tf_op jit(solution)/shard_map/field/pallas_call | solution.py:401
  33.0 3.9 %all-to-all-start.1 = ((bf16[32,144,128]{2,1,0:T(8,128)(2,1)}), bf16[32,144,128]{2,1,0:T(8,128)(2,1)S(1)}, u32[]{:S(2)}, u32[]{:S(2)}) async-start(bf16[32,144,128]{2,1,0:T(8,128)(2,1)} %get-tuple-element.23), calls=%async_computation.1 | async-start | bytes 2359296 | tf_op jit(solution)/shard_map/all_to_all | solution.py:346
  37.0 0.2 collective-permute-done
  37.2 3.4 %collective-permute-start.1 = (bf16[256,128]{1,0:T(8,128)(2,1)S(1)}, bf16[256,128]{1,0:T(8,128)(2,1)S(1)}, u32[]{:S(2)}, u32[]{:S(2)}) collective-permute-start(bf16[256,128]{1,0:T(8,128)(2,1)S(1)} %add_convert_fusion.3), channel_id=1, source_target_pairs={{0,64},{16,80},{32,96},{48,112},{64,0},{80,16},{96,32},{112,48},{1... | collective-permute-start | bytes 196616 | tf_op jit(solution)/shard_map/ppermute | solution.py:430
  40.5 3.2 %collective-permute-done.1 = bf16[256,128]{1,0:T(8,128)(2,1)S(1)} collective-permute-done((bf16[256,128]{1,0:T(8,128)(2,1)S(1)}, bf16[256,128]{1,0:T(8,128)(2,1)S(1)}, u32[]{:S(2)}, u32[]{:S(2)}) %collective-permute-start.1) | collective-permute-done | bytes 65568 | tf_op jit(solution)/shard_map/ppermute | solution.py:430
  43.8 6.2 %collective-permute-start.2 = (bf16[256,128]{1,0:T(8,128)(2,1)S(1)}, bf16[256,128]{1,0:T(8,128)(2,1)S(1)}, u32[]{:S(2)}, u32[]{:S(2)}) collective-permute-start(bf16[256,128]{1,0:T(8,128)(2,1)S(1)} %add_convert_fusion.2), channel_id=1, source_target_pairs={{0,192},{16,208},{32,224},{48,240},{64,128},{80,144},{96,160},{112... | collective-permute-start | bytes 196616 | tf_op jit(solution)/shard_map/ppermute | solution.py:432
  50.0 0.7 %collective-permute-start.3 = (bf16[256,128]{1,0:T(8,128)(2,1)S(1)}, bf16[256,128]{1,0:T(8,128)(2,1)S(1)}, u32[]{:S(2)}, u32[]{:S(2)}) collective-permute-start(bf16[256,128]{1,0:T(8,128)(2,1)S(1)} %add_convert_fusion.2), channel_id=1, source_target_pairs={{0,32},{16,48},{32,0},{48,16},{64,96},{80,112},{96,64},{112,80},{1... | collective-permute-start | bytes 196616 | tf_op jit(solution)/shard_map/ppermute | solution.py:432
  50.7 2.3 %collective-permute-done.2 = bf16[256,128]{1,0:T(8,128)(2,1)S(1)} collective-permute-done((bf16[256,128]{1,0:T(8,128)(2,1)S(1)}, bf16[256,128]{1,0:T(8,128)(2,1)S(1)}, u32[]{:S(2)}, u32[]{:S(2)}) %collective-permute-start.2) | collective-permute-done | bytes 65568 | tf_op jit(solution)/shard_map/ppermute | solution.py:432
  53.0 4.2 %collective-permute-done.4 = bf16[256,128]{1,0:T(8,128)(2,1)S(1)} collective-permute-done((bf16[256,128]{1,0:T(8,128)(2,1)S(1)}, bf16[256,128]{1,0:T(8,128)(2,1)S(1)}, u32[]{:S(2)}, u32[]{:S(2)}) %collective-permute-start.4) | collective-permute-done | bytes 65568 | tf_op jit(solution)/shard_map/ppermute | solution.py:432
  57.3 3.3 %collective-permute-start.5 = (bf16[2,256,128]{2,1,0:T(8,128)(2,1)S(1)}, bf16[2,256,128]{2,1,0:T(8,128)(2,1)S(1)}, u32[]{:S(2)}, u32[]{:S(2)}) collective-permute-start(bf16[2,256,128]{2,1,0:T(8,128)(2,1)S(1)} %maximum_select_fusion.1), channel_id=1, source_target_pairs={{0,16},{16,0},{32,48},{48,32},{64,80},{80,64},{96,112},{112,96},{1... | collective-permute-start | bytes 393224 | tf_op jit(solution)/shard_map/ppermute | solution.py:437
  60.7 5.5 %apply.1 = bf16[2,32,32,256]{3,2,1,0:T(8,128)(2,1)} custom-call(bf16[32,144,128]{2,1,0:T(8,128)(2,1)S(1)} %all-to-all-done.1.returned_ref.overlap_ref, bf16[32,144,128]{2,1,0:T(8,128)(2,1)S(1)} %all-to-all-done.1.returned_ref.overlap_ref, bf16[2,32,32,256]{3,2,1,0:T(8,128)(2,1)S(1)} %copy-done.3, bf16[5,32,32,128]{3,2,1,0:T(8,128)(2,1)} %copy-done.5, ...), custom_call_target="tpu_custom_call" | custom-call | flops 4000000000 | bytes 4000000 | tf_op jit(solution)/shard_map/apply/pallas_call | solution.py:438
  66.3 0.8 %convert.11 = f32[8,128,128]{2,1,0:T(8,128)} convert(bf16[8,128,128]{2,1,0:T(8,128)(2,1)S(1)} %bitcast.19) | non-fusion elementwise | flops 131072 | bytes 786432 | tf_op jit(solution)/shard_map/convert_element_type | solution.py:464
  (46 shorter events, 0.5 us)
Async XLA Ops:
  0.6 17.0 %copy-start = (f32[8,128,128]{2,1,0:T(8,128)S(1)}, f32[8,128,128]{2,1,0:T(8,128)}, u32[]{:S(2)}) copy-start(f32[8,128,128]{2,1,0:T(8,128)} %param.15) | copy-start | bytes 1572868
  4.0 7.6 %copy-start.13 = (f32[8,3]{0,1:T(4,128)S(1)}, f32[8,3]{0,1:T(4,128)}, u32[]{:S(2)}) copy-start(f32[8,3]{0,1:T(4,128)} %param.18) | copy-start | bytes 292
  4.0 8.1 %copy-start.6 = (s32[32]{0:T(128)S(1)}, s32[32]{0:T(128)}, u32[]{:S(2)}) copy-start(s32[32]{0:T(128)} %atom_ref.1) | copy-start | bytes 388
  4.1 8.1 %copy-start.7 = (s32[32]{0:T(128)S(1)}, s32[32]{0:T(128)}, u32[]{:S(2)}) copy-start(s32[32]{0:T(128)} %kind_ref.1) | copy-start | bytes 388
  4.1 8.1 %copy-start.8 = (f32[32]{0:T(128)S(1)}, f32[32]{0:T(128)}, u32[]{:S(2)}) copy-start(f32[32]{0:T(128)} %coupling_ref) | copy-start | bytes 388
  4.1 8.9 %copy-start.1 = (bf16[4,32,32,128]{3,2,1,0:T(8,128)(2,1)S(1)}, bf16[4,32,32,128]{3,2,1,0:T(8,128)(2,1)}, u32[]{:S(2)}) copy-start(bf16[4,32,32,128]{3,2,1,0:T(8,128)(2,1)} %channels_ref.1) | copy-start | bytes 3145732
  4.1 24.6 %all-to-all-start = ((bf16[32,4,32,128]{3,2,1,0:T(8,128)(2,1)}), bf16[32,4,32,128]{3,2,1,0:T(8,128)(2,1)S(1)}, u32[]{:S(2)}, u32[]{:S(2)}) async-start(bf16[32,4,32,128]{3,2,1,0:T(8,128)(2,1)} %spread.1), calls=%async_computation | async-start | bytes 2097152 | tf_op jit(solution)/shard_map/all_to_all | solution.py:346
  12.9 1.2 %copy-start.2 = (bf16[2,32,32,256]{3,2,1,0:T(8,128)(2,1)S(1)}, bf16[2,32,32,256]{3,2,1,0:T(8,128)(2,1)}, u32[]{:S(2)}) copy-start(bf16[2,32,32,256]{3,2,1,0:T(8,128)(2,1)} %orbitals_ref.5) | copy-start | bytes 3145732
  14.2 1.0 %copy-start.4 = (s32[32,32,128]{2,1,0:T(8,128)S(1)}, s32[32,32,128]{2,1,0:T(8,128)}, u32[]{:S(2)}) copy-start(s32[32,32,128]{2,1,0:T(8,128)} %mask_ref.3) | copy-start | bytes 1572868
  15.2 13.5 %copy-start.11 = (bf16[256,256]{1,0:T(8,128)(2,1)S(1)}, bf16[256,256]{1,0:T(8,128)(2,1)}, u32[]{:S(2)}) copy-start(bf16[256,256]{1,0:T(8,128)(2,1)} %constant.72.clone.fwd_y_ref) | copy-start | bytes 393220
  15.2 13.5 %copy-start.12 = (bf16[256,256]{1,0:T(8,128)(2,1)S(1)}, bf16[256,256]{1,0:T(8,128)(2,1)}, u32[]{:S(2)}) copy-start(bf16[256,256]{1,0:T(8,128)(2,1)} %constant.70.clone.inv_y_ref) | copy-start | bytes 393220
  16.5 1.1 %copy-start.5 = (bf16[5,32,32,128]{3,2,1,0:T(8,128)(2,1)}, bf16[5,32,32,128]{3,2,1,0:T(8,128)(2,1)S(1)}, u32[]{:S(2)}) copy-start(bf16[5,32,32,128]{3,2,1,0:T(8,128)(2,1)S(1)} %get-tuple-element.24.profile_ref) | copy-start | bytes 3932164
  32.9 4.3 %collective-permute-start = (bf16[256,128]{1,0:T(8,128)(2,1)S(1)}, bf16[256,128]{1,0:T(8,128)(2,1)S(1)}, u32[]{:S(2)}, u32[]{:S(2)}) collective-permute-start(bf16[256,128]{1,0:T(8,128)(2,1)S(1)} %get-tuple-element.22), channel_id=1, source_target_pairs={{0,32},{16,48},{32,0},{48,16},{64,96},{80,112},{96,64},{112,80},{1... | collective-permute-start | bytes 196616 | tf_op jit(solution)/shard_map/ppermute | solution.py:428
  33.0 27.7 %all-to-all-start.1 = ((bf16[32,144,128]{2,1,0:T(8,128)(2,1)}), bf16[32,144,128]{2,1,0:T(8,128)(2,1)S(1)}, u32[]{:S(2)}, u32[]{:S(2)}) async-start(bf16[32,144,128]{2,1,0:T(8,128)(2,1)} %get-tuple-element.23), calls=%async_computation.1 | async-start | bytes 2359296 | tf_op jit(solution)/shard_map/all_to_all | solution.py:346
  36.9 23.8 %copy-start.3 = (bf16[2,32,32,256]{3,2,1,0:T(8,128)(2,1)S(1)}, bf16[2,32,32,256]{3,2,1,0:T(8,128)(2,1)}, u32[]{:S(2)}) copy-start(bf16[2,32,32,256]{3,2,1,0:T(8,128)(2,1)} %orbitals_ref.5) | copy-start | bytes 3145732
  37.0 23.8 %copy-start.9 = (f32[2]{0:T(128)S(1)}, f32[2]{0:T(128)}, u32[]{:S(2)}) copy-start(f32[2]{0:T(128)} %weight_ref.3) | copy-start | bytes 28
  37.0 23.8 %copy-start.10 = (bf16[128,512]{1,0:T(8,128)(2,1)S(1)}, bf16[128,512]{1,0:T(8,128)(2,1)}, u32[]{:S(2)}) copy-start(bf16[128,512]{1,0:T(8,128)(2,1)} %constant.73.clone.table_ref) | copy-start | bytes 393220
  37.2 6.6 %collective-permute-start.1 = (bf16[256,128]{1,0:T(8,128)(2,1)S(1)}, bf16[256,128]{1,0:T(8,128)(2,1)S(1)}, u32[]{:S(2)}, u32[]{:S(2)}) collective-permute-start(bf16[256,128]{1,0:T(8,128)(2,1)S(1)} %add_convert_fusion.3), channel_id=1, source_target_pairs={{0,64},{16,80},{32,96},{48,112},{64,0},{80,16},{96,32},{112,48},{1... | collective-permute-start | bytes 196616 | tf_op jit(solution)/shard_map/ppermute | solution.py:430
  43.8 9.2 %collective-permute-start.2 = (bf16[256,128]{1,0:T(8,128)(2,1)S(1)}, bf16[256,128]{1,0:T(8,128)(2,1)S(1)}, u32[]{:S(2)}, u32[]{:S(2)}) collective-permute-start(bf16[256,128]{1,0:T(8,128)(2,1)S(1)} %add_convert_fusion.2), channel_id=1, source_target_pairs={{0,192},{16,208},{32,224},{48,240},{64,128},{80,144},{96,160},{112... | collective-permute-start | bytes 196616 | tf_op jit(solution)/shard_map/ppermute | solution.py:432
  50.0 7.3 %collective-permute-start.4 = (bf16[256,128]{1,0:T(8,128)(2,1)S(1)}, bf16[256,128]{1,0:T(8,128)(2,1)S(1)}, u32[]{:S(2)}, u32[]{:S(2)}) collective-permute-start(bf16[256,128]{1,0:T(8,128)(2,1)S(1)} %add_convert_fusion.2), channel_id=1, source_target_pairs={{0,224},{16,240},{32,192},{48,208},{64,160},{80,176},{96,128},{112... | collective-permute-start | bytes 196616 | tf_op jit(solution)/shard_map/ppermute | solution.py:432
  50.0 7.3 %collective-permute-start.3 = (bf16[256,128]{1,0:T(8,128)(2,1)S(1)}, bf16[256,128]{1,0:T(8,128)(2,1)S(1)}, u32[]{:S(2)}, u32[]{:S(2)}) collective-permute-start(bf16[256,128]{1,0:T(8,128)(2,1)S(1)} %add_convert_fusion.2), channel_id=1, source_target_pairs={{0,32},{16,48},{32,0},{48,16},{64,96},{80,112},{96,64},{112,80},{1... | collective-permute-start | bytes 196616 | tf_op jit(solution)/shard_map/ppermute | solution.py:432
  57.3 8.9 %collective-permute-start.5 = (bf16[2,256,128]{2,1,0:T(8,128)(2,1)S(1)}, bf16[2,256,128]{2,1,0:T(8,128)(2,1)S(1)}, u32[]{:S(2)}, u32[]{:S(2)}) collective-permute-start(bf16[2,256,128]{2,1,0:T(8,128)(2,1)S(1)} %maximum_select_fusion.1), channel_id=1, source_target_pairs={{0,16},{16,0},{32,48},{48,32},{64,80},{80,64},{96,112},{112,96},{1... | collective-permute-start | bytes 393224 | tf_op jit(solution)/shard_map/ppermute | solution.py:437

commit v12 on v11

--- a/solution.py
+++ b/solution.py
@@ -134,13 +134,23 @@
     mine_ref,
     theirs_ref,
     out_ref,
+    tables_ref,
+    chunks_ref,
+    loads,
+    stores,
 ):
     planes, length = potential_ref.shape[:2]
     parts = 4
     places = 4 * parts
+    tables = [pltpu.make_async_copy(z_ref.at[i], tables_ref.at[i], loads.at[i]) for i in range(2)]
+    for table in tables:
+        table.start()
     bands = arrived_ref.shape[0] // places
     rows = arrived_ref.shape[1] // planes
     span = rows // 2
+    for place in range(out_ref.shape[0]):
+        chunks_ref[place, planes * rows :, :] = overlap_ref[...]
+    tables[0].wait()
     halfway = []
     for b in range(bands):
         columns = jnp.concatenate(
@@ -150,7 +160,7 @@
             ],
             axis=0,
         )
-        halfway.append(dot(columns, z_ref[0]).astype(bf16))
+        halfway.append(dot(columns, tables_ref[0]).astype(bf16))
     fields = []
     for b in range(bands):
         for x in range(planes):
@@ -171,6 +181,8 @@
             potential = jnp.concatenate([potential, potential], axis=0)
             scaled.append((potential * fields[b * planes + x]).astype(bf16))
     folded = [dot(fwd_y_ref[...], block).astype(bf16) for block in scaled]
+    tables[1].wait()
+    copies = []
     for b in range(bands):
         back = []
         for block in folded[b * planes : (b + 1) * planes]:
@@ -178,24 +190,27 @@
             back.append(
                 jnp.concatenate([real[:, :length], imag[:, :length], real[:, length:], imag[:, length:]], axis=1)
             )
-        back = dot(jnp.concatenate(back, axis=0), z_ref[1]).astype(bf16)
+        back = dot(jnp.concatenate(back, axis=0), tables_ref[1]).astype(bf16)
         for x in range(planes):
             for sy in range(parts):
                 for half in range(2):
                     start = x * length + sy * rows + half * span
                     row = (half * planes + x) * span
                     for sz in range(4):
-                        out_ref[b * places + sy * 4 + sz, row : row + span, :] = back[
+                        chunks_ref[b * places + sy * 4 + sz, row : row + span, :] = back[
                             start : start + span, sz * 128 : sz * 128 + 128
                         ]
-    for place in range(out_ref.shape[0]):
-        out_ref[place, planes * rows :, :] = overlap_ref[...]
+        here = pl.ds(b * places, places)
+        copies.append(pltpu.make_async_copy(chunks_ref.at[here], out_ref.at[here], stores.at[b]))
+        copies[b].start()
     upper = lax.axis_index("band") // 2 % 2
     half = planes // 2
     for x in range(half):
         here = slice(x * length, (x + 1) * length)
         mine_ref[here, :] = jnp.where(upper == 0, density[x], density[half + x])
         theirs_ref[here, :] = jnp.where(upper == 0, density[half + x], density[x])
+    for copy in copies:
+        copy.wait()
 
 
 def apply_kernel(
@@ -405,19 +420,25 @@
             whole(bands * places, rows, 128),
             whole(planes, length, length),
             whole(2 * atoms, 128),
-            whole(2, 4 * length, 4 * length),
+            pl.BlockSpec(memory_space=pl.ANY),
             whole(2 * length, 2 * length),
             whole(2 * length, 2 * length),
         ],
         out_specs=[
             whole(half, length),
             whole(half, length),
-            whole(bands * places, rows + 2 * atoms, 128),
+            pl.BlockSpec(memory_space=pl.ANY),
         ],
         out_shape=[
             jax.ShapeDtypeStruct((half, length), bf16),
             jax.ShapeDtypeStruct((half, length), bf16),
             jax.ShapeDtypeStruct((bands * places, rows + 2 * atoms, 128), bf16),
+        ],
+        scratch_shapes=[
+            pltpu.VMEM((2, 4 * length, 4 * length), bf16),
+            pltpu.VMEM((bands * places, rows + 2 * atoms, 128), bf16),
+            pltpu.SemaphoreType.DMA((2,)),
+            pltpu.SemaphoreType.DMA((bands,)),
         ],
         compiler_params=pltpu.CompilerParams(vmem_limit_bytes=53248 * 1024),
         cost_estimate=cost(6),

time: 67.6 us -> 67.5 us (level)
  no operation moved by 1% of the time
where the time goes in v12:
time: 67.5 us; the launch traced here: 67 us
  starting transfers between devices  25.2 us (37%)
  waiting for transfers between devices  21 us (31%)
  Pallas kernels  14.8 us (22%)
  local copies, waits for them, and re-layouts  3.69 us (5%)
  other arithmetic  1.36 us (2%)
  between operations  0.94 us (1%)
    all_to_all x2, starting transfers between devices, exchange(): lax.all_to_all(chunks, ('band', 'gy', 'gz'), split_axis=0, concat_axis=0,...  11.4 us
    all_to_all x2, waiting for transfers between devices, exchange(): lax.all_to_all(chunks, ('band', 'gy', 'gz'), split_axis=0, concat_axis=0,...  11.1 us
    ppermute x3, starting transfers between devices, shards(): lax.ppermute(mine, 'band', partners('band', d * bands))  6.92 us
    ppermute x3, waiting for transfers between devices, shards(): lax.ppermute(mine, 'band', partners('band', d * bands))  6.55 us
    pallas_call x1, Pallas kernels, shards(): pl.pallas_call(apply_kernel, grid=(steps,), in_specs=[pl.BlockSpec((bands...  5.52 us
    pallas_call x1, Pallas kernels, shards(): pl.pallas_call(field_kernel, grid=(1,), in_specs=[whole(bands * places, r...  4 us
    pallas_call x1, Pallas kernels, shards(): pl.pallas_call(spread_kernel, grid=(steps,), in_specs=[orbitals_spec, mas...  3.4 us
    unnamed x29, local copies, waits for them, and re-layouts  3.4 us
  transfers between devices with their start and end apart: 8, of which 5 were waited for; matrix products, arithmetic and copies ran while one was open for 1% of the time, Pallas kernels for 11%

profile of v12, /device:TPU:32, one launch (start us, length us, event | category | flops | bytes accessed | tf_op | source)
XLA Modules:
  0.0 67.0 jit_solution(9254350979252373878)
XLA Ops:
  0.6 3.4 %spread.1 = bf16[32,4,32,128]{3,2,1,0:T(8,128)(2,1)} custom-call(bf16[2,32,32,256]{3,2,1,0:T(8,128)(2,1)} %orbitals_ref.5, s32[32,32,128]{2,1,0:T(8,128)} %mask_ref.3, f32[2]{0:T(128)} %weight_ref.3, bf16[256,256]{1,0:T(8,128)(2,1)} %constant.69.clone.table_ref), custom_call_target="tpu_custom_call" | custom-call | flops 4000000000 | bytes 4000000 | tf_op jit(solution)/shard_map/spread/pallas_call | solution.py:365
  4.1 7.5 %all-to-all-start = ((bf16[32,4,32,128]{3,2,1,0:T(8,128)(2,1)}), bf16[32,4,32,128]{3,2,1,0:T(8,128)(2,1)S(1)}, u32[]{:S(2)}, u32[]{:S(2)}) async-start(bf16[32,4,32,128]{3,2,1,0:T(8,128)(2,1)} %spread.1), calls=%async_computation | async-start | bytes 2097152 | tf_op jit(solution)/shard_map/all_to_all | solution.py:361
  11.7 0.1 add_convert_fusion.4
  11.9 0.1 add.71
  12.0 0.1 sub.25
  12.2 0.6 strength.1.strength_ref
  13.0 1.2 %copy-done.2 = bf16[2,32,32,256]{3,2,1,0:T(8,128)(2,1)S(1)} copy-done((bf16[2,32,32,256]{3,2,1,0:T(8,128)(2,1)S(1)}, bf16[2,32,32,256]{3,2,1,0:T(8,128)(2,1)}, u32[]{:S(2)}) %copy-start.2) | copy-done | bytes 1048600
  14.2 1.0 %copy-done.4 = s32[32,32,128]{2,1,0:T(8,128)S(1)} copy-done((s32[32,32,128]{2,1,0:T(8,128)S(1)}, s32[32,32,128]{2,1,0:T(8,128)}, u32[]{:S(2)}) %copy-start.4) | copy-done | bytes 524312
  15.2 1.3 %overlap.1 = (bf16[16,128]{1,0:T(8,128)(2,1)S(1)}, bf16[5,32,32,128]{3,2,1,0:T(8,128)(2,1)S(1)}) custom-call(bf16[2,32,32,256]{3,2,1,0:T(8,128)(2,1)S(1)} %copy-done.2, s32[32,32,128]{2,1,0:T(8,128)S(1)} %copy-done.4, bf16[4,32,32,128]{3,2,1,0:T(8,128)(2,1)S(1)} %copy-done.1, bf16[16,1024]{1,0:T(8,128)(2,1)S(1)} %constant_dynamic-update-slice_fusion.phase_ref, ...), custom_call_target="tpu_custom_call" | custom-call | flops 100000000 | bytes 100000 | tf_op jit(solution)/shard_map/overlap/pallas_call | solution.py:398
  16.5 1.1 %copy-done.5 = bf16[5,32,32,128]{3,2,1,0:T(8,128)(2,1)} copy-done((bf16[5,32,32,128]{3,2,1,0:T(8,128)(2,1)}, bf16[5,32,32,128]{3,2,1,0:T(8,128)(2,1)S(1)}, u32[]{:S(2)}) %copy-start.5) | copy-done | bytes 1310744
  17.6 11.1 %all-to-all-done = bf16[32,4,32,128]{3,2,1,0:T(8,128)(2,1)S(1)} async-done(((bf16[32,4,32,128]{3,2,1,0:T(8,128)(2,1)}), bf16[32,4,32,128]{3,2,1,0:T(8,128)(2,1)S(1)}, u32[]{:S(2)}, u32[]{:S(2)}) %all-to-all-start) | async-done | bytes 1048608 | tf_op jit(solution)/shard_map/all_to_all | solution.py:361
  28.7 4.0 %field.1 = (bf16[256,128]{1,0:T(8,128)(2,1)S(1)}, bf16[256,128]{1,0:T(8,128)(2,1)S(1)}, bf16[32,144,128]{2,1,0:T(8,128)(2,1)}) custom-call(bf16[32,128,128]{2,1,0:T(8,128)(2,1)S(1)} %bitcast.18, f32[4,128,128]{2,1,0:T(8,128)S(1)} %constant_dynamic-slice_fusion.potential_ref, bf16[16,128]{1,0:T(8,128)(2,1)S(1)} %get-tuple-element.20.overlap_ref, ...), custom_call_target="tpu_custom_call" | custom-call | flops 6000000000 | bytes 6000000 | tf_op jit(solution)/shard_map/field/pallas_call | solution.py:416
  32.7 0.2 collective-permute-start
  32.9 3.9 %all-to-all-start.1 = ((bf16[32,144,128]{2,1,0:T(8,128)(2,1)}), bf16[32,144,128]{2,1,0:T(8,128)(2,1)S(1)}, u32[]{:S(2)}, u32[]{:S(2)}) async-start(bf16[32,144,128]{2,1,0:T(8,128)(2,1)} %get-tuple-element.23), calls=%async_computation.1 | async-start | bytes 2359296 | tf_op jit(solution)/shard_map/all_to_all | solution.py:361
  36.9 0.2 collective-permute-done
  37.1 3.4 %collective-permute-start.1 = (bf16[256,128]{1,0:T(8,128)(2,1)S(1)}, bf16[256,128]{1,0:T(8,128)(2,1)S(1)}, u32[]{:S(2)}, u32[]{:S(2)}) collective-permute-start(bf16[256,128]{1,0:T(8,128)(2,1)S(1)} %add_convert_fusion.3), channel_id=1, source_target_pairs={{0,64},{16,80},{32,96},{48,112},{64,0},{80,16},{96,32},{112,48},{1... | collective-permute-start | bytes 196616 | tf_op jit(solution)/shard_map/ppermute | solution.py:451
  40.4 3.2 %collective-permute-done.1 = bf16[256,128]{1,0:T(8,128)(2,1)S(1)} collective-permute-done((bf16[256,128]{1,0:T(8,128)(2,1)S(1)}, bf16[256,128]{1,0:T(8,128)(2,1)S(1)}, u32[]{:S(2)}, u32[]{:S(2)}) %collective-permute-start.1) | collective-permute-done | bytes 65568 | tf_op jit(solution)/shard_map/ppermute | solution.py:451
  43.7 6.2 %collective-permute-start.2 = (bf16[256,128]{1,0:T(8,128)(2,1)S(1)}, bf16[256,128]{1,0:T(8,128)(2,1)S(1)}, u32[]{:S(2)}, u32[]{:S(2)}) collective-permute-start(bf16[256,128]{1,0:T(8,128)(2,1)S(1)} %add_convert_fusion.2), channel_id=1, source_target_pairs={{0,192},{16,208},{32,224},{48,240},{64,128},{80,144},{96,160},{112... | collective-permute-start | bytes 196616 | tf_op jit(solution)/shard_map/ppermute | solution.py:453
  49.9 0.7 %collective-permute-start.3 = (bf16[256,128]{1,0:T(8,128)(2,1)S(1)}, bf16[256,128]{1,0:T(8,128)(2,1)S(1)}, u32[]{:S(2)}, u32[]{:S(2)}) collective-permute-start(bf16[256,128]{1,0:T(8,128)(2,1)S(1)} %add_convert_fusion.2), channel_id=1, source_target_pairs={{0,32},{16,48},{32,0},{48,16},{64,96},{80,112},{96,64},{112,80},{1... | collective-permute-start | bytes 196616 | tf_op jit(solution)/shard_map/ppermute | solution.py:453
  50.6 2.3 %collective-permute-done.2 = bf16[256,128]{1,0:T(8,128)(2,1)S(1)} collective-permute-done((bf16[256,128]{1,0:T(8,128)(2,1)S(1)}, bf16[256,128]{1,0:T(8,128)(2,1)S(1)}, u32[]{:S(2)}, u32[]{:S(2)}) %collective-permute-start.2) | collective-permute-done | bytes 65568 | tf_op jit(solution)/shard_map/ppermute | solution.py:453
  52.9 4.2 %collective-permute-done.4 = bf16[256,128]{1,0:T(8,128)(2,1)S(1)} collective-permute-done((bf16[256,128]{1,0:T(8,128)(2,1)S(1)}, bf16[256,128]{1,0:T(8,128)(2,1)S(1)}, u32[]{:S(2)}, u32[]{:S(2)}) %collective-permute-start.4) | collective-permute-done | bytes 65568 | tf_op jit(solution)/shard_map/ppermute | solution.py:453
  57.2 3.3 %collective-permute-start.5 = (bf16[2,256,128]{2,1,0:T(8,128)(2,1)S(1)}, bf16[2,256,128]{2,1,0:T(8,128)(2,1)S(1)}, u32[]{:S(2)}, u32[]{:S(2)}) collective-permute-start(bf16[2,256,128]{2,1,0:T(8,128)(2,1)S(1)} %maximum_select_fusion.1), channel_id=1, source_target_pairs={{0,16},{16,0},{32,48},{48,32},{64,80},{80,64},{96,112},{112,96},{1... | collective-permute-start | bytes 393224 | tf_op jit(solution)/shard_map/ppermute | solution.py:458
  60.6 5.5 %apply.1 = bf16[2,32,32,256]{3,2,1,0:T(8,128)(2,1)} custom-call(bf16[32,144,128]{2,1,0:T(8,128)(2,1)S(1)} %all-to-all-done.1.returned_ref.overlap_ref, bf16[32,144,128]{2,1,0:T(8,128)(2,1)S(1)} %all-to-all-done.1.returned_ref.overlap_ref, bf16[2,32,32,256]{3,2,1,0:T(8,128)(2,1)S(1)} %copy-done.3, bf16[5,32,32,128]{3,2,1,0:T(8,128)(2,1)} %copy-done.5, ...), custom_call_target="tpu_custom_call" | custom-call | flops 4000000000 | bytes 4000000 | tf_op jit(solution)/shard_map/apply/pallas_call | solution.py:459
  66.2 0.8 %convert.11 = f32[8,128,128]{2,1,0:T(8,128)} convert(bf16[8,128,128]{2,1,0:T(8,128)(2,1)S(1)} %bitcast.19) | non-fusion elementwise | flops 131072 | bytes 786432 | tf_op jit(solution)/shard_map/convert_element_type | solution.py:485
  (46 shorter events, 0.5 us)
Async XLA Ops:
  0.6 17.0 %copy-start = (f32[8,128,128]{2,1,0:T(8,128)S(1)}, f32[8,128,128]{2,1,0:T(8,128)}, u32[]{:S(2)}) copy-start(f32[8,128,128]{2,1,0:T(8,128)} %param.15) | copy-start | bytes 1572868
  4.0 7.6 %copy-start.13 = (f32[8,3]{0,1:T(4,128)S(1)}, f32[8,3]{0,1:T(4,128)}, u32[]{:S(2)}) copy-start(f32[8,3]{0,1:T(4,128)} %param.18) | copy-start | bytes 292
  4.0 8.1 %copy-start.6 = (s32[32]{0:T(128)S(1)}, s32[32]{0:T(128)}, u32[]{:S(2)}) copy-start(s32[32]{0:T(128)} %atom_ref.1) | copy-start | bytes 388
  4.1 8.1 %copy-start.7 = (s32[32]{0:T(128)S(1)}, s32[32]{0:T(128)}, u32[]{:S(2)}) copy-start(s32[32]{0:T(128)} %kind_ref.1) | copy-start | bytes 388
  4.1 8.1 %copy-start.8 = (f32[32]{0:T(128)S(1)}, f32[32]{0:T(128)}, u32[]{:S(2)}) copy-start(f32[32]{0:T(128)} %coupling_ref) | copy-start | bytes 388
  4.1 8.9 %copy-start.1 = (bf16[4,32,32,128]{3,2,1,0:T(8,128)(2,1)S(1)}, bf16[4,32,32,128]{3,2,1,0:T(8,128)(2,1)}, u32[]{:S(2)}) copy-start(bf16[4,32,32,128]{3,2,1,0:T(8,128)(2,1)} %channels_ref.1) | copy-start | bytes 3145732
  4.1 24.6 %all-to-all-start = ((bf16[32,4,32,128]{3,2,1,0:T(8,128)(2,1)}), bf16[32,4,32,128]{3,2,1,0:T(8,128)(2,1)S(1)}, u32[]{:S(2)}, u32[]{:S(2)}) async-start(bf16[32,4,32,128]{3,2,1,0:T(8,128)(2,1)} %spread.1), calls=%async_computation | async-start | bytes 2097152 | tf_op jit(solution)/shard_map/all_to_all | solution.py:361
  12.9 1.2 %copy-start.2 = (bf16[2,32,32,256]{3,2,1,0:T(8,128)(2,1)S(1)}, bf16[2,32,32,256]{3,2,1,0:T(8,128)(2,1)}, u32[]{:S(2)}) copy-start(bf16[2,32,32,256]{3,2,1,0:T(8,128)(2,1)} %orbitals_ref.5) | copy-start | bytes 3145732
  14.2 1.0 %copy-start.4 = (s32[32,32,128]{2,1,0:T(8,128)S(1)}, s32[32,32,128]{2,1,0:T(8,128)}, u32[]{:S(2)}) copy-start(s32[32,32,128]{2,1,0:T(8,128)} %mask_ref.3) | copy-start | bytes 1572868
  15.2 13.5 %copy-start.11 = (bf16[256,256]{1,0:T(8,128)(2,1)S(1)}, bf16[256,256]{1,0:T(8,128)(2,1)}, u32[]{:S(2)}) copy-start(bf16[256,256]{1,0:T(8,128)(2,1)} %constant.72.clone.fwd_y_ref) | copy-start | bytes 393220
  15.2 13.5 %copy-start.12 = (bf16[256,256]{1,0:T(8,128)(2,1)S(1)}, bf16[256,256]{1,0:T(8,128)(2,1)}, u32[]{:S(2)}) copy-start(bf16[256,256]{1,0:T(8,128)(2,1)} %constant.70.clone.inv_y_ref) | copy-start | bytes 393220
  16.5 1.1 %copy-start.5 = (bf16[5,32,32,128]{3,2,1,0:T(8,128)(2,1)}, bf16[5,32,32,128]{3,2,1,0:T(8,128)(2,1)S(1)}, u32[]{:S(2)}) copy-start(bf16[5,32,32,128]{3,2,1,0:T(8,128)(2,1)S(1)} %get-tuple-element.24.profile_ref) | copy-start | bytes 3932164
  32.7 4.4 %collective-permute-start = (bf16[256,128]{1,0:T(8,128)(2,1)S(1)}, bf16[256,128]{1,0:T(8,128)(2,1)S(1)}, u32[]{:S(2)}, u32[]{:S(2)}) collective-permute-start(bf16[256,128]{1,0:T(8,128)(2,1)S(1)} %get-tuple-element.22), channel_id=1, source_target_pairs={{0,32},{16,48},{32,0},{48,16},{64,96},{80,112},{96,64},{112,80},{1... | collective-permute-start | bytes 196616 | tf_op jit(solution)/shard_map/ppermute | solution.py:449
  32.9 27.7 %all-to-all-start.1 = ((bf16[32,144,128]{2,1,0:T(8,128)(2,1)}), bf16[32,144,128]{2,1,0:T(8,128)(2,1)S(1)}, u32[]{:S(2)}, u32[]{:S(2)}) async-start(bf16[32,144,128]{2,1,0:T(8,128)(2,1)} %get-tuple-element.23), calls=%async_computation.1 | async-start | bytes 2359296 | tf_op jit(solution)/shard_map/all_to_all | solution.py:361
  36.8 23.8 %copy-start.3 = (bf16[2,32,32,256]{3,2,1,0:T(8,128)(2,1)S(1)}, bf16[2,32,32,256]{3,2,1,0:T(8,128)(2,1)}, u32[]{:S(2)}) copy-start(bf16[2,32,32,256]{3,2,1,0:T(8,128)(2,1)} %orbitals_ref.5) | copy-start | bytes 3145732
  36.8 23.8 %copy-start.9 = (f32[2]{0:T(128)S(1)}, f32[2]{0:T(128)}, u32[]{:S(2)}) copy-start(f32[2]{0:T(128)} %weight_ref.3) | copy-start | bytes 28
  36.9 23.8 %copy-start.10 = (bf16[128,512]{1,0:T(8,128)(2,1)S(1)}, bf16[128,512]{1,0:T(8,128)(2,1)}, u32[]{:S(2)}) copy-start(bf16[128,512]{1,0:T(8,128)(2,1)} %constant.73.clone.table_ref) | copy-start | bytes 393220
  37.1 6.6 %collective-permute-start.1 = (bf16[256,128]{1,0:T(8,128)(2,1)S(1)}, bf16[256,128]{1,0:T(8,128)(2,1)S(1)}, u32[]{:S(2)}, u32[]{:S(2)}) collective-permute-start(bf16[256,128]{1,0:T(8,128)(2,1)S(1)} %add_convert_fusion.3), channel_id=1, source_target_pairs={{0,64},{16,80},{32,96},{48,112},{64,0},{80,16},{96,32},{112,48},{1... | collective-permute-start | bytes 196616 | tf_op jit(solution)/shard_map/ppermute | solution.py:451
  43.7 9.2 %collective-permute-start.2 = (bf16[256,128]{1,0:T(8,128)(2,1)S(1)}, bf16[256,128]{1,0:T(8,128)(2,1)S(1)}, u32[]{:S(2)}, u32[]{:S(2)}) collective-permute-start(bf16[256,128]{1,0:T(8,128)(2,1)S(1)} %add_convert_fusion.2), channel_id=1, source_target_pairs={{0,192},{16,208},{32,224},{48,240},{64,128},{80,144},{96,160},{112... | collective-permute-start | bytes 196616 | tf_op jit(solution)/shard_map/ppermute | solution.py:453
  49.9 7.3 %collective-permute-start.4 = (bf16[256,128]{1,0:T(8,128)(2,1)S(1)}, bf16[256,128]{1,0:T(8,128)(2,1)S(1)}, u32[]{:S(2)}, u32[]{:S(2)}) collective-permute-start(bf16[256,128]{1,0:T(8,128)(2,1)S(1)} %add_convert_fusion.2), channel_id=1, source_target_pairs={{0,224},{16,240},{32,192},{48,208},{64,160},{80,176},{96,128},{112... | collective-permute-start | bytes 196616 | tf_op jit(solution)/shard_map/ppermute | solution.py:453
  49.9 7.3 %collective-permute-start.3 = (bf16[256,128]{1,0:T(8,128)(2,1)S(1)}, bf16[256,128]{1,0:T(8,128)(2,1)S(1)}, u32[]{:S(2)}, u32[]{:S(2)}) collective-permute-start(bf16[256,128]{1,0:T(8,128)(2,1)S(1)} %add_convert_fusion.2), channel_id=1, source_target_pairs={{0,32},{16,48},{32,0},{48,16},{64,96},{80,112},{96,64},{112,80},{1... | collective-permute-start | bytes 196616 | tf_op jit(solution)/shard_map/ppermute | solution.py:453
  57.2 8.9 %collective-permute-start.5 = (bf16[2,256,128]{2,1,0:T(8,128)(2,1)S(1)}, bf16[2,256,128]{2,1,0:T(8,128)(2,1)S(1)}, u32[]{:S(2)}, u32[]{:S(2)}) collective-permute-start(bf16[2,256,128]{2,1,0:T(8,128)(2,1)S(1)} %maximum_select_fusion.1), channel_id=1, source_target_pairs={{0,16},{16,0},{32,48},{48,32},{64,80},{80,64},{96,112},{112,96},{1... | collective-permute-start | bytes 393224 | tf_op jit(solution)/shard_map/ppermute | solution.py:458

commit v13 on v12

--- a/solution.py
+++ b/solution.py
@@ -234,8 +234,13 @@
     atoms = wave_ref.shape[0] // 2
 
     work_ref[...] = returned_ref[...].astype(f32).reshape(work_ref.shape)
-    planes = [work_ref[pl.ds(y, length, stride=rows_y), :].astype(bf16) for y in range(rows_y)]
-    local = [dot_tn(jnp.concatenate(planes[y : y + 2], axis=1), table_ref[...]) for y in range(0, rows_y, 2)]
+    lane = lax.broadcasted_iota(jnp.int32, (length, 128), 1)
+    local = []
+    for y in range(0, rows_y, 2):
+        even, odd = [work_ref[pl.ds(row, length, stride=rows_y), :] for row in (y, y + 1)]
+        real = jnp.where(lane < 64, even, pltpu.roll(odd, 64, 1))
+        imag = jnp.where(lane < 64, pltpu.roll(even, 64, 1), odd)
+        local.append(dot_tn(jnp.concatenate([real, imag], axis=0).astype(bf16), table_ref[...]))
 
     @pl.when(step == 0)
     def factors():
@@ -268,8 +273,7 @@
     energy = kinetic_scale * 0.5 * energy.astype(f32)
     scale = 1.0 / root_weights(weight_ref, (2 * rows_z, 1), 0, rows_z)
     for y in range(rows_y):
-        block = local[y // 2][y % 2 * 128 : y % 2 * 128 + 128]
-        both = scale * (block[:64, : 2 * length] + block[64:, 2 * length :])
+        both = scale * local[y // 2][y % 2 * 64 : y % 2 * 64 + 64]
         radials = [profile_ref[c, y].astype(f32) for c in range(kinds + 1)]
         for n in range(2):
             for part in range(2):
@@ -334,7 +338,7 @@
     fwd_z = np.einsum("cslfz,nm->nfzscml", split_forward, pick).reshape(4 * length, 4 * length)
     both_z = rounded(np.stack([inv_z, fwd_z]), 8 * length).reshape(2, 4 * length, 4 * length)
     fwd_y = rounded(forward, 2 * length)
-    fwd_x = rounded(np.einsum("rkcx->xcrk", forward[..., order]), length)
+    fwd_x = rounded(np.einsum("rkcx->cxrk", forward[..., order]), 2 * length)
     first_y = lax.axis_index("gy") * rows_y
     first_z = lax.axis_index("gz") * rows_z
     band = lax.axis_index("band") % bands
@@ -468,7 +472,7 @@
             whole(2 * atoms, length),
             whole(atoms, 128),
             smem_spec,
-            whole(length, 4 * length),
+            whole(2 * length, 2 * length),
         ],
         out_specs=orbitals_spec,
         out_shape=jax.ShapeDtypeStruct(orbitals.shape, bf16),

time: 67.5 us -> 67.5 us (level)
  no operation moved by 1% of the time
where the time goes in v13:
time: 67.5 us; the launch traced here: 67.1 us
  starting transfers between devices  25.2 us (37%)
  waiting for transfers between devices  21 us (31%)
  Pallas kernels  14.8 us (22%)
  local copies, waits for them, and re-layouts  3.69 us (5%)
  other arithmetic  1.36 us (2%)
  between operations  0.94 us (1%)
    all_to_all x2, starting transfers between devices, exchange(): lax.all_to_all(chunks, ('band', 'gy', 'gz'), split_axis=0, concat_axis=0,...  11.4 us
    all_to_all x2, waiting for transfers between devices, exchange(): lax.all_to_all(chunks, ('band', 'gy', 'gz'), split_axis=0, concat_axis=0,...  11.1 us
    ppermute x3, starting transfers between devices, shards(): lax.ppermute(mine, 'band', partners('band', d * bands))  6.92 us
    ppermute x3, waiting for transfers between devices, shards(): lax.ppermute(mine, 'band', partners('band', d * bands))  6.55 us
    pallas_call x1, Pallas kernels, shards(): pl.pallas_call(apply_kernel, grid=(steps,), in_specs=[pl.BlockSpec((bands...  5.57 us
    pallas_call x1, Pallas kernels, shards(): pl.pallas_call(field_kernel, grid=(1,), in_specs=[whole(bands * places, r...  4 us
    pallas_call x1, Pallas kernels, shards(): pl.pallas_call(spread_kernel, grid=(steps,), in_specs=[orbitals_spec, mas...  3.4 us
    unnamed x29, local copies, waits for them, and re-layouts  3.4 us
  transfers between devices with their start and end apart: 8, of which 5 were waited for; matrix products, arithmetic and copies ran while one was open for 1% of the time, Pallas kernels for 11%

profile of v13, /device:TPU:32, one launch (start us, length us, event | category | flops | bytes accessed | tf_op | source)
XLA Modules:
  0.0 67.1 jit_solution(2295206664483343782)
XLA Ops:
  0.6 3.4 %spread.1 = bf16[32,4,32,128]{3,2,1,0:T(8,128)(2,1)} custom-call(bf16[2,32,32,256]{3,2,1,0:T(8,128)(2,1)} %orbitals_ref.5, s32[32,32,128]{2,1,0:T(8,128)} %mask_ref.3, f32[2]{0:T(128)} %weight_ref.3, bf16[256,256]{1,0:T(8,128)(2,1)} %constant.67.clone.table_ref), custom_call_target="tpu_custom_call" | custom-call | flops 4000000000 | bytes 4000000 | tf_op jit(solution)/shard_map/spread/pallas_call | solution.py:369
  4.1 7.5 %all-to-all-start = ((bf16[32,4,32,128]{3,2,1,0:T(8,128)(2,1)}), bf16[32,4,32,128]{3,2,1,0:T(8,128)(2,1)S(1)}, u32[]{:S(2)}, u32[]{:S(2)}) async-start(bf16[32,4,32,128]{3,2,1,0:T(8,128)(2,1)} %spread.1), calls=%async_computation | async-start | bytes 2097152 | tf_op jit(solution)/shard_map/all_to_all | solution.py:365
  11.7 0.1 add_convert_fusion.4
  11.9 0.1 add.71
  12.0 0.1 sub.25
  12.2 0.6 strength.1.strength_ref
  13.0 1.2 %copy-done.2 = bf16[2,32,32,256]{3,2,1,0:T(8,128)(2,1)S(1)} copy-done((bf16[2,32,32,256]{3,2,1,0:T(8,128)(2,1)S(1)}, bf16[2,32,32,256]{3,2,1,0:T(8,128)(2,1)}, u32[]{:S(2)}) %copy-start.2) | copy-done | bytes 1048600
  14.2 1.0 %copy-done.4 = s32[32,32,128]{2,1,0:T(8,128)S(1)} copy-done((s32[32,32,128]{2,1,0:T(8,128)S(1)}, s32[32,32,128]{2,1,0:T(8,128)}, u32[]{:S(2)}) %copy-start.4) | copy-done | bytes 524312
  15.2 1.3 %overlap.1 = (bf16[16,128]{1,0:T(8,128)(2,1)S(1)}, bf16[5,32,32,128]{3,2,1,0:T(8,128)(2,1)S(1)}) custom-call(bf16[2,32,32,256]{3,2,1,0:T(8,128)(2,1)S(1)} %copy-done.2, s32[32,32,128]{2,1,0:T(8,128)S(1)} %copy-done.4, bf16[4,32,32,128]{3,2,1,0:T(8,128)(2,1)S(1)} %copy-done.1, bf16[16,1024]{1,0:T(8,128)(2,1)S(1)} %constant_dynamic-update-slice_fusion.phase_ref, ...), custom_call_target="tpu_custom_call" | custom-call | flops 100000000 | bytes 100000 | tf_op jit(solution)/shard_map/overlap/pallas_call | solution.py:402
  16.5 1.1 %copy-done.5 = bf16[5,32,32,128]{3,2,1,0:T(8,128)(2,1)} copy-done((bf16[5,32,32,128]{3,2,1,0:T(8,128)(2,1)}, bf16[5,32,32,128]{3,2,1,0:T(8,128)(2,1)S(1)}, u32[]{:S(2)}) %copy-start.5) | copy-done | bytes 1310744
  17.6 11.1 %all-to-all-done = bf16[32,4,32,128]{3,2,1,0:T(8,128)(2,1)S(1)} async-done(((bf16[32,4,32,128]{3,2,1,0:T(8,128)(2,1)}), bf16[32,4,32,128]{3,2,1,0:T(8,128)(2,1)S(1)}, u32[]{:S(2)}, u32[]{:S(2)}) %all-to-all-start) | async-done | bytes 1048608 | tf_op jit(solution)/shard_map/all_to_all | solution.py:365
  28.7 4.0 %field.1 = (bf16[256,128]{1,0:T(8,128)(2,1)S(1)}, bf16[256,128]{1,0:T(8,128)(2,1)S(1)}, bf16[32,144,128]{2,1,0:T(8,128)(2,1)}) custom-call(bf16[32,128,128]{2,1,0:T(8,128)(2,1)S(1)} %bitcast.18, f32[4,128,128]{2,1,0:T(8,128)S(1)} %constant_dynamic-slice_fusion.potential_ref, bf16[16,128]{1,0:T(8,128)(2,1)S(1)} %get-tuple-element.20.overlap_ref, ...), custom_call_target="tpu_custom_call" | custom-call | flops 6000000000 | bytes 6000000 | tf_op jit(solution)/shard_map/field/pallas_call | solution.py:420
  32.7 0.2 collective-permute-start
  32.9 3.9 %all-to-all-start.1 = ((bf16[32,144,128]{2,1,0:T(8,128)(2,1)}), bf16[32,144,128]{2,1,0:T(8,128)(2,1)S(1)}, u32[]{:S(2)}, u32[]{:S(2)}) async-start(bf16[32,144,128]{2,1,0:T(8,128)(2,1)} %get-tuple-element.23), calls=%async_computation.1 | async-start | bytes 2359296 | tf_op jit(solution)/shard_map/all_to_all | solution.py:365
  36.9 0.2 collective-permute-done
  37.1 3.4 %collective-permute-start.1 = (bf16[256,128]{1,0:T(8,128)(2,1)S(1)}, bf16[256,128]{1,0:T(8,128)(2,1)S(1)}, u32[]{:S(2)}, u32[]{:S(2)}) collective-permute-start(bf16[256,128]{1,0:T(8,128)(2,1)S(1)} %add_convert_fusion.3), channel_id=1, source_target_pairs={{0,64},{16,80},{32,96},{48,112},{64,0},{80,16},{96,32},{112,48},{1... | collective-permute-start | bytes 196616 | tf_op jit(solution)/shard_map/ppermute | solution.py:455
  40.4 3.2 %collective-permute-done.1 = bf16[256,128]{1,0:T(8,128)(2,1)S(1)} collective-permute-done((bf16[256,128]{1,0:T(8,128)(2,1)S(1)}, bf16[256,128]{1,0:T(8,128)(2,1)S(1)}, u32[]{:S(2)}, u32[]{:S(2)}) %collective-permute-start.1) | collective-permute-done | bytes 65568 | tf_op jit(solution)/shard_map/ppermute | solution.py:455
  43.7 6.2 %collective-permute-start.2 = (bf16[256,128]{1,0:T(8,128)(2,1)S(1)}, bf16[256,128]{1,0:T(8,128)(2,1)S(1)}, u32[]{:S(2)}, u32[]{:S(2)}) collective-permute-start(bf16[256,128]{1,0:T(8,128)(2,1)S(1)} %add_convert_fusion.2), channel_id=1, source_target_pairs={{0,192},{16,208},{32,224},{48,240},{64,128},{80,144},{96,160},{112... | collective-permute-start | bytes 196616 | tf_op jit(solution)/shard_map/ppermute | solution.py:457
  49.9 0.7 %collective-permute-start.3 = (bf16[256,128]{1,0:T(8,128)(2,1)S(1)}, bf16[256,128]{1,0:T(8,128)(2,1)S(1)}, u32[]{:S(2)}, u32[]{:S(2)}) collective-permute-start(bf16[256,128]{1,0:T(8,128)(2,1)S(1)} %add_convert_fusion.2), channel_id=1, source_target_pairs={{0,32},{16,48},{32,0},{48,16},{64,96},{80,112},{96,64},{112,80},{1... | collective-permute-start | bytes 196616 | tf_op jit(solution)/shard_map/ppermute | solution.py:457
  50.6 2.3 %collective-permute-done.2 = bf16[256,128]{1,0:T(8,128)(2,1)S(1)} collective-permute-done((bf16[256,128]{1,0:T(8,128)(2,1)S(1)}, bf16[256,128]{1,0:T(8,128)(2,1)S(1)}, u32[]{:S(2)}, u32[]{:S(2)}) %collective-permute-start.2) | collective-permute-done | bytes 65568 | tf_op jit(solution)/shard_map/ppermute | solution.py:457
  52.9 4.2 %collective-permute-done.4 = bf16[256,128]{1,0:T(8,128)(2,1)S(1)} collective-permute-done((bf16[256,128]{1,0:T(8,128)(2,1)S(1)}, bf16[256,128]{1,0:T(8,128)(2,1)S(1)}, u32[]{:S(2)}, u32[]{:S(2)}) %collective-permute-start.4) | collective-permute-done | bytes 65568 | tf_op jit(solution)/shard_map/ppermute | solution.py:457
  57.2 3.3 %collective-permute-start.5 = (bf16[2,256,128]{2,1,0:T(8,128)(2,1)S(1)}, bf16[2,256,128]{2,1,0:T(8,128)(2,1)S(1)}, u32[]{:S(2)}, u32[]{:S(2)}) collective-permute-start(bf16[2,256,128]{2,1,0:T(8,128)(2,1)S(1)} %maximum_select_fusion.1), channel_id=1, source_target_pairs={{0,16},{16,0},{32,48},{48,32},{64,80},{80,64},{96,112},{112,96},{1... | collective-permute-start | bytes 393224 | tf_op jit(solution)/shard_map/ppermute | solution.py:462
  60.6 5.6 %apply.1 = bf16[2,32,32,256]{3,2,1,0:T(8,128)(2,1)} custom-call(bf16[32,144,128]{2,1,0:T(8,128)(2,1)S(1)} %all-to-all-done.1.returned_ref.overlap_ref, bf16[32,144,128]{2,1,0:T(8,128)(2,1)S(1)} %all-to-all-done.1.returned_ref.overlap_ref, bf16[2,32,32,256]{3,2,1,0:T(8,128)(2,1)S(1)} %copy-done.3, bf16[5,32,32,128]{3,2,1,0:T(8,128)(2,1)} %copy-done.5, ...), custom_call_target="tpu_custom_call" | custom-call | flops 4000000000 | bytes 4000000 | tf_op jit(solution)/shard_map/apply/pallas_call | solution.py:463
  66.2 0.8 %convert.11 = f32[8,128,128]{2,1,0:T(8,128)} convert(bf16[8,128,128]{2,1,0:T(8,128)(2,1)S(1)} %bitcast.19) | non-fusion elementwise | flops 131072 | bytes 786432 | tf_op jit(solution)/shard_map/convert_element_type | solution.py:489
  (46 shorter events, 0.5 us)
Async XLA Ops:
  0.6 17.0 %copy-start = (f32[8,128,128]{2,1,0:T(8,128)S(1)}, f32[8,128,128]{2,1,0:T(8,128)}, u32[]{:S(2)}) copy-start(f32[8,128,128]{2,1,0:T(8,128)} %param.15) | copy-start | bytes 1572868
  4.0 7.6 %copy-start.13 = (f32[8,3]{0,1:T(4,128)S(1)}, f32[8,3]{0,1:T(4,128)}, u32[]{:S(2)}) copy-start(f32[8,3]{0,1:T(4,128)} %param.18) | copy-start | bytes 292
  4.0 8.1 %copy-start.6 = (s32[32]{0:T(128)S(1)}, s32[32]{0:T(128)}, u32[]{:S(2)}) copy-start(s32[32]{0:T(128)} %atom_ref.1) | copy-start | bytes 388
  4.1 8.1 %copy-start.7 = (s32[32]{0:T(128)S(1)}, s32[32]{0:T(128)}, u32[]{:S(2)}) copy-start(s32[32]{0:T(128)} %kind_ref.1) | copy-start | bytes 388
  4.1 8.1 %copy-start.8 = (f32[32]{0:T(128)S(1)}, f32[32]{0:T(128)}, u32[]{:S(2)}) copy-start(f32[32]{0:T(128)} %coupling_ref) | copy-start | bytes 388
  4.1 8.9 %copy-start.1 = (bf16[4,32,32,128]{3,2,1,0:T(8,128)(2,1)S(1)}, bf16[4,32,32,128]{3,2,1,0:T(8,128)(2,1)}, u32[]{:S(2)}) copy-start(bf16[4,32,32,128]{3,2,1,0:T(8,128)(2,1)} %channels_ref.1) | copy-start | bytes 3145732
  4.1 24.6 %all-to-all-start = ((bf16[32,4,32,128]{3,2,1,0:T(8,128)(2,1)}), bf16[32,4,32,128]{3,2,1,0:T(8,128)(2,1)S(1)}, u32[]{:S(2)}, u32[]{:S(2)}) async-start(bf16[32,4,32,128]{3,2,1,0:T(8,128)(2,1)} %spread.1), calls=%async_computation | async-start | bytes 2097152 | tf_op jit(solution)/shard_map/all_to_all | solution.py:365
  12.9 1.2 %copy-start.2 = (bf16[2,32,32,256]{3,2,1,0:T(8,128)(2,1)S(1)}, bf16[2,32,32,256]{3,2,1,0:T(8,128)(2,1)}, u32[]{:S(2)}) copy-start(bf16[2,32,32,256]{3,2,1,0:T(8,128)(2,1)} %orbitals_ref.5) | copy-start | bytes 3145732
  14.2 1.0 %copy-start.4 = (s32[32,32,128]{2,1,0:T(8,128)S(1)}, s32[32,32,128]{2,1,0:T(8,128)}, u32[]{:S(2)}) copy-start(s32[32,32,128]{2,1,0:T(8,128)} %mask_ref.3) | copy-start | bytes 1572868
  15.2 13.5 %copy-start.11 = (bf16[256,256]{1,0:T(8,128)(2,1)S(1)}, bf16[256,256]{1,0:T(8,128)(2,1)}, u32[]{:S(2)}) copy-start(bf16[256,256]{1,0:T(8,128)(2,1)} %constant.70.clone.fwd_y_ref) | copy-start | bytes 393220
  15.2 13.5 %copy-start.12 = (bf16[256,256]{1,0:T(8,128)(2,1)S(1)}, bf16[256,256]{1,0:T(8,128)(2,1)}, u32[]{:S(2)}) copy-start(bf16[256,256]{1,0:T(8,128)(2,1)} %constant.68.clone.inv_y_ref) | copy-start | bytes 393220
  16.5 1.1 %copy-start.5 = (bf16[5,32,32,128]{3,2,1,0:T(8,128)(2,1)}, bf16[5,32,32,128]{3,2,1,0:T(8,128)(2,1)S(1)}, u32[]{:S(2)}) copy-start(bf16[5,32,32,128]{3,2,1,0:T(8,128)(2,1)S(1)} %get-tuple-element.24.profile_ref) | copy-start | bytes 3932164
  32.7 4.4 %collective-permute-start = (bf16[256,128]{1,0:T(8,128)(2,1)S(1)}, bf16[256,128]{1,0:T(8,128)(2,1)S(1)}, u32[]{:S(2)}, u32[]{:S(2)}) collective-permute-start(bf16[256,128]{1,0:T(8,128)(2,1)S(1)} %get-tuple-element.22), channel_id=1, source_target_pairs={{0,32},{16,48},{32,0},{48,16},{64,96},{80,112},{96,64},{112,80},{1... | collective-permute-start | bytes 196616 | tf_op jit(solution)/shard_map/ppermute | solution.py:453
  32.9 27.7 %all-to-all-start.1 = ((bf16[32,144,128]{2,1,0:T(8,128)(2,1)}), bf16[32,144,128]{2,1,0:T(8,128)(2,1)S(1)}, u32[]{:S(2)}, u32[]{:S(2)}) async-start(bf16[32,144,128]{2,1,0:T(8,128)(2,1)} %get-tuple-element.23), calls=%async_computation.1 | async-start | bytes 2359296 | tf_op jit(solution)/shard_map/all_to_all | solution.py:365
  36.8 23.8 %copy-start.3 = (bf16[2,32,32,256]{3,2,1,0:T(8,128)(2,1)S(1)}, bf16[2,32,32,256]{3,2,1,0:T(8,128)(2,1)}, u32[]{:S(2)}) copy-start(bf16[2,32,32,256]{3,2,1,0:T(8,128)(2,1)} %orbitals_ref.5) | copy-start | bytes 3145732
  36.8 23.8 %copy-start.9 = (f32[2]{0:T(128)S(1)}, f32[2]{0:T(128)}, u32[]{:S(2)}) copy-start(f32[2]{0:T(128)} %weight_ref.3) | copy-start | bytes 28
  36.9 23.8 %copy-start.10 = (bf16[256,256]{1,0:T(8,128)(2,1)S(1)}, bf16[256,256]{1,0:T(8,128)(2,1)}, u32[]{:S(2)}) copy-start(bf16[256,256]{1,0:T(8,128)(2,1)} %constant.67.clone.table_ref) | copy-start | bytes 393220
  37.1 6.6 %collective-permute-start.1 = (bf16[256,128]{1,0:T(8,128)(2,1)S(1)}, bf16[256,128]{1,0:T(8,128)(2,1)S(1)}, u32[]{:S(2)}, u32[]{:S(2)}) collective-permute-start(bf16[256,128]{1,0:T(8,128)(2,1)S(1)} %add_convert_fusion.3), channel_id=1, source_target_pairs={{0,64},{16,80},{32,96},{48,112},{64,0},{80,16},{96,32},{112,48},{1... | collective-permute-start | bytes 196616 | tf_op jit(solution)/shard_map/ppermute | solution.py:455
  43.7 9.2 %collective-permute-start.2 = (bf16[256,128]{1,0:T(8,128)(2,1)S(1)}, bf16[256,128]{1,0:T(8,128)(2,1)S(1)}, u32[]{:S(2)}, u32[]{:S(2)}) collective-permute-start(bf16[256,128]{1,0:T(8,128)(2,1)S(1)} %add_convert_fusion.2), channel_id=1, source_target_pairs={{0,192},{16,208},{32,224},{48,240},{64,128},{80,144},{96,160},{112... | collective-permute-start | bytes 196616 | tf_op jit(solution)/shard_map/ppermute | solution.py:457
  49.9 7.3 %collective-permute-start.4 = (bf16[256,128]{1,0:T(8,128)(2,1)S(1)}, bf16[256,128]{1,0:T(8,128)(2,1)S(1)}, u32[]{:S(2)}, u32[]{:S(2)}) collective-permute-start(bf16[256,128]{1,0:T(8,128)(2,1)S(1)} %add_convert_fusion.2), channel_id=1, source_target_pairs={{0,224},{16,240},{32,192},{48,208},{64,160},{80,176},{96,128},{112... | collective-permute-start | bytes 196616 | tf_op jit(solution)/shard_map/ppermute | solution.py:457
  49.9 7.3 %collective-permute-start.3 = (bf16[256,128]{1,0:T(8,128)(2,1)S(1)}, bf16[256,128]{1,0:T(8,128)(2,1)S(1)}, u32[]{:S(2)}, u32[]{:S(2)}) collective-permute-start(bf16[256,128]{1,0:T(8,128)(2,1)S(1)} %add_convert_fusion.2), channel_id=1, source_target_pairs={{0,32},{16,48},{32,0},{48,16},{64,96},{80,112},{96,64},{112,80},{1... | collective-permute-start | bytes 196616 | tf_op jit(solution)/shard_map/ppermute | solution.py:457
  57.2 9.0 %collective-permute-start.5 = (bf16[2,256,128]{2,1,0:T(8,128)(2,1)S(1)}, bf16[2,256,128]{2,1,0:T(8,128)(2,1)S(1)}, u32[]{:S(2)}, u32[]{:S(2)}) collective-permute-start(bf16[2,256,128]{2,1,0:T(8,128)(2,1)S(1)} %maximum_select_fusion.1), channel_id=1, source_target_pairs={{0,16},{16,0},{32,48},{48,32},{64,80},{80,64},{96,112},{112,96},{1... | collective-permute-start | bytes 393224 | tf_op jit(solution)/shard_map/ppermute | solution.py:462
